TPU v7x, 32 devices: a whole 2x2x4 slice. The times are simulated.
32 devices in a mesh: seg: 16 (over z, y, x), bond: 2 (over core).
Axes of the slice: x: 2, y: 2, z: 4, core: 2. Of those that a mesh axis runs over, the one named last changes fastest.
Arguments:
- left_env: bfloat16 [16, 512, 14, 512], P('seg', 'bond'), may hold values from -0.25 to 0.25
- right_env: bfloat16 [16, 512, 14, 512], P('seg', 'bond'), may hold values from -0.25 to 0.25
- states: bfloat16 [16, 4, 512, 2, 512], P('seg', None, 'bond'), may hold values from -6 to 6
- mpo: bfloat16 [14, 2, 2, 14], replicated, may hold values from -0.3125 to 0.3125
Outputs:
- applied: bfloat16 [16, 4, 512, 2, 512], P('seg', None, 'bond')
- new_env: bfloat16 [16, 512, 14, 512], P('seg', 'bond')
All inputs are finite; a program needn't handle non-finite values.
Results may differ from a plain program's by a relative error of at most 0.013.
Values may be sent and summed in bfloat16 or wider, within the bound.
No kernel may reach another device: no remote copies, remote signals or barrier semaphores. Data moves between devices by JAX's collectives and lax.ppermute only.
A program may use at most 192 MiB of HBM per device.

v0:
```python
import math

import jax
import jax.numpy as jnp
from jax import lax
from jax.sharding import PartitionSpec as P


def passed_along(array, axis, by):
    size = lax.axis_size(axis)
    pairs = [(i, i + by) for i in range(size) if 0 <= i + by < size]
    return lax.ppermute(array, axis, pairs)


def on_device(left_env, right_env, states, mpo):
    num_states = states.shape[1]
    chi_full = states.shape[4]
    scaling = 1.0 / math.sqrt(num_states * chi_full)
    wave_all = lax.all_gather(states, "bond", axis=2, tiled=True)[0]
    inner = jnp.einsum("awc,kcte->awkte", left_env[0], wave_all, preferred_element_type=jnp.float32)
    inner_low = inner.astype(jnp.bfloat16)
    through = jnp.einsum("wstv,awkte->aksve", mpo, inner_low, preferred_element_type=jnp.float32)
    through_low = through.astype(jnp.bfloat16)
    arrived = passed_along(right_env, "seg", -1)
    applied = jnp.einsum(
        "aksvc,bvc->kasb",
        through_low,
        lax.all_gather(arrived, "bond", axis=1, tiled=True)[0],
        preferred_element_type=jnp.float32,
    )
    applied = applied.astype(jnp.bfloat16)[None]
    wave_here = states[0]
    summed = lax.psum_scatter(
        (
            jnp.einsum(
                "kasb,aksve->bve", wave_here, through_low, preferred_element_type=jnp.float32
            )
            * scaling
        ).astype(jnp.bfloat16),
        "bond",
        scatter_dimension=0,
        tiled=True,
    )
    new_env = summed[None]
    return (applied, new_env)


def solution(mesh):
    in_specs = (
        P("seg", "bond", None, None),
        P("seg", "bond", None, None),
        P("seg", None, "bond", None, None),
        P(),
    )
    out_specs = (P("seg", None, "bond", None, None), P("seg", "bond", None, None))
    return jax.shard_map(
        on_device, mesh=mesh, in_specs=in_specs, out_specs=out_specs, check_vma=False
    )
```

profile of v0, /device:TPU:22, one launch (start us, length us, event | category | flops | bytes accessed | tf_op | source)
XLA Modules:
  0.0 308.2 jit_solution(4804708563169173399)
XLA Ops:
  7.2 0.0 copy-start
  7.2 0.0 all-gather.3.cloned.1.call-start
  7.2 0.7 all-gather.3.cloned.1.call-update
  7.9 0.0 all-gather.5.cloned.1.call-start
  8.0 2.4 collective-permute-start
  10.4 82.6 %collective-permute-done = bf16[1,256,14,512]{3,1,2,0:T(8,128)(2,1)} collective-permute-done((bf16[1,256,14,512]{3,1,2,0:T(8,128)(2,1)}, bf16[1,256,14,512]{3,1,2,0:T(8,128)(2,1)}, u32[]{:S(2)}, u32[]{:S(2)}) %collective-permute-start) | collective-permute-done | bytes 3670048 | tf_op jit(solution)/shard_map/ppermute | solution.py:12
  93.0 0.0 all-gather.5.cloned.1.call-update
  93.1 0.0 reduce-scatter.2.cloned.1.call-start
  93.1 0.0 all-gather.3.cloned.1.call-done
  93.1 22.4 %fusion.17 = bf16[256,14,4,2,512]{4,0,3,2,1:T(8,128)(2,1)} fusion(bf16[4,512,2,512,1]{3,2,1,0,4:T(2,128)(2,1)} %bitcast.62, bf16[1,256,14,512]{3,1,2,0:T(8,128)(2,1)} %param.4), kind=kOutput, calls=%fused_computation.14 | convolution fusion | flops 15032385536 | bytes 37224448 | tf_op jit(solution)/shard_map/awc,kcte->awkte/dot_general | solution.py:20
  115.5 0.0 copy-done
  115.5 0.0 copy-start.2
  115.5 40.1 %fusion.3 = bf16[256,4,2,14,512]{4,3,2,1,0:T(8,128)(2,1)} fusion(bf16[256,14,4,2,512]{4,0,3,2,1:T(8,128)(2,1)} %fusion.17, bf16[14,2,2,14,1,1]{3,2,1,0,5,4:T(2,128)(2,1)S(1)} %bitcast.59), kind=kOutput, calls=%fused_computation.4 | convolution fusion | flops 836763648 | bytes 58721824 | tf_op jit(solution)/shard_map/wstv,awkte->aksve/dot_general | solution.py:22
  155.6 0.0 copy-done.2
  155.6 84.4 %fusion.14 = bf16[512,14,512]{0,2,1:T(8,128)(2,1)} fusion(bf16[256,4,2,14,512]{4,3,2,1,0:T(8,128)(2,1)} %fusion.3, bf16[4,256,2,512]{3,2,1,0:T(2,128)(2,1)S(1)} %bitcast.61), kind=kOutput, calls=%fused_computation.12 | convolution fusion | flops 15039725568 | bytes 38797312 | tf_op jit(solution)/shard_map/kasb,aksve->bve/dot_general | solution.py:35
  240.0 0.0 reduce-scatter.2.cloned.1.call-update
  240.0 0.0 all-gather.5.cloned.1.call-done
  240.1 0.0 copy-start.1
  240.1 51.9 %fusion.26 = bf16[1,4,256,2,512]{4,2,3,1,0:T(8,128)(2,1)S(1)} fusion(bf16[1,512,14,512]{3,1,2,0:T(8,128)(2,1)} %all-gather.5.cloned.1.call-done, bf16[256,4,2,14,512]{4,3,2,1,0:T(8,128)(2,1)} %fusion.3), kind=kOutput, calls=%fused_computation.19 | convolution fusion | flops 15033434112 | bytes 38797312 | tf_op jit(solution)/shard_map/aksvc,bvc->kasb/dot_general | solution.py:25
  292.0 3.5 %copy.10 = bf16[1,4,256,2,512]{4,3,2,1,0:T(2,128)(2,1)} copy(bf16[1,4,256,2,512]{4,2,3,1,0:T(8,128)(2,1)S(1)} %fusion.26) | data formatting | bytes 4194304
  295.5 0.0 reduce-scatter.2.cloned.1.call-done
  295.5 5.9 %copy.11 = bf16[1,256,14,512]{3,1,2,0:T(8,128)(2,1)} copy(bf16[1,256,14,512]{1,3,2,0:T(8,128)(2,1)} %bitcast.60) | data formatting | bytes 7340032
  301.4 0.0 copy-done.1
Async XLA Ops:
  7.2 108.4 %copy-start = (bf16[14,2,2,14]{3,2,1,0:T(2,128)(2,1)S(1)}, bf16[14,2,2,14]{3,2,1,0:T(2,128)(2,1)}, u32[]{:S(2)}) copy-start(bf16[14,2,2,14]{3,2,1,0:T(2,128)(2,1)} %param.7) | copy-start | bytes 4708
  7.2 86.0 %all-gather.3.cloned.1.call-start = ((), (), s32[]{:S(2)}) async-start(), calls=%async_computation.1 | async-start | bytes 6291456 | tf_op jit(solution)/shard_map/all_gather | solution.py:19
  7.9 232.1 %all-gather.5.cloned.1.call-start = ((), (), s32[]{:S(2)}) async-start(), calls=%async_computation.2 | async-start | bytes 11010048 | tf_op jit(solution)/shard_map/all_gather | solution.py:28
  8.0 85.1 %collective-permute-start = (bf16[1,256,14,512]{3,1,2,0:T(8,128)(2,1)}, bf16[1,256,14,512]{3,1,2,0:T(8,128)(2,1)}, u32[]{:S(2)}, u32[]{:S(2)}) collective-permute-start(bf16[1,256,14,512]{3,1,2,0:T(8,128)(2,1)} %param.5), channel_id=1, source_target_pairs={{2,0},{4,2},{6,4},{8,6},{10,8},{12,10},{14,12},{16,14},{18,16},{20... | collective-permute-start | bytes 11010056 | tf_op jit(solution)/shard_map/ppermute | solution.py:12
  93.1 202.4 %reduce-scatter.2.cloned.1.call-start = ((), (), s32[]{:S(2)}) async-start(), calls=%async_computation.3 | async-start | bytes 11010048 | tf_op jit(solution)/shard_map/reduce_scatter | solution.py:33
  115.5 40.1 %copy-start.2 = (bf16[1,4,256,2,512]{4,3,2,1,0:T(2,128)(2,1)S(1)}, bf16[1,4,256,2,512]{4,3,2,1,0:T(2,128)(2,1)}, u32[]{:S(2)}) copy-start(bf16[1,4,256,2,512]{4,3,2,1,0:T(2,128)(2,1)} %param.6) | copy-start | bytes 6291460
  240.1 61.3 %copy-start.1 = (bf16[14,2,2,14]{3,2,1,0:T(2,128)(2,1)S(1)}, bf16[14,2,2,14]{3,2,1,0:T(2,128)(2,1)}, u32[]{:S(2)}) copy-start(bf16[14,2,2,14]{3,2,1,0:T(2,128)(2,1)} %param.7) | copy-start | bytes 4708
Sparse Core Ops, SparseCore 0:
  9.6 14.9 all-gather.2
  93.2 18.5 all-gather.4
  240.2 16.0 reduce-scatter.1
where the time goes:
time: 312 us; the launch traced here: 308 us
  matrix products  199 us (64%)
  waiting for transfers between devices  83.4 us (27%)
  between operations  14 us (4%)
  local copies, waits for them, and re-layouts  9.42 us (3%)
    dot_general x1, matrix products, on_device(): jnp.einsum('kasb,aksve->bve', wave_here, through_low, preferred_element_t...  84.4 us
    ppermute x1, waiting for transfers between devices, passed_along(): return lax.ppermute(array, axis, pairs)  82.6 us
    dot_general x1, matrix products, on_device(): jnp.einsum('aksvc,bvc->kasb', through_low, lax.all_gather(arrived, 'bond'...  51.9 us
    dot_general x1, matrix products, on_device(): jnp.einsum('wstv,awkte->aksve', mpo, inner_low, preferred_element_type=jn...  40.1 us
    dot_general x1, matrix products, on_device(): jnp.einsum('awc,kcte->awkte', left_env[0], wave_all, preferred_element_ty...  22.4 us
    unnamed x8, local copies, waits for them, and re-layouts  9.42 us
  transfers between devices with their start and end apart: 4, of which 1 were waited for; matrix products, arithmetic and copies ran while one was open for 66% of the time, Pallas kernels for 0%

commit v1 on v0

v1 whole, which is shorter than its diff:
```python
import functools
import math

import jax
import jax.numpy as jnp
from jax import lax
from jax.experimental import pallas as pl
from jax.experimental.pallas import tpu as pltpu
from jax.sharding import PartitionSpec as P

GROUP = 8
MIB = 1 << 20


def passed_along(array, axis, by):
    size = lax.axis_size(axis)
    pairs = [(i, i + by) for i in range(size) if 0 <= i + by < size]
    return lax.ppermute(array, axis, pairs)


def swapped(array, axis):
    return lax.ppermute(array, axis, [(0, 1), (1, 0)])


def product(left, right, contract):
    return lax.dot_general(left, right, (contract, ((), ())), preferred_element_type=jnp.float32)


def block_diagonal(mpo):
    mw, phys = mpo.shape[0], mpo.shape[1]
    eye = jnp.eye(GROUP, dtype=mpo.dtype)
    table = mpo.transpose(3, 1, 2, 0)[:, None, :, :, :, None] * eye[None, :, None, None, None, :]
    return table.reshape(mw * GROUP * phys, phys * mw * GROUP)


def through_kernel(parts, places, table_ref, *refs):
    envs, waves, out_ref = refs[:parts], refs[parts : 2 * parts], refs[2 * parts]
    mw, rows, _ = envs[0].shape
    num_states, phys, _, chi = waves[0].shape
    table = table_ref[...]
    for k in range(num_states):
        inner = []
        for t in range(phys):
            total = None
            for env, wave in zip(envs, waves):
                lhs = env[...].reshape(mw * rows, env.shape[2])
                term = product(lhs, wave[k, t], ((1,), (0,)))
                total = term if total is None else total + term
            inner.append(total.reshape(mw, rows // GROUP, GROUP, chi))
        for g in range(rows // GROUP):
            low = jnp.concatenate(
                [part[:, g].reshape(mw * GROUP, chi) for part in inner], axis=0
            ).astype(jnp.bfloat16)
            through = product(table, low, ((1,), (0,)))
            out_ref[:, k, g * phys * GROUP : (g + 1) * phys * GROUP, :] = through.astype(
                jnp.bfloat16
            ).reshape(mw, GROUP * phys, chi)


def through_low(table, env, waves, places):
    mw, rows_all, chi_in = env.shape
    num_states, phys, _, chi = waves[0].shape
    rows = min(32, rows_all)
    parts = len(waves)
    steps = rows_all // rows
    width = chi_in // parts

    def env_spec(part):
        return pl.BlockSpec((mw, rows, width), lambda i, at: (0, i, at[part]))

    return pl.pallas_call(
        functools.partial(through_kernel, parts),
        grid_spec=pltpu.PrefetchScalarGridSpec(
            num_scalar_prefetch=1,
            grid=(steps,),
            in_specs=[pl.BlockSpec(table.shape, lambda i, at: (0, 0))]
            + [env_spec(part) for part in range(parts)]
            + [pl.BlockSpec(wave.shape, lambda i, at: (0, 0, 0, 0)) for wave in waves],
            out_specs=pl.BlockSpec(
                (mw, num_states, rows * phys, chi), lambda i, at: (0, 0, i, 0)
            ),
        ),
        out_shape=jax.ShapeDtypeStruct((mw, num_states, rows_all * phys, chi), jnp.bfloat16),
        compiler_params=pltpu.CompilerParams(vmem_limit_bytes=48 * MIB),
        cost_estimate=pl.CostEstimate(
            flops=2 * mw * rows_all * chi_in * num_states * phys * chi * 3 // 2,
            bytes_accessed=2 * mw * num_states * rows_all * phys * chi,
            transcendentals=0,
        ),
        name="through",
    )(places, table, *([env] * parts), *waves)


def env_kernel(scaling, places, wave_ref, through_ref, *refs):
    out_ref = refs[-1]
    through = through_ref[0].reshape(wave_ref.shape[1], through_ref.shape[3])
    total = product(wave_ref[...], through, ((1,), (0,))) * scaling
    if len(refs) > 1:
        total = total + refs[0][0].astype(jnp.float32)
    out_ref[0] = total.astype(jnp.bfloat16)


def env_rows(scaling, wave_turned, through, places, which, count, arrived=None):
    mw, num_states, rows, chi = through.shape
    depth = wave_turned.shape[1]
    width = wave_turned.shape[0] // count
    arrivals = [] if arrived is None else [arrived]
    return pl.pallas_call(
        functools.partial(env_kernel, scaling),
        grid_spec=pltpu.PrefetchScalarGridSpec(
            num_scalar_prefetch=1,
            grid=(mw,),
            in_specs=[
                pl.BlockSpec((width, depth), lambda v, at: (at[which], 0)),
                pl.BlockSpec((1, num_states, rows, chi), lambda v, at: (v, 0, 0, 0)),
            ]
            + [pl.BlockSpec((1, width, chi), lambda v, at: (v, 0, 0)) for _ in arrivals],
            out_specs=pl.BlockSpec((1, width, chi), lambda v, at: (v, 0, 0)),
        ),
        out_shape=jax.ShapeDtypeStruct((mw, width, chi), jnp.bfloat16),
        compiler_params=pltpu.CompilerParams(vmem_limit_bytes=32 * MIB),
        cost_estimate=pl.CostEstimate(
            flops=2 * mw * width * depth * chi,
            bytes_accessed=2 * mw * depth * chi,
            transcendentals=0,
        ),
        name="env_rows",
    )(places, wave_turned, through, *arrivals)


def applied_kernel(parts, first, last, places, through_ref, *refs):
    rights = refs[:parts]
    sums = refs[parts : 2 * parts] if not first else [None] * parts
    outs = refs[parts if first else 2 * parts :]
    count = through_ref.shape[0]
    for part, (right, held) in enumerate(zip(rights, sums)):
        total = None if held is None else held[0]
        for v in range(count):
            term = product(through_ref[v, 0], right[v], ((1,), (1,)))
            total = term if total is None else total + term
        if last:
            width = right.shape[1]
            columns = pl.ds(pl.multiple_of(places[part] * width, width), width)
            outs[0][0, :, columns] = total.astype(jnp.bfloat16)
        else:
            outs[part][0] = total


def applied_part(through, rights, sums, at, places, last):
    mw, num_states, rows, chi = through.shape
    count = rights[0].shape[0]
    parts = len(rights)
    first = sums is None
    width = rights[0].shape[1]
    if last:
        out_shape = jax.ShapeDtypeStruct((num_states, rows, width * parts), jnp.bfloat16)
        out_specs = pl.BlockSpec((1, rows, width * parts), lambda k, at: (k, 0, 0))
    else:
        out_shape = [jax.ShapeDtypeStruct((num_states, rows, width), jnp.float32)] * parts
        out_specs = [pl.BlockSpec((1, rows, width), lambda k, at: (k, 0, 0))] * parts
    slab = at // count
    assert at % count == 0
    return pl.pallas_call(
        functools.partial(applied_kernel, parts, first, last),
        grid_spec=pltpu.PrefetchScalarGridSpec(
            num_scalar_prefetch=1,
            grid=(num_states,),
            in_specs=[pl.BlockSpec((count, 1, rows, chi), lambda k, at: (slab, k, 0, 0))]
            + [pl.BlockSpec(right.shape, lambda k, at: (0, 0, 0)) for right in rights]
            + ([] if first else [pl.BlockSpec((1, rows, width), lambda k, at: (k, 0, 0))] * parts),
            out_specs=out_specs,
        ),
        out_shape=out_shape,
        compiler_params=pltpu.CompilerParams(vmem_limit_bytes=48 * MIB),
        cost_estimate=pl.CostEstimate(
            flops=2 * num_states * rows * width * parts * count * chi,
            bytes_accessed=2 * count * num_states * rows * chi,
            transcendentals=0,
        ),
        name="applied_part",
    )(places, through, *rights, *([] if first else sums))


def cuts(size):
    if size % 7 == 0 and size > 7:
        step = size // 7
        return [(0, 2 * step), (2 * step, 2 * step), (4 * step, 2 * step), (6 * step, step)]
    return [(0, size)]


def on_device(left_env, right_env, states, mpo):
    num_states, rows, phys, chi = states.shape[1:]
    bonds = lax.axis_size("bond")
    paired = bonds == 2
    me = lax.axis_index("bond").astype(jnp.int32)
    places = jnp.stack([me, 1 - me]) if paired else jnp.stack([me, me]) * 0
    scaling = 1.0 / math.sqrt(num_states * chi)
    left = left_env[0].transpose(1, 0, 2)
    right = right_env[0].transpose(1, 0, 2)

    pieces = [
        (at, passed_along(right[at : at + count], "seg", -1)) for at, count in cuts(right.shape[0])
    ]

    wave_split = states[0].transpose(0, 2, 1, 3)
    if paired:
        waves = [wave_split, swapped(wave_split, "bond")]
    else:
        waves = [lax.all_gather(wave_split, "bond", axis=2, tiled=True)]
    wave_turned = states[0].transpose(3, 0, 1, 2).reshape(chi, num_states * rows * phys)
    through = through_low(block_diagonal(mpo), left, waves, places)

    if paired:
        sent = env_rows(scaling, wave_turned, through, places, 1, 2)
        arrived = swapped(sent, "bond")
        new_env = env_rows(scaling, wave_turned, through, places, 0, 2, arrived)
    else:
        share = env_rows(scaling, wave_turned, through, places, 0, 1)
        new_env = lax.psum_scatter(share, "bond", scatter_dimension=1, tiled=True)

    sums = None
    for index, (at, piece) in enumerate(pieces):
        if paired:
            rights = [piece, swapped(piece, "bond")]
        else:
            rights = [lax.all_gather(piece, "bond", axis=1, tiled=True)]
        sums = applied_part(through, rights, sums, at, places, index == len(pieces) - 1)
    applied = sums.reshape(num_states, rows, phys, chi)
    return (applied[None], new_env.transpose(1, 0, 2)[None])


def solution(mesh):
    in_specs = (
        P("seg", "bond", None, None),
        P("seg", "bond", None, None),
        P("seg", None, "bond", None, None),
        P(),
    )
    out_specs = (P("seg", None, "bond", None, None), P("seg", "bond", None, None))
    return jax.shard_map(
        on_device, mesh=mesh, in_specs=in_specs, out_specs=out_specs, check_vma=False
    )
```

time: 312 us -> 218 us (0.70)
  the two profiles are of different devices: /device:TPU:22 before, /device:TPU:13 now
where the time goes in v1:
time: 218 us; the launch traced here: 215 us
  Pallas kernels  106 us (49%)
  waiting for transfers between devices  62 us (28%)
  local copies, waits for them, and re-layouts  23.3 us (11%)
  starting transfers between devices  22.3 us (10%)
    ppermute x4, waiting for transfers between devices, passed_along(): return lax.ppermute(array, axis, pairs)  62 us
    pallas_call x2, Pallas kernels, env_rows(): pl.pallas_call(functools.partial(env_kernel, scaling), grid_spec=pltpu.Pr...  39.7 us
    pallas_call x1, Pallas kernels, through_low(): pl.pallas_call(functools.partial(through_kernel, parts), grid_spec=pltpu....  33.4 us
    pallas_call x4, Pallas kernels, applied_part(): pl.pallas_call(functools.partial(applied_kernel, parts, first, last), gri...  33.1 us
    ppermute x4, starting transfers between devices, passed_along(): return lax.ppermute(array, axis, pairs)  13.3 us
    ppermute x6, starting transfers between devices, swapped(): return lax.ppermute(array, axis, [(0, 1), (1, 0)])  8.96 us
    unnamed x11, local copies, waits for them, and re-layouts  7.24 us
    reshape x2, local copies, waits for them, and re-layouts, on_device(): states[0].transpose(3, 0, 1, 2).reshape(chi, num_states * rows * phys)  5.14 us
  transfers between devices with their start and end apart: 10, of which 4 were waited for; matrix products, arithmetic and copies ran while one was open for 8% of the time, Pallas kernels for 15%

profile of v1, /device:TPU:13, one launch (start us, length us, event | category | flops | bytes accessed | tf_op | source)
XLA Modules:
  0.0 214.8 jit_solution(12011559737910975573)
XLA Ops:
  0.6 3.3 %copy.16 = bf16[1,4,256,2,512]{4,2,3,1,0:T(8,128)(2,1)} copy(bf16[1,4,256,2,512]{4,3,2,1,0:T(2,128)(2,1)} %param.6) | data formatting | bytes 4194304 | tf_op args[2]
  4.9 2.7 %mul.20.table_ref = bf16[224,224]{1,0:T(8,128)(2,1)S(1)} reshape(bf16[14,8,2,2,14,8]{5,4,3,2,1,0:T(8,128)(2,1)S(1)} %broadcast_multiply_fusion) | data formatting | bytes 200704 | tf_op jit(solution)/shard_map/mul | solution.py:32
  7.6 3.8 %copy.11 = bf16[512,4,256,2]{0,3,2,1:T(2,128)(2,1)S(1)} copy(bf16[512,4,256,2]{0,2,3,1:T(8,128)(2,1)} %bitcast.21) | data formatting | bytes 4194304 | tf_op jit(solution)/shard_map/transpose | solution.py:210
  11.4 2.2 %reshape.20 = bf16[512,2048]{0,1:T(8,128)(2,1)} reshape(bf16[512,4,256,2]{0,3,2,1:T(2,128)(2,1)S(1)} %copy.11) | data formatting | bytes 4194304 | tf_op jit(solution)/shard_map/reshape | solution.py:210
  13.6 2.9 %copy.13.wave_ref = bf16[512,2048]{1,0:T(8,128)(2,1)S(1)} copy(bf16[512,2048]{0,1:T(8,128)(2,1)} %reshape.20) | data formatting | bytes 4194304 | tf_op jit(solution)/shard_map/reshape | solution.py:210
  16.6 33.4 %through.1.through_ref = bf16[14,4,512,512]{3,2,1,0:T(8,128)(2,1)} custom-call(s32[2]{0:T(128)S(1)} %pad_add_fusion.places, bf16[224,224]{1,0:T(8,128)(2,1)S(1)} %mul.20.table_ref, bf16[14,256,512]{2,1,0:T(8,128)(2,1)} %bitcast.26, bf16[14,256,512]{2,1,0:T(8,128)(2,1)} %bitcast.27, bf16[4,2,256,512]{3,2,1,0:T(8,128)(2,1)} %bitcast.18.clone.2.refs_2_, ...), custom_call_target="tpu_custom_call" | custom-call | flops 22548578304 | bytes 29360128 | tf_op jit(solution)/shard_map/through/pallas_call | solution.py:71
  50.0 19.9 %env_rows.2 = bf16[14,256,512]{2,1,0:T(8,128)(2,1)} custom-call(s32[2]{0:T(128)S(1)} %pad_add_fusion.places, bf16[512,2048]{1,0:T(8,128)(2,1)S(1)} %copy.13.wave_ref, bf16[14,4,512,512]{3,2,1,0:T(8,128)(2,1)} %through.1.through_ref), custom_call_target="tpu_custom_call" | custom-call | flops 7516192768 | bytes 29360128 | tf_op jit(solution)/shard_map/env_rows/pallas_call | solution.py:108
  70.1 3.1 %collective-permute-start.7 = (bf16[4,256,512]{2,1,0:T(8,128)(2,1)S(1)}, bf16[4,256,512]{2,1,0:T(8,128)(2,1)S(1)}, u32[]{:S(2)}, u32[]{:S(2)}) collective-permute-start(bf16[4,256,512]{2,1,0:T(8,128)(2,1)S(1)} %get-tuple-element.14), channel_id=1, source_target_pairs={{2,0},{4,2},{6,4},{8,6},{10,8},{12,10},{14,12},{16,14},{18,16},{20... | collective-permute-start | bytes 3145736 | tf_op jit(solution)/shard_map/ppermute | solution.py:18
  73.2 2.2 %collective-permute-start.5 = (bf16[4,256,512]{2,1,0:T(8,128)(2,1)S(1)}, bf16[4,256,512]{2,1,0:T(8,128)(2,1)S(1)}, u32[]{:S(2)}, u32[]{:S(2)}) collective-permute-start(bf16[4,256,512]{2,1,0:T(8,128)(2,1)S(1)} %get-tuple-element.15), channel_id=1, source_target_pairs={{2,0},{4,2},{6,4},{8,6},{10,8},{12,10},{14,12},{16,14},{18,16},{20... | collective-permute-start | bytes 3145736 | tf_op jit(solution)/shard_map/ppermute | solution.py:18
  75.4 4.0 %collective-permute-start.3 = (bf16[4,256,512]{2,1,0:T(8,128)(2,1)S(1)}, bf16[4,256,512]{2,1,0:T(8,128)(2,1)S(1)}, u32[]{:S(2)}, u32[]{:S(2)}) collective-permute-start(bf16[4,256,512]{2,1,0:T(8,128)(2,1)S(1)} %get-tuple-element.16), channel_id=1, source_target_pairs={{2,0},{4,2},{6,4},{8,6},{10,8},{12,10},{14,12},{16,14},{18,16},{20... | collective-permute-start | bytes 3145736 | tf_op jit(solution)/shard_map/ppermute | solution.py:18
  79.3 16.9 %collective-permute-done.7.refs_0_ = bf16[4,256,512]{2,1,0:T(8,128)(2,1)S(1)} collective-permute-done((bf16[4,256,512]{2,1,0:T(8,128)(2,1)S(1)}, bf16[4,256,512]{2,1,0:T(8,128)(2,1)S(1)}, u32[]{:S(2)}, u32[]{:S(2)}) %collective-permute-start.7) | collective-permute-done | bytes 1048608 | tf_op jit(solution)/shard_map/ppermute | solution.py:18
  96.2 2.3 %collective-permute-start.8 = (bf16[4,256,512]{2,1,0:T(8,128)(2,1)S(1)}, bf16[4,256,512]{2,1,0:T(8,128)(2,1)S(1)}, u32[]{:S(2)}, u32[]{:S(2)}) collective-permute-start(bf16[4,256,512]{2,1,0:T(8,128)(2,1)S(1)} %collective-permute-done.7.refs_0_), channel_id=1, source_target_pairs={{0,1},{1,0},{2,3},{3,2},{4,5},{5,4},{6,7},{7,6},{8,9},{9,8},{10,11... | collective-permute-start | bytes 3145736 | tf_op jit(solution)/shard_map/ppermute | solution.py:22
  98.5 20.2 %collective-permute-done.5.refs_0_ = bf16[4,256,512]{2,1,0:T(8,128)(2,1)S(1)} collective-permute-done((bf16[4,256,512]{2,1,0:T(8,128)(2,1)S(1)}, bf16[4,256,512]{2,1,0:T(8,128)(2,1)S(1)}, u32[]{:S(2)}, u32[]{:S(2)}) %collective-permute-start.5) | collective-permute-done | bytes 1048608 | tf_op jit(solution)/shard_map/ppermute | solution.py:18
  118.7 2.3 %collective-permute-start.6 = (bf16[4,256,512]{2,1,0:T(8,128)(2,1)S(1)}, bf16[4,256,512]{2,1,0:T(8,128)(2,1)S(1)}, u32[]{:S(2)}, u32[]{:S(2)}) collective-permute-start(bf16[4,256,512]{2,1,0:T(8,128)(2,1)S(1)} %collective-permute-done.5.refs_0_), channel_id=1, source_target_pairs={{0,1},{1,0},{2,3},{3,2},{4,5},{5,4},{6,7},{7,6},{8,9},{9,8},{10,11... | collective-permute-start | bytes 3145736 | tf_op jit(solution)/shard_map/ppermute | solution.py:22
  121.1 4.1 %collective-permute-start.1 = (bf16[2,256,512]{2,1,0:T(8,128)(2,1)S(1)}, bf16[2,256,512]{2,1,0:T(8,128)(2,1)S(1)}, u32[]{:S(2)}, u32[]{:S(2)}) collective-permute-start(bf16[2,256,512]{2,1,0:T(8,128)(2,1)S(1)} %slice.16), channel_id=1, source_target_pairs={{2,0},{4,2},{6,4},{8,6},{10,8},{12,10},{14,12},{16,14},{18,16},{20... | collective-permute-start | bytes 1572872 | tf_op jit(solution)/shard_map/ppermute | solution.py:18
  125.2 16.0 %collective-permute-done.3.refs_0_ = bf16[4,256,512]{2,1,0:T(8,128)(2,1)S(1)} collective-permute-done((bf16[4,256,512]{2,1,0:T(8,128)(2,1)S(1)}, bf16[4,256,512]{2,1,0:T(8,128)(2,1)S(1)}, u32[]{:S(2)}, u32[]{:S(2)}) %collective-permute-start.3) | collective-permute-done | bytes 1048608 | tf_op jit(solution)/shard_map/ppermute | solution.py:18
  141.2 2.3 %collective-permute-start.4 = (bf16[4,256,512]{2,1,0:T(8,128)(2,1)S(1)}, bf16[4,256,512]{2,1,0:T(8,128)(2,1)S(1)}, u32[]{:S(2)}, u32[]{:S(2)}) collective-permute-start(bf16[4,256,512]{2,1,0:T(8,128)(2,1)S(1)} %collective-permute-done.3.refs_0_), channel_id=1, source_target_pairs={{0,1},{1,0},{2,3},{3,2},{4,5},{5,4},{6,7},{7,6},{8,9},{9,8},{10,11... | collective-permute-start | bytes 3145736 | tf_op jit(solution)/shard_map/ppermute | solution.py:22
  143.5 8.9 %collective-permute-done.1.refs_0_ = bf16[2,256,512]{2,1,0:T(8,128)(2,1)S(1)} collective-permute-done((bf16[2,256,512]{2,1,0:T(8,128)(2,1)S(1)}, bf16[2,256,512]{2,1,0:T(8,128)(2,1)S(1)}, u32[]{:S(2)}, u32[]{:S(2)}) %collective-permute-start.1) | collective-permute-done | bytes 524320 | tf_op jit(solution)/shard_map/ppermute | solution.py:18
  153.8 8.7 %applied_part.4 = (f32[4,512,256]{2,1,0:T(8,128)S(1)}, f32[4,512,256]{2,1,0:T(8,128)}) custom-call(s32[2]{0:T(128)S(1)} %pad_add_fusion.places, bf16[14,4,512,512]{3,2,1,0:T(8,128)(2,1)} %through.1.through_ref, bf16[4,256,512]{2,1,0:T(8,128)(2,1)S(1)} %collective-permute-done.7.refs_0_, bf16[4,256,512]{2,1,0:T(8,128)(2,1)S(1)} %collective-permute-done.8.refs_1_), custom_call_target="tpu_custom_call" | custom-call | flops 4294967296 | bytes 8388608 | tf_op jit(solution)/shard_map/applied_part/pallas_call | solution.py:163
  163.8 9.3 %applied_part.5 = (f32[4,512,256]{2,1,0:T(8,128)S(1)}, f32[4,512,256]{2,1,0:T(8,128)}) custom-call(s32[2]{0:T(128)S(1)} %pad_add_fusion.places, bf16[14,4,512,512]{3,2,1,0:T(8,128)(2,1)} %through.1.through_ref, bf16[4,256,512]{2,1,0:T(8,128)(2,1)S(1)} %collective-permute-done.5.refs_0_, bf16[4,256,512]{2,1,0:T(8,128)(2,1)S(1)} %collective-permute-done.6.refs_1_, ...), custom_call_target="tpu_custom_call" | custom-call | flops 4294967296 | bytes 8388608 | tf_op jit(solution)/shard_map/applied_part/pallas_call | solution.py:163
  174.4 9.3 %applied_part.6 = (f32[4,512,256]{2,1,0:T(8,128)S(1)}, f32[4,512,256]{2,1,0:T(8,128)}) custom-call(s32[2]{0:T(128)S(1)} %pad_add_fusion.places, bf16[14,4,512,512]{3,2,1,0:T(8,128)(2,1)} %through.1.through_ref, bf16[4,256,512]{2,1,0:T(8,128)(2,1)S(1)} %collective-permute-done.3.refs_0_, bf16[4,256,512]{2,1,0:T(8,128)(2,1)S(1)} %collective-permute-done.4.refs_1_, ...), custom_call_target="tpu_custom_call" | custom-call | flops 4294967296 | bytes 8388608 | tf_op jit(solution)/shard_map/applied_part/pallas_call | solution.py:163
  183.7 5.8 %applied_part.7 = bf16[4,512,512]{2,1,0:T(8,128)(2,1)S(1)} custom-call(s32[2]{0:T(128)S(1)} %pad_add_fusion.places, bf16[14,4,512,512]{3,2,1,0:T(8,128)(2,1)} %through.1.through_ref, bf16[2,256,512]{2,1,0:T(8,128)(2,1)S(1)} %collective-permute-done.1.refs_0_, bf16[2,256,512]{2,1,0:T(8,128)(2,1)S(1)} %collective-permute-done.2.refs_1_, ...), custom_call_target="tpu_custom_call" | custom-call | flops 2147483648 | bytes 4194304 | tf_op jit(solution)/shard_map/applied_part/pallas_call | solution.py:163
  190.8 4.1 %broadcast_in_dim_reshape.3 = bf16[1,4,256,2,512]{4,3,2,1,0:T(2,128)(2,1)} reshape(bf16[4,512,512]{2,1,0:T(8,128)(2,1)} %copy-done) | data formatting | bytes 4194304 | tf_op jit(solution)/shard_map/broadcast_in_dim;reshape | solution.py:229
  194.9 19.8 %env_rows.3 = bf16[14,256,512]{2,1,0:T(8,128)(2,1)} custom-call(s32[2]{0:T(128)S(1)} %pad_add_fusion.places, bf16[512,2048]{1,0:T(8,128)(2,1)S(1)} %copy.13.wave_ref, bf16[14,4,512,512]{3,2,1,0:T(8,128)(2,1)} %through.1.through_ref, bf16[14,256,512]{2,1,0:T(8,128)(2,1)} %collective-permute-done.9.refs_0_), custom_call_target="tpu_custom_call" | custom-call | flops 7516192768 | bytes 29360128 | tf_op jit(solution)/shard_map/env_rows/pallas_call | solution.py:108
  (25 shorter events, 6.6 us)
Async XLA Ops:
  0.6 4.0 %copy-start.4 = (bf16[14,2,2,14]{3,2,1,0:T(2,128)(2,1)S(1)}, bf16[14,2,2,14]{3,2,1,0:T(2,128)(2,1)}, u32[]{:S(2)}) copy-start(bf16[14,2,2,14]{3,2,1,0:T(2,128)(2,1)} %param.7) | copy-start | bytes 4708
  3.9 12.7 %collective-permute-start = (bf16[4,2,256,512]{3,2,1,0:T(8,128)(2,1)}, bf16[4,2,256,512]{3,2,1,0:T(8,128)(2,1)}, u32[]{:S(2)}, u32[]{:S(2)}) collective-permute-start(bf16[4,2,256,512]{3,2,1,0:T(8,128)(2,1)} %bitcast.18.clone.2.refs_2_), channel_id=1, source_target_pairs={{0,1},{1,0},{2,3},{3,2},{4,5},{5,4},{6,7},{7,6},{8,9},{9,8},{10,11... | collective-permute-start | bytes 6291464 | tf_op jit(solution)/shard_map/ppermute | solution.py:22
  50.0 19.9 %copy-start.3 = (bf16[1,256,14,512]{3,1,2,0:T(8,128)(2,1)S(1)}, bf16[1,256,14,512]{3,1,2,0:T(8,128)(2,1)}, u32[]{:S(2)}) copy-start(bf16[1,256,14,512]{3,1,2,0:T(8,128)(2,1)} %param.5) | copy-start | bytes 11010052
  69.9 125.0 %collective-permute-start.9 = (bf16[14,256,512]{2,1,0:T(8,128)(2,1)}, bf16[14,256,512]{2,1,0:T(8,128)(2,1)}, u32[]{:S(2)}, u32[]{:S(2)}) collective-permute-start(bf16[14,256,512]{2,1,0:T(8,128)(2,1)} %env_rows.2), channel_id=1, source_target_pairs={{0,1},{1,0},{2,3},{3,2},{4,5},{5,4},{6,7},{7,6},{8,9},{9,8},{10,11... | collective-permute-start | bytes 11010056 | tf_op jit(solution)/shard_map/ppermute | solution.py:22
  70.1 26.1 %collective-permute-start.7 = (bf16[4,256,512]{2,1,0:T(8,128)(2,1)S(1)}, bf16[4,256,512]{2,1,0:T(8,128)(2,1)S(1)}, u32[]{:S(2)}, u32[]{:S(2)}) collective-permute-start(bf16[4,256,512]{2,1,0:T(8,128)(2,1)S(1)} %get-tuple-element.14), channel_id=1, source_target_pairs={{2,0},{4,2},{6,4},{8,6},{10,8},{12,10},{14,12},{16,14},{18,16},{20... | collective-permute-start | bytes 3145736 | tf_op jit(solution)/shard_map/ppermute | solution.py:18
  73.2 45.5 %collective-permute-start.5 = (bf16[4,256,512]{2,1,0:T(8,128)(2,1)S(1)}, bf16[4,256,512]{2,1,0:T(8,128)(2,1)S(1)}, u32[]{:S(2)}, u32[]{:S(2)}) collective-permute-start(bf16[4,256,512]{2,1,0:T(8,128)(2,1)S(1)} %get-tuple-element.15), channel_id=1, source_target_pairs={{2,0},{4,2},{6,4},{8,6},{10,8},{12,10},{14,12},{16,14},{18,16},{20... | collective-permute-start | bytes 3145736 | tf_op jit(solution)/shard_map/ppermute | solution.py:18
  75.4 65.8 %collective-permute-start.3 = (bf16[4,256,512]{2,1,0:T(8,128)(2,1)S(1)}, bf16[4,256,512]{2,1,0:T(8,128)(2,1)S(1)}, u32[]{:S(2)}, u32[]{:S(2)}) collective-permute-start(bf16[4,256,512]{2,1,0:T(8,128)(2,1)S(1)} %get-tuple-element.16), channel_id=1, source_target_pairs={{2,0},{4,2},{6,4},{8,6},{10,8},{12,10},{14,12},{16,14},{18,16},{20... | collective-permute-start | bytes 3145736 | tf_op jit(solution)/shard_map/ppermute | solution.py:18
  96.2 57.5 %collective-permute-start.8 = (bf16[4,256,512]{2,1,0:T(8,128)(2,1)S(1)}, bf16[4,256,512]{2,1,0:T(8,128)(2,1)S(1)}, u32[]{:S(2)}, u32[]{:S(2)}) collective-permute-start(bf16[4,256,512]{2,1,0:T(8,128)(2,1)S(1)} %collective-permute-done.7.refs_0_), channel_id=1, source_target_pairs={{0,1},{1,0},{2,3},{3,2},{4,5},{5,4},{6,7},{7,6},{8,9},{9,8},{10,11... | collective-permute-start | bytes 3145736 | tf_op jit(solution)/shard_map/ppermute | solution.py:22
  118.7 45.1 %collective-permute-start.6 = (bf16[4,256,512]{2,1,0:T(8,128)(2,1)S(1)}, bf16[4,256,512]{2,1,0:T(8,128)(2,1)S(1)}, u32[]{:S(2)}, u32[]{:S(2)}) collective-permute-start(bf16[4,256,512]{2,1,0:T(8,128)(2,1)S(1)} %collective-permute-done.5.refs_0_), channel_id=1, source_target_pairs={{0,1},{1,0},{2,3},{3,2},{4,5},{5,4},{6,7},{7,6},{8,9},{9,8},{10,11... | collective-permute-start | bytes 3145736 | tf_op jit(solution)/shard_map/ppermute | solution.py:22
  121.1 31.4 %collective-permute-start.1 = (bf16[2,256,512]{2,1,0:T(8,128)(2,1)S(1)}, bf16[2,256,512]{2,1,0:T(8,128)(2,1)S(1)}, u32[]{:S(2)}, u32[]{:S(2)}) collective-permute-start(bf16[2,256,512]{2,1,0:T(8,128)(2,1)S(1)} %slice.16), channel_id=1, source_target_pairs={{2,0},{4,2},{6,4},{8,6},{10,8},{12,10},{14,12},{16,14},{18,16},{20... | collective-permute-start | bytes 1572872 | tf_op jit(solution)/shard_map/ppermute | solution.py:18
  141.2 33.3 %collective-permute-start.4 = (bf16[4,256,512]{2,1,0:T(8,128)(2,1)S(1)}, bf16[4,256,512]{2,1,0:T(8,128)(2,1)S(1)}, u32[]{:S(2)}, u32[]{:S(2)}) collective-permute-start(bf16[4,256,512]{2,1,0:T(8,128)(2,1)S(1)} %collective-permute-done.3.refs_0_), channel_id=1, source_target_pairs={{0,1},{1,0},{2,3},{3,2},{4,5},{5,4},{6,7},{7,6},{8,9},{9,8},{10,11... | collective-permute-start | bytes 3145736 | tf_op jit(solution)/shard_map/ppermute | solution.py:22
  152.4 31.3 %collective-permute-start.2 = (bf16[2,256,512]{2,1,0:T(8,128)(2,1)S(1)}, bf16[2,256,512]{2,1,0:T(8,128)(2,1)S(1)}, u32[]{:S(2)}, u32[]{:S(2)}) collective-permute-start(bf16[2,256,512]{2,1,0:T(8,128)(2,1)S(1)} %collective-permute-done.1.refs_0_), channel_id=1, source_target_pairs={{0,1},{1,0},{2,3},{3,2},{4,5},{5,4},{6,7},{7,6},{8,9},{9,8},{10,11... | collective-permute-start | bytes 1572872 | tf_op jit(solution)/shard_map/ppermute | solution.py:22
  162.5 1.3 copy-start.2
  173.1 1.3 copy-start.1
  189.5 1.3 copy-start

commit v2 on v0

v2 whole, which is shorter than its diff:
```python
import functools
import math

import jax
import jax.numpy as jnp
from jax import lax
from jax.experimental import pallas as pl
from jax.experimental.pallas import tpu as pltpu
from jax.sharding import PartitionSpec as P

GROUP = 8
MIB = 1 << 20
ANY = pl.BlockSpec(memory_space=pl.ANY)


def passed_along(array, axis, by):
    size = lax.axis_size(axis)
    pairs = [(i, i + by) for i in range(size) if 0 <= i + by < size]
    return lax.ppermute(array, axis, pairs)


def swapped(array, axis):
    return lax.ppermute(array, axis, [(0, 1), (1, 0)])


def product(left, right, contract):
    return lax.dot_general(left, right, (contract, ((), ())), preferred_element_type=jnp.float32)


def after(array, *others):
    return pl.pallas_call(
        lambda *refs: None,
        in_specs=[ANY] * (1 + len(others)),
        out_specs=ANY,
        out_shape=jax.ShapeDtypeStruct(array.shape, array.dtype),
        input_output_aliases={0: 0},
        name="after",
    )(array, *others)


def block_diagonal(bonds, mw, phys):
    size = mw * phys
    full = size * GROUP
    row = lax.broadcasted_iota(jnp.int32, (full, size), 0)
    which = lax.broadcasted_iota(jnp.int32, (full, size), 1)
    pick_row = (row // (GROUP * phys) * phys + row % phys == which).astype(jnp.bfloat16)
    column = lax.broadcasted_iota(jnp.int32, (size, full), 1)
    which = lax.broadcasted_iota(jnp.int32, (size, full), 0)
    pick_column = (column // GROUP == which).astype(jnp.bfloat16)
    spread = product(pick_row, bonds, ((1,), (0,))).astype(jnp.bfloat16)
    spread = product(spread, pick_column, ((1,), (0,)))
    row = lax.broadcasted_iota(jnp.int32, (full, full), 0)
    column = lax.broadcasted_iota(jnp.int32, (full, full), 1)
    same = row % (GROUP * phys) // phys == column % GROUP
    return jnp.where(same, spread, 0.0).astype(jnp.bfloat16)


def sweep_kernel(parts, scaling, places, bonds_ref, *refs):
    envs, refs = refs[:parts], refs[parts:]
    waves, refs = refs[:parts], refs[parts:]
    here_ref, through_ref, refs = refs[0], refs[1], refs[2:]
    outs, refs = refs[:parts], refs[parts:]
    table, lhs, low, turned, total, stage, sems = refs
    mw, rows, _ = envs[0].shape
    num_states, phys, _, chi = waves[0].shape
    groups = rows // GROUP
    part = mw * GROUP
    step, steps = pl.program_id(0), pl.num_programs(0)

    @pl.when(step == 0)
    def _():
        table[...] = block_diagonal(bonds_ref[...], mw, phys)

    env = jnp.concatenate([env[...] for env in envs], axis=2).astype(jnp.float32)
    env = env.reshape(mw, groups, GROUP, chi)
    for g in range(groups):
        lhs[g * part : (g + 1) * part, :] = env[:, g].reshape(part, chi).astype(jnp.bfloat16)
    depth = rows * phys
    for k in range(num_states):
        turned[:, k * depth : (k + 1) * depth] = here_ref[k].T

    def state(k, _):
        for t in range(phys):
            wave = jnp.concatenate([wave[k, t] for wave in waves], axis=0)
            low[t] = product(lhs[...], wave, ((1,), (0,))).astype(jnp.bfloat16)
        for g in range(groups):
            right = jnp.concatenate([low[t, g * part : (g + 1) * part] for t in range(phys)], axis=0)
            through = product(table[...], right, ((1,), (0,))).astype(jnp.bfloat16)
            size = GROUP * phys
            through_ref[:, k, g * size : (g + 1) * size, :] = through.reshape(mw, size, chi)
        return 0

    lax.fori_loop(0, num_states, state, 0)

    def copies(v, slot):
        found = []
        for index, out in enumerate(outs):
            width = out.shape[1]
            at = pl.multiple_of(places[index] * width, width)
            found.append(
                pltpu.make_async_copy(
                    stage.at[slot, pl.ds(at, width)], out.at[v], sems.at[slot, index]
                )
            )
        return found

    def bond(v, _):
        right = through_ref[v].reshape(num_states * depth, chi)
        before = jnp.where(step == 0, 0.0, total[v])
        now = before + product(turned[...], right, ((1,), (0,)))

        @pl.when(step < steps - 1)
        def _():
            total[v] = now

        @pl.when(step == steps - 1)
        def _():
            slot = v % 2

            @pl.when(v >= 2)
            def _():
                for copy in copies(v - 2, slot):
                    copy.wait()

            stage[slot] = (now * scaling).astype(jnp.bfloat16)
            for copy in copies(v, slot):
                copy.start()

        return 0

    lax.fori_loop(0, mw, bond, 0)

    @pl.when(step == steps - 1)
    def _():
        for v in range(max(mw - 2, 0), mw):
            for copy in copies(v, v % 2):
                copy.wait()


def sweep(bonds, env, waves, here, places, scaling):
    mw, rows_all, chi_in = env.shape
    num_states, phys, _, chi = waves[0].shape
    rows = min(64, rows_all)
    parts = len(waves)
    width = chi_in // parts
    once = pl.Buffered(1)

    def env_spec(part):
        return pl.BlockSpec((mw, rows, width), lambda i, at: (0, i, at[part]))

    share = jax.ShapeDtypeStruct((mw, chi // parts, chi), jnp.bfloat16)
    return pl.pallas_call(
        functools.partial(sweep_kernel, parts, scaling),
        grid_spec=pltpu.PrefetchScalarGridSpec(
            num_scalar_prefetch=1,
            grid=(rows_all // rows,),
            in_specs=[pl.BlockSpec(bonds.shape, lambda i, at: (0, 0), pipeline_mode=once)]
            + [env_spec(part) for part in range(parts)]
            + [
                pl.BlockSpec(wave.shape, lambda i, at: (0, 0, 0, 0), pipeline_mode=once)
                for wave in waves
            ]
            + [pl.BlockSpec((num_states, rows * phys, chi), lambda i, at: (0, i, 0))],
            out_specs=[
                pl.BlockSpec((mw, num_states, rows * phys, chi), lambda i, at: (0, 0, i, 0))
            ]
            + [ANY] * parts,
            scratch_shapes=[
                pltpu.VMEM((mw * phys * GROUP, mw * phys * GROUP), jnp.bfloat16),
                pltpu.VMEM((mw * rows, chi_in), jnp.bfloat16),
                pltpu.VMEM((phys, mw * rows, chi), jnp.bfloat16),
                pltpu.VMEM((chi, num_states * rows * phys), jnp.bfloat16),
                pltpu.VMEM((mw, chi, chi), jnp.float32),
                pltpu.VMEM((2, chi, chi), jnp.bfloat16),
                pltpu.SemaphoreType.DMA((2, parts)),
            ],
        ),
        out_shape=[
            jax.ShapeDtypeStruct((mw, num_states, rows_all * phys, chi), jnp.bfloat16)
        ]
        + [share] * parts,
        compiler_params=pltpu.CompilerParams(vmem_limit_bytes=56 * MIB),
        cost_estimate=pl.CostEstimate(
            flops=5 * mw * rows_all * chi_in * num_states * phys * chi,
            bytes_accessed=2 * mw * num_states * rows_all * phys * chi,
            transcendentals=0,
        ),
        name="sweep",
    )(places, bonds, *([env] * parts), *waves, here)


def applied_kernel(begun, phys, places, through_ref, right_ref, *refs):
    out_ref = refs[-1]
    last = out_ref.dtype == jnp.bfloat16
    v = pl.program_id(1)
    for k in range(through_ref.shape[1]):
        term = product(through_ref[0, k], right_ref[0], ((1,), (1,)))
        if last:
            term = term + refs[0][k] if begun else term
            rows, width = term.shape
            out_ref[k] = term.astype(jnp.bfloat16).reshape(rows // phys, phys, width)
        elif begun:
            out_ref[k] = term + jnp.where(v == 0, refs[0][k], out_ref[k])
        else:
            out_ref[k] = term + jnp.where(v == 0, 0.0, out_ref[k])


def applied_part(through, right, held, at, places, part, phys, last, earlier):
    mw, num_states, rows, chi = through.shape
    count, width, _ = right.shape
    together = 1 if count == 1 else num_states
    begun = held is not None
    if last:
        assert count == 1
        out_shape = jax.ShapeDtypeStruct((num_states, rows // phys, phys, chi), jnp.bfloat16)
        out_spec = pl.BlockSpec(
            (together, rows // phys, phys, width), lambda j, v, at: (j, 0, 0, at[part])
        )
    else:
        out_shape = jax.ShapeDtypeStruct((num_states, rows, width), jnp.float32)
        out_spec = pl.BlockSpec((together, rows, width), lambda j, v, at: (j, 0, 0))
    operands = [through, right]
    in_specs = [
        pl.BlockSpec((1, together, rows, chi), lambda j, v, _: (at + v, j, 0, 0)),
        pl.BlockSpec((1, width, chi), lambda j, v, _: (v, 0, 0)),
    ]
    if begun:
        operands.append(held)
        in_specs.append(pl.BlockSpec((together, rows, width), lambda j, v, _: (j, 0, 0)))
    aliases = {}
    if earlier is not None:
        if last and earlier.shape == out_shape.shape:
            aliases = {1 + len(operands): 0}
        operands.append(earlier)
        in_specs.append(ANY)
    return pl.pallas_call(
        functools.partial(applied_kernel, begun, phys),
        grid_spec=pltpu.PrefetchScalarGridSpec(
            num_scalar_prefetch=1,
            grid=(num_states // together, count),
            in_specs=in_specs,
            out_specs=out_spec,
        ),
        out_shape=out_shape,
        input_output_aliases=aliases,
        compiler_params=pltpu.CompilerParams(vmem_limit_bytes=32 * MIB),
        cost_estimate=pl.CostEstimate(
            flops=2 * num_states * rows * width * count * chi,
            bytes_accessed=2 * count * num_states * rows * chi,
            transcendentals=0,
        ),
        name="applied_part",
    )(places, *operands)


def cuts(size):
    middle = max((size - 1) * 5 // 13, 0)
    sizes = [count for count in (size - 1 - middle, middle, 1) if count > 0]
    found, at = [], 0
    for count in sizes:
        found.append((at, count))
        at += count
    return found


def on_device(left_env, right_env, states, mpo):
    num_states, rows, phys, chi = states.shape[1:]
    mw = mpo.shape[0]
    bonds = lax.axis_size("bond")
    paired = bonds == 2
    me = lax.axis_index("bond").astype(jnp.int32)
    places = jnp.stack([me, 1 - me]) if paired else jnp.stack([me, me]) * 0
    scaling = 1.0 / math.sqrt(num_states * chi)
    left = left_env[0].transpose(1, 0, 2)
    right = right_env[0].transpose(1, 0, 2)

    pieces = [(at, passed_along(right[at : at + count], "seg", -1)) for at, count in cuts(mw)]

    wave_split = states[0].transpose(0, 2, 1, 3)
    if paired:
        waves = [wave_split, swapped(wave_split, "bond")]
    else:
        waves = [lax.all_gather(wave_split, "bond", axis=2, tiled=True)]
    here = states[0].reshape(num_states, rows * phys, chi)
    bond_table = mpo.transpose(3, 1, 2, 0).reshape(mw * phys, phys * mw)
    through, *shares = sweep(bond_table, left, waves, here, places, scaling)

    if paired:
        arrived = swapped(shares[1], "bond")
        new_env = shares[0].astype(jnp.float32) + arrived.astype(jnp.float32)
        new_env = new_env.astype(jnp.bfloat16)
    else:
        new_env = lax.psum_scatter(shares[0], "bond", scatter_dimension=1, tiled=True)

    sums = [None, None]
    done = None
    for index, (at, piece) in enumerate(pieces):
        last = index == len(pieces) - 1
        if paired:
            piece = after(piece, through if done is None else done)
            rights = [piece, swapped(piece, "bond")]
        else:
            rights = [lax.all_gather(piece, "bond", axis=1, tiled=True)]
        for part, block in enumerate(rights):
            done = applied_part(through, block, sums[part], at, places, part, phys, last, done)
            if not last:
                sums[part] = done
    return (done[None], new_env.transpose(1, 0, 2)[None])


def solution(mesh):
    in_specs = (
        P("seg", "bond", None, None),
        P("seg", "bond", None, None),
        P("seg", None, "bond", None, None),
        P(),
    )
    out_specs = (P("seg", None, "bond", None, None), P("seg", "bond", None, None))
    return jax.shard_map(
        on_device, mesh=mesh, in_specs=in_specs, out_specs=out_specs, check_vma=False
    )
```

time: 312 us -> 162 us (0.52)
  the two profiles are of different devices: /device:TPU:22 before, /device:TPU:13 now
where the time goes in v2:
time: 162 us; the launch traced here: 159 us
  Pallas kernels  111 us (69%)
  local copies, waits for them, and re-layouts  24.8 us (15%)
  starting transfers between devices  11 us (7%)
  waiting for transfers between devices  5.93 us (4%)
  other arithmetic  5.63 us (3%)
    pallas_call x1, Pallas kernels, sweep(): pl.pallas_call(functools.partial(sweep_kernel, parts, scaling), grid_spec...  62.6 us
    pallas_call x6, Pallas kernels, applied_part(): pl.pallas_call(functools.partial(applied_kernel, begun, phys), grid_spec=...  48 us
    unnamed x37, local copies, waits for them, and re-layouts  15.8 us
    ppermute x3, starting transfers between devices, passed_along(): return lax.ppermute(array, axis, pairs)  8.27 us
    ppermute x3, waiting for transfers between devices, passed_along(): return lax.ppermute(array, axis, pairs)  5.92 us
    broadcast_in_dim x1, other arithmetic, on_device(): return (done[None], new_env.transpose(1, 0, 2)[None])  5.04 us
    another operation x1, local copies, waits for them, and re-layouts, on_device(): here = states[0].reshape(num_states, rows * phys, chi)  4.11 us
    slice x3, local copies, waits for them, and re-layouts, on_device(): right[at:at + count]  4.06 us
  transfers between devices with their start and end apart: 8, of which 1 were waited for; matrix products, arithmetic and copies ran while one was open for 6% of the time, Pallas kernels for 70%

profile of v2, /device:TPU:13, one launch (start us, length us, event | category | flops | bytes accessed | tf_op | source)
XLA Modules:
  0.0 158.8 jit_solution(9030623871868387724)
XLA Ops:
  0.6 3.4 %copy.13 = bf16[1,4,256,2,512]{4,2,3,1,0:T(8,128)(2,1)} copy(bf16[1,4,256,2,512]{4,3,2,1,0:T(2,128)(2,1)} %param.6) | data formatting | bytes 4194304 | tf_op args[2]
  4.8 1.5 slice.14
  6.3 3.0 %collective-permute-start.3 = (bf16[8,256,512]{2,1,0:T(8,128)(2,1)}, bf16[8,256,512]{2,1,0:T(8,128)(2,1)S(1)}, u32[]{:S(2)}, u32[]{:S(2)}) collective-permute-start(bf16[8,256,512]{2,1,0:T(8,128)(2,1)} %slice.14), channel_id=1, source_target_pairs={{2,0},{4,2},{6,4},{8,6},{10,8},{12,10},{14,12},{16,14},{18,16},{20... | collective-permute-start | bytes 6291464 | tf_op jit(solution)/shard_map/ppermute | solution.py:19
  9.4 4.1 %reshape_squeeze.3.refs_4_ = bf16[4,512,512]{2,1,0:T(8,128)(2,1)} reshape(bf16[1,4,256,2,512]{4,3,2,1,0:T(2,128)(2,1)} %param.6) | data formatting | bytes 4194304 | tf_op jit(solution)/shard_map/reshape;squeeze | solution.py:284
  14.9 62.6 %sweep.1 = (bf16[14,4,512,512]{3,2,1,0:T(8,128)(2,1)}, bf16[14,256,512]{2,1,0:T(8,128)(2,1)}, bf16[14,256,512]{2,1,0:T(8,128)(2,1)}) custom-call(s32[2]{0:T(128)} %pad_add_fusion.places, bf16[28,28]{1,0:T(8,128)(2,1)} %reshape.7.bonds_ref, bf16[14,256,512]{2,1,0:T(8,128)(2,1)} %bitcast.24, bf16[14,256,512]{2,1,0:T(8,128)(2,1)} %bitcast.25, ...), custom_call_target="tpu_custom_call" | custom-call | flops 37580963840 | bytes 29360128 | tf_op jit(solution)/shard_map/sweep/pallas_call | solution.py:152
  77.6 1.3 copy-done.8
  79.4 1.6 slice.13
  81.0 2.2 %collective-permute-start.2 = (bf16[5,256,512]{2,1,0:T(8,128)(2,1)S(1)}, bf16[5,256,512]{2,1,0:T(8,128)(2,1)S(1)}, u32[]{:S(2)}, u32[]{:S(2)}) collective-permute-start(bf16[5,256,512]{2,1,0:T(8,128)(2,1)S(1)} %slice.13), channel_id=1, source_target_pairs={{2,0},{4,2},{6,4},{8,6},{10,8},{12,10},{14,12},{16,14},{18,16},{20... | collective-permute-start | bytes 3932168 | tf_op jit(solution)/shard_map/ppermute | solution.py:19
  83.1 11.2 %applied_part.6.refs_0_ = f32[4,512,256]{2,1,0:T(8,128)S(1)} custom-call(s32[2]{0:T(128)S(1)} %copy-done.14, bf16[14,4,512,512]{3,2,1,0:T(8,128)(2,1)} %get-tuple-element.5.refs_1_.through_ref, bf16[8,256,512]{2,1,0:T(8,128)(2,1)S(1)} %copy-done.9), custom_call_target="tpu_custom_call" | custom-call | flops 4294967296 | bytes 16777216 | tf_op jit(solution)/shard_map/applied_part/pallas_call | solution.py:236
  94.4 11.3 %applied_part.7.refs_1_.refs_0_ = f32[4,512,256]{2,1,0:T(8,128)S(1)} custom-call(s32[2]{0:T(128)S(1)} %copy-done.14, bf16[14,4,512,512]{3,2,1,0:T(8,128)(2,1)} %get-tuple-element.5.refs_1_.through_ref, bf16[8,256,512]{2,1,0:T(8,128)(2,1)S(1)} %collective-permute-done.4.right_ref, f32[4,512,256]{2,1,0:T(8,128)S(1)} %applied_part.6.refs_0_), custom_call_target="tpu_custom_call" | custom-call | flops 4294967296 | bytes 16777216 | tf_op jit(solution)/shard_map/applied_part/pallas_call | solution.py:236
  105.7 1.3 copy-done
  107.0 5.9 %collective-permute-done.2.refs_0_ = bf16[5,256,512]{2,1,0:T(8,128)(2,1)S(1)} collective-permute-done((bf16[5,256,512]{2,1,0:T(8,128)(2,1)S(1)}, bf16[5,256,512]{2,1,0:T(8,128)(2,1)S(1)}, u32[]{:S(2)}, u32[]{:S(2)}) %collective-permute-start.2) | collective-permute-done | bytes 1310752 | tf_op jit(solution)/shard_map/ppermute | solution.py:19
  114.0 1.1 collective-permute-start.5
  116.1 3.1 %collective-permute-start.1 = (bf16[1,256,512]{2,1,0:T(8,128)(2,1)S(1)}, bf16[1,256,512]{2,1,0:T(8,128)(2,1)S(1)}, u32[]{:S(2)}, u32[]{:S(2)}) collective-permute-start(bf16[1,256,512]{2,1,0:T(8,128)(2,1)S(1)} %slice.12), channel_id=1, source_target_pairs={{2,0},{4,2},{6,4},{8,6},{10,8},{12,10},{14,12},{16,14},{18,16},{20... | collective-permute-start | bytes 786440 | tf_op jit(solution)/shard_map/ppermute | solution.py:19
  119.2 1.6 copy-done.5
  120.8 1.3 copy-done.11
  122.1 7.6 %applied_part.8.refs_1_.refs_0_ = f32[4,512,256]{2,1,0:T(8,128)S(1)} custom-call(s32[2]{0:T(128)S(1)} %copy-done.14, bf16[14,4,512,512]{3,2,1,0:T(8,128)(2,1)} %get-tuple-element.5.refs_1_.through_ref, bf16[5,256,512]{2,1,0:T(8,128)(2,1)S(1)} %copy-done.11, f32[4,512,256]{2,1,0:T(8,128)S(1)} %copy-done.5, f32[4,512,256]{2,1,0:T(8,128)S(1)} %copy-done.1), custom_call_target="tpu_custom_call" | custom-call | flops 2684354560 | bytes 10485760 | tf_op jit(solution)/shard_map/applied_part/pallas_call | solution.py:236
  129.7 8.1 %applied_part.9.refs_1_.refs_0_ = f32[4,512,256]{2,1,0:T(8,128)S(1)} custom-call(s32[2]{0:T(128)S(1)} %copy-done.14, bf16[14,4,512,512]{3,2,1,0:T(8,128)(2,1)} %get-tuple-element.5.refs_1_.through_ref, bf16[5,256,512]{2,1,0:T(8,128)(2,1)S(1)} %collective-permute-done.5.right_ref, f32[4,512,256]{2,1,0:T(8,128)S(1)} %copy-done.1, ...), custom_call_target="tpu_custom_call" | custom-call | flops 2684354560 | bytes 10485760 | tf_op jit(solution)/shard_map/applied_part/pallas_call | solution.py:236
  137.8 1.3 copy-done.2
  140.3 1.1 copy-done.3
  141.5 1.6 %copy-done.7 = f32[4,512,256]{2,1,0:T(8,128)S(1)} copy-done((f32[4,512,256]{2,1,0:T(8,128)S(1)}, f32[4,512,256]{2,1,0:T(8,128)}, u32[]{:S(2)}) %copy-start.7) | copy-done | bytes 2097176
  144.0 4.8 %applied_part.10.refs_1_ = bf16[4,256,2,512]{3,2,1,0:T(2,128)(2,1)} custom-call(s32[2]{0:T(128)S(1)} %copy-done.14, bf16[14,4,512,512]{3,2,1,0:T(8,128)(2,1)} %get-tuple-element.5.refs_1_.through_ref, bf16[1,256,512]{2,1,0:T(8,128)(2,1)S(1)} %copy-done.13, f32[4,512,256]{2,1,0:T(8,128)S(1)} %copy-done.7, f32[4,512,256]{2,1,0:T(8,128)S(1)} %copy-done.3), custom_call_target="tpu_custom_call" | custom-call | flops 536870912 | bytes 2097152 | tf_op jit(solution)/shard_map/applied_part/pallas_call | solution.py:236
  148.8 5.0 %applied_part.11 = bf16[4,256,2,512]{3,2,1,0:T(2,128)(2,1)} custom-call(s32[2]{0:T(128)S(1)} %copy-done.14, bf16[14,4,512,512]{3,2,1,0:T(8,128)(2,1)} %get-tuple-element.5.refs_1_.through_ref, bf16[1,256,512]{2,1,0:T(8,128)(2,1)S(1)} %collective-permute-done.6.right_ref, f32[4,512,256]{2,1,0:T(8,128)S(1)} %copy-done.3, ...), custom_call_target="tpu_custom_call", output_to_operand_aliasing={{}: (4, {})} | custom-call | flops 536870912 | bytes 2097152 | tf_op jit(solution)/shard_map/applied_part/pallas_call | solution.py:236
  153.8 5.0 %fusion = bf16[1,256,14,512]{3,1,2,0:T(8,128)(2,1)} fusion(bf16[14,256,512]{2,1,0:T(8,128)(2,1)} %collective-permute-done.7, bf16[14,256,512]{2,1,0:T(8,128)(2,1)S(1)} %copy-done.16), kind=kLoop, calls=%fused_computation.1 | loop fusion | flops 7340032 | bytes 11010048 | tf_op jit(solution)/shard_map/broadcast_in_dim | solution.py:308
  (47 shorter events, 6.8 us)
Async XLA Ops:
  0.6 4.1 %copy-start.15 = (bf16[1,256,14,512]{3,1,2,0:T(8,128)(2,1)S(1)}, bf16[1,256,14,512]{3,1,2,0:T(8,128)(2,1)}, u32[]{:S(2)}) copy-start(bf16[1,256,14,512]{3,1,2,0:T(8,128)(2,1)} %param.5) | copy-start | bytes 11010052
  4.1 10.8 %collective-permute-start = (bf16[4,2,256,512]{3,2,1,0:T(8,128)(2,1)}, bf16[4,2,256,512]{3,2,1,0:T(8,128)(2,1)}, u32[]{:S(2)}, u32[]{:S(2)}) collective-permute-start(bf16[4,2,256,512]{3,2,1,0:T(8,128)(2,1)} %bitcast.18.refs_2_), channel_id=1, source_target_pairs={{0,1},{1,0},{2,3},{3,2},{4,5},{5,4},{6,7},{7,6},{8,9},{9,8},{10,11... | collective-permute-start | bytes 6291464 | tf_op jit(solution)/shard_map/ppermute | solution.py:23
  6.3 71.3 %collective-permute-start.3 = (bf16[8,256,512]{2,1,0:T(8,128)(2,1)}, bf16[8,256,512]{2,1,0:T(8,128)(2,1)S(1)}, u32[]{:S(2)}, u32[]{:S(2)}) collective-permute-start(bf16[8,256,512]{2,1,0:T(8,128)(2,1)} %slice.14), channel_id=1, source_target_pairs={{2,0},{4,2},{6,4},{8,6},{10,8},{12,10},{14,12},{16,14},{18,16},{20... | collective-permute-start | bytes 6291464 | tf_op jit(solution)/shard_map/ppermute | solution.py:19
  9.4 4.1 %copy-start.17 = (bf16[14,2,2,14]{3,2,1,0:T(2,128)(2,1)S(1)}, bf16[14,2,2,14]{3,2,1,0:T(2,128)(2,1)}, u32[]{:S(2)}) copy-start(bf16[14,2,2,14]{3,2,1,0:T(2,128)(2,1)} %param.7) | copy-start | bytes 4708
  77.6 1.3 copy-start.8
  78.9 4.3 %copy-start.9 = (bf16[8,256,512]{2,1,0:T(8,128)(2,1)S(1)}, bf16[8,256,512]{2,1,0:T(8,128)(2,1)}, u32[]{:S(2)}) copy-start(bf16[8,256,512]{2,1,0:T(8,128)(2,1)} %after.3.right_ref) | copy-start | bytes 6291460
  78.9 4.3 %copy-start.14 = (s32[2]{0:T(128)S(1)}, s32[2]{0:T(128)}, u32[]{:S(2)}) copy-start(s32[2]{0:T(128)} %pad_add_fusion.places) | copy-start | bytes 28
  78.9 15.5 %collective-permute-start.4 = (bf16[8,256,512]{2,1,0:T(8,128)(2,1)}, bf16[8,256,512]{2,1,0:T(8,128)(2,1)S(1)}, u32[]{:S(2)}, u32[]{:S(2)}) collective-permute-start(bf16[8,256,512]{2,1,0:T(8,128)(2,1)} %after.3.right_ref), channel_id=1, source_target_pairs={{0,1},{1,0},{2,3},{3,2},{4,5},{5,4},{6,7},{7,6},{8,9},{9,8},{10,11... | collective-permute-start | bytes 6291464 | tf_op jit(solution)/shard_map/ppermute | solution.py:23
  79.2 74.6 %collective-permute-start.7 = (bf16[14,256,512]{2,1,0:T(8,128)(2,1)}, bf16[14,256,512]{2,1,0:T(8,128)(2,1)}, u32[]{:S(2)}, u32[]{:S(2)}) collective-permute-start(bf16[14,256,512]{2,1,0:T(8,128)(2,1)} %get-tuple-element.7), channel_id=1, source_target_pairs={{0,1},{1,0},{2,3},{3,2},{4,5},{5,4},{6,7},{7,6},{8,9},{9,8},{10,11... | collective-permute-start | bytes 11010056 | tf_op jit(solution)/shard_map/ppermute | solution.py:23
  81.0 32.0 %collective-permute-start.2 = (bf16[5,256,512]{2,1,0:T(8,128)(2,1)S(1)}, bf16[5,256,512]{2,1,0:T(8,128)(2,1)S(1)}, u32[]{:S(2)}, u32[]{:S(2)}) collective-permute-start(bf16[5,256,512]{2,1,0:T(8,128)(2,1)S(1)} %slice.13), channel_id=1, source_target_pairs={{2,0},{4,2},{6,4},{8,6},{10,8},{12,10},{14,12},{16,14},{18,16},{20... | collective-permute-start | bytes 3932168 | tf_op jit(solution)/shard_map/ppermute | solution.py:19
  94.4 11.3 %copy-start.4 = (f32[4,512,256]{2,1,0:T(8,128)}, f32[4,512,256]{2,1,0:T(8,128)S(1)}, u32[]{:S(2)}) copy-start(f32[4,512,256]{2,1,0:T(8,128)S(1)} %applied_part.6.refs_0_) | copy-start | bytes 6291460
  105.7 1.3 copy-start
  113.0 1.1 copy-start.10
  114.0 5.1 %copy-start.1 = (f32[4,512,256]{2,1,0:T(8,128)S(1)}, f32[4,512,256]{2,1,0:T(8,128)}, u32[]{:S(2)}) copy-start(f32[4,512,256]{2,1,0:T(8,128)} %copy-done) | copy-start | bytes 6291460
  114.0 15.7 %collective-permute-start.5 = (bf16[5,256,512]{2,1,0:T(8,128)(2,1)}, bf16[5,256,512]{2,1,0:T(8,128)(2,1)S(1)}, u32[]{:S(2)}, u32[]{:S(2)}) collective-permute-start(bf16[5,256,512]{2,1,0:T(8,128)(2,1)} %after.4.right_ref), channel_id=1, source_target_pairs={{0,1},{1,0},{2,3},{3,2},{4,5},{5,4},{6,7},{7,6},{8,9},{9,8},{10,11... | collective-permute-start | bytes 3932168 | tf_op jit(solution)/shard_map/ppermute | solution.py:23
  116.1 23.1 %collective-permute-start.1 = (bf16[1,256,512]{2,1,0:T(8,128)(2,1)S(1)}, bf16[1,256,512]{2,1,0:T(8,128)(2,1)S(1)}, u32[]{:S(2)}, u32[]{:S(2)}) collective-permute-start(bf16[1,256,512]{2,1,0:T(8,128)(2,1)S(1)} %slice.12), channel_id=1, source_target_pairs={{2,0},{4,2},{6,4},{8,6},{10,8},{12,10},{14,12},{16,14},{18,16},{20... | collective-permute-start | bytes 786440 | tf_op jit(solution)/shard_map/ppermute | solution.py:19
  119.2 1.6 %copy-start.5 = (f32[4,512,256]{2,1,0:T(8,128)S(1)}, f32[4,512,256]{2,1,0:T(8,128)}, u32[]{:S(2)}) copy-start(f32[4,512,256]{2,1,0:T(8,128)} %copy-done.4) | copy-start | bytes 6291460
  120.8 1.3 copy-start.11
  129.7 8.1 %copy-start.6 = (f32[4,512,256]{2,1,0:T(8,128)}, f32[4,512,256]{2,1,0:T(8,128)S(1)}, u32[]{:S(2)}) copy-start(f32[4,512,256]{2,1,0:T(8,128)S(1)} %applied_part.8.refs_1_.refs_0_) | copy-start | bytes 6291460
  137.8 1.3 copy-start.2
  139.9 1.6 %copy-start.3 = (f32[4,512,256]{2,1,0:T(8,128)S(1)}, f32[4,512,256]{2,1,0:T(8,128)}, u32[]{:S(2)}) copy-start(f32[4,512,256]{2,1,0:T(8,128)} %copy-done.2) | copy-start | bytes 6291460
  139.9 8.9 %collective-permute-start.6 = (bf16[1,256,512]{2,1,0:T(8,128)(2,1)}, bf16[1,256,512]{2,1,0:T(8,128)(2,1)S(1)}, u32[]{:S(2)}, u32[]{:S(2)}) collective-permute-start(bf16[1,256,512]{2,1,0:T(8,128)(2,1)} %after.5.right_ref), channel_id=1, source_target_pairs={{0,1},{1,0},{2,3},{3,2},{4,5},{5,4},{6,7},{7,6},{8,9},{9,8},{10,11... | collective-permute-start | bytes 786440 | tf_op jit(solution)/shard_map/ppermute | solution.py:23
  141.5 1.6 %copy-start.7 = (f32[4,512,256]{2,1,0:T(8,128)S(1)}, f32[4,512,256]{2,1,0:T(8,128)}, u32[]{:S(2)}) copy-start(f32[4,512,256]{2,1,0:T(8,128)} %copy-done.6) | copy-start | bytes 6291460
  148.8 5.0 %copy-start.16 = (bf16[14,256,512]{2,1,0:T(8,128)(2,1)S(1)}, bf16[14,256,512]{2,1,0:T(8,128)(2,1)}, u32[]{:S(2)}) copy-start(bf16[14,256,512]{2,1,0:T(8,128)(2,1)} %get-tuple-element.6) | copy-start | bytes 11010052
  (2 other events, 1.7 us)

commit v3 on v0

v3 whole, which is shorter than its diff:
```python
import functools
import math

import jax
import jax.numpy as jnp
from jax import lax
from jax.experimental import pallas as pl
from jax.experimental.pallas import tpu as pltpu
from jax.sharding import PartitionSpec as P

GROUP = 8
MIB = 1 << 20
SWEEP_MIB = 34
ENV_MIB = 34
APPLIED_MIB = 34
ANY = pl.BlockSpec(memory_space=pl.ANY)


def passed_along(array, axis, by):
    size = lax.axis_size(axis)
    pairs = [(i, i + by) for i in range(size) if 0 <= i + by < size]
    return lax.ppermute(array, axis, pairs)


def swapped(array, axis):
    return lax.ppermute(array, axis, [(0, 1), (1, 0)])


def product(left, right, contract):
    return lax.dot_general(left, right, (contract, ((), ())), preferred_element_type=jnp.float32)


def after(array, *others):
    return pl.pallas_call(
        lambda *refs: None,
        in_specs=[ANY] * (1 + len(others)),
        out_specs=ANY,
        out_shape=jax.ShapeDtypeStruct(array.shape, array.dtype),
        input_output_aliases={0: 0},
        compiler_params=pltpu.CompilerParams(vmem_limit_bytes=MIB),
        name="after",
    )(array, *others)


def block_diagonal(bonds, mw, phys):
    size = mw * phys
    full = size * GROUP
    row = lax.broadcasted_iota(jnp.int32, (full, size), 0)
    which = lax.broadcasted_iota(jnp.int32, (full, size), 1)
    pick_row = (row // (GROUP * phys) * phys + row % phys == which).astype(jnp.bfloat16)
    column = lax.broadcasted_iota(jnp.int32, (size, full), 1)
    which = lax.broadcasted_iota(jnp.int32, (size, full), 0)
    pick_column = (column // GROUP == which).astype(jnp.bfloat16)
    spread = product(pick_row, bonds, ((1,), (0,))).astype(jnp.bfloat16)
    spread = product(spread, pick_column, ((1,), (0,)))
    row = lax.broadcasted_iota(jnp.int32, (full, full), 0)
    column = lax.broadcasted_iota(jnp.int32, (full, full), 1)
    same = row % (GROUP * phys) // phys == column % GROUP
    return jnp.where(same, spread, 0.0).astype(jnp.bfloat16)


def sweep_kernel(parts, places, bonds_ref, env_ref, *refs):
    waves, (through_ref, token_ref, lhs, low) = refs[:parts], refs[parts:]
    mw, rows_all, chi_in = env_ref.shape
    num_states, phys, width, chi = waves[0].shape
    part = mw * GROUP
    groups = lhs.shape[0] // part
    rows = groups * GROUP
    table = block_diagonal(bonds_ref[...], mw, phys)
    depth = table.shape[0]
    padded = low.shape[1]
    table = jnp.concatenate([table, jnp.zeros((depth, padded - depth), table.dtype)], axis=1)
    low[:, depth:, :] = jnp.zeros((groups, padded - depth, chi), low.dtype)

    def block(i, _):
        env = env_ref[:, pl.ds(pl.multiple_of(i * rows, rows), rows), :].astype(jnp.float32)
        if parts == 2:
            first, second = env[..., :width], env[..., width:]
            swap = places[0] != 0
            env = jnp.concatenate(
                [jnp.where(swap, second, first), jnp.where(swap, first, second)], axis=2
            )
        env = env.reshape(mw, groups, GROUP, chi_in)
        for g in range(groups):
            lhs[g * part : (g + 1) * part, :] = env[:, g].reshape(part, chi_in).astype(jnp.bfloat16)

        def state(k, _):
            for t in range(phys):
                wave = jnp.concatenate([wave[k, t] for wave in waves], axis=0)
                inner = product(lhs[...], wave, ((1,), (0,))).astype(jnp.bfloat16)
                low[:, t * part : (t + 1) * part, :] = inner.reshape(groups, part, chi)
            for g in range(groups):
                through = product(table, low[g], ((1,), (0,))).astype(jnp.bfloat16)
                size = GROUP * phys
                at = pl.multiple_of(i * rows * phys + g * size, size)
                through_ref[:, k, pl.ds(at, size), :] = through.reshape(mw, size, chi)
            return 0

        lax.fori_loop(0, num_states, state, 0)
        return 0

    lax.fori_loop(0, rows_all // rows, block, 0)
    token_ref[...] = jnp.zeros_like(token_ref)


TOKEN = jax.ShapeDtypeStruct((8, 128), jnp.float32)
WHOLE = pl.BlockSpec(memory_space=pltpu.VMEM)
SCALARS = pl.BlockSpec(memory_space=pltpu.SMEM)


def held_near(array):
    return pltpu.with_memory_space_constraint(array, pltpu.VMEM)


def sweep(bonds, env, waves, places):
    mw, rows_all, chi_in = env.shape
    num_states, phys, _, chi = waves[0].shape
    rows = min(64, rows_all)
    padded = -(-mw * phys * GROUP // 128) * 128
    return pl.pallas_call(
        functools.partial(sweep_kernel, len(waves)),
        in_specs=[SCALARS] + [WHOLE] * (2 + len(waves)),
        out_specs=[WHOLE] * 2,
        scratch_shapes=[
            pltpu.VMEM((mw * rows, chi_in), jnp.bfloat16),
            pltpu.VMEM((rows // GROUP, padded, chi), jnp.bfloat16),
        ],
        out_shape=[
            pltpu.VMEM((mw, num_states, rows_all * phys, chi), jnp.bfloat16),
            TOKEN,
        ],
        compiler_params=pltpu.CompilerParams(vmem_limit_bytes=SWEEP_MIB * MIB),
        cost_estimate=pl.CostEstimate(
            flops=3 * mw * rows_all * chi_in * num_states * phys * chi,
            bytes_accessed=2 * mw * num_states * rows_all * phys * chi,
            transcendentals=0,
        ),
        name="sweep",
    )(places, bonds, env, *waves)


def env_kernel(parts, scaling, places, here_ref, through_ref, *refs):
    outs, turned = refs[:parts], refs[-1]
    num_states, depth, chi = here_ref.shape
    for k in range(num_states):
        turned[:, k * depth : (k + 1) * depth] = here_ref[k].T

    def bond(v, _):
        right = through_ref[v].reshape(num_states * depth, through_ref.shape[3])
        share = (product(turned[...], right, ((1,), (0,))) * scaling).astype(jnp.bfloat16)
        if parts == 2:
            first, second = share[: chi // 2], share[chi // 2 :]
            swap = places[0] != 0
            outs[0][v] = jnp.where(swap, second, first)
            outs[1][v] = jnp.where(swap, first, second)
        else:
            outs[0][v] = share
        return 0

    lax.fori_loop(0, through_ref.shape[0], bond, 0)


def env_shares(here, through, places, parts, scaling):
    mw, num_states, depth, chi = through.shape
    share = jax.ShapeDtypeStruct((mw, chi // parts, chi), jnp.bfloat16)
    return pl.pallas_call(
        functools.partial(env_kernel, parts, scaling),
        in_specs=[SCALARS, WHOLE, WHOLE],
        out_specs=[WHOLE] * (parts + 1),
        input_output_aliases={2: parts},
        scratch_shapes=[pltpu.VMEM((chi, num_states * depth), jnp.bfloat16)],
        out_shape=[share] * parts + [pltpu.VMEM(through.shape, through.dtype)],
        compiler_params=pltpu.CompilerParams(vmem_limit_bytes=ENV_MIB * MIB),
        cost_estimate=pl.CostEstimate(
            flops=2 * mw * num_states * depth * chi * chi,
            bytes_accessed=2 * mw * num_states * depth * chi,
            transcendentals=0,
        ),
        name="env_shares",
    )(places, here, held_near(through))


def applied_kernel(parts, begun, at, phys, places, through_ref, *refs):
    rights, refs = refs[:parts], refs[parts:]
    if begun:
        held_ref, refs = refs[0], refs[1:]
    out_ref, token_ref, turned = refs[0], refs[1], refs[-1]
    last = out_ref.dtype == jnp.bfloat16
    count, chi = rights[0].shape[0], rights[0].shape[2]
    for v in range(count):
        right = jnp.concatenate([right[v] for right in rights], axis=0)
        turned[v * chi : (v + 1) * chi, :] = right.T

    def state(k, _):
        left = jnp.concatenate([through_ref[at + v, k] for v in range(count)], axis=1)
        total = product(left, turned[...], ((1,), (0,)))
        if begun:
            total = total + held_ref[k]
        if last:
            rows, columns = total.shape
            total = total.astype(jnp.bfloat16)
            if parts == 2:
                own, other = total[:, : columns // 2], total[:, columns // 2 :]
                swap = places[0] != 0
                total = jnp.concatenate(
                    [jnp.where(swap, other, own), jnp.where(swap, own, other)], axis=1
                )
            out_ref[k] = total.reshape(rows // phys, phys, columns)
        else:
            out_ref[k] = total
        return 0

    lax.fori_loop(0, through_ref.shape[1], state, 0)
    token_ref[...] = jnp.zeros_like(token_ref)


def applied_part(through, rights, held, at, places, phys, last):
    mw, num_states, rows, chi = through.shape
    count, width, _ = rights[0].shape
    parts = len(rights)
    begun = held is not None
    if last:
        out_shape = jax.ShapeDtypeStruct(
            (num_states, rows // phys, phys, width * parts), jnp.bfloat16
        )
    else:
        out_shape = jax.ShapeDtypeStruct((num_states, rows, width * parts), jnp.float32)
    operands = [held_near(through), *rights] + ([held] if begun else [])
    return pl.pallas_call(
        functools.partial(applied_kernel, parts, begun, at, phys),
        in_specs=[SCALARS] + [WHOLE] * len(operands),
        out_specs=[WHOLE] * (2 if last else 3),
        out_shape=[out_shape, TOKEN]
        + ([] if last else [pltpu.VMEM(through.shape, through.dtype)]),
        input_output_aliases={} if last else {1: 2},
        scratch_shapes=[pltpu.VMEM((count * chi, width * parts), jnp.bfloat16)],
        compiler_params=pltpu.CompilerParams(vmem_limit_bytes=APPLIED_MIB * MIB),
        cost_estimate=pl.CostEstimate(
            flops=2 * num_states * rows * width * parts * count * chi,
            bytes_accessed=2 * count * num_states * rows * chi,
            transcendentals=0,
        ),
        name="applied_part",
    )(places, *operands)


def cuts(size):
    middle = max((size - 1) * 5 // 13, 0)
    sizes = [count for count in (size - 1 - middle, middle, 1) if count > 0]
    found, at = [], 0
    for count in sizes:
        found.append((at, count))
        at += count
    return found


def on_device(left_env, right_env, states, mpo):
    num_states, rows, phys, chi = states.shape[1:]
    mw = mpo.shape[0]
    bonds = lax.axis_size("bond")
    paired = bonds == 2
    me = lax.axis_index("bond").astype(jnp.int32)
    places = jnp.stack([me, 1 - me]) if paired else jnp.stack([me, me]) * 0
    scaling = 1.0 / math.sqrt(num_states * chi)
    left = left_env[0].transpose(1, 0, 2)
    right = right_env[0].transpose(1, 0, 2)

    pieces = [(at, passed_along(right[at : at + count], "seg", -1)) for at, count in cuts(mw)]

    wave_split = states[0].transpose(0, 2, 1, 3)
    if paired:
        waves = [wave_split, swapped(wave_split, "bond")]
    else:
        waves = [lax.all_gather(wave_split, "bond", axis=2, tiled=True)]
    here = states[0].reshape(num_states, rows * phys, chi)
    bond_table = mpo.transpose(3, 1, 2, 0).reshape(mw * phys, phys * mw)
    through, token = sweep(bond_table, left, waves, places)
    *shares, through = env_shares(here, through, places, len(waves), scaling)
    if paired:
        arrived = swapped(shares[1], "bond")
        new_env = shares[0].astype(jnp.float32) + arrived.astype(jnp.float32)
        new_env = new_env.astype(jnp.bfloat16)
    else:
        new_env = lax.psum_scatter(shares[0], "bond", scatter_dimension=1, tiled=True)

    held = None
    for index, (at, piece) in enumerate(pieces):
        if paired:
            piece = after(piece, token)
            rights = [piece, swapped(piece, "bond")]
        else:
            rights = [lax.all_gather(piece, "bond", axis=1, tiled=True)]
        last = index == len(pieces) - 1
        held, token, *rest = applied_part(through, rights, held, at, places, phys, last)
        through = rest[0] if rest else None
    return (held[None], new_env.transpose(1, 0, 2)[None])


def solution(mesh):
    in_specs = (
        P("seg", "bond", None, None),
        P("seg", "bond", None, None),
        P("seg", None, "bond", None, None),
        P(),
    )
    out_specs = (P("seg", None, "bond", None, None), P("seg", "bond", None, None))
    return jax.shard_map(
        on_device, mesh=mesh, in_specs=in_specs, out_specs=out_specs, check_vma=False
    )
```

time: 312 us -> 173 us (0.55)
  the two profiles are of different devices: /device:TPU:22 before, /device:TPU:13 now
where the time goes in v3:
time: 173 us; the launch traced here: 170 us
  Pallas kernels  85.3 us (49%)
  local copies, waits for them, and re-layouts  35.8 us (21%)
  waiting for transfers between devices  27.8 us (16%)
  starting transfers between devices  13.3 us (8%)
  other arithmetic  6.71 us (4%)
    pallas_call x3, Pallas kernels, applied_part(): pl.pallas_call(functools.partial(applied_kernel, parts, begun, at, phys),...  32.1 us
    pallas_call x1, Pallas kernels, sweep(): pl.pallas_call(functools.partial(sweep_kernel, len(waves)), in_specs=[SCA...  30.3 us
    ppermute x3, waiting for transfers between devices, passed_along(): return lax.ppermute(array, axis, pairs)  27.7 us
    unnamed x23, local copies, waits for them, and re-layouts  26.3 us
    pallas_call x1, Pallas kernels, env_shares(): pl.pallas_call(functools.partial(env_kernel, parts, scaling), in_specs=[S...  22.9 us
    ppermute x3, starting transfers between devices, passed_along(): return lax.ppermute(array, axis, pairs)  10.3 us
    slice x3, local copies, waits for them, and re-layouts, on_device(): right[at:at + count]  6.54 us
    broadcast_in_dim x1, other arithmetic, on_device(): return (held[None], new_env.transpose(1, 0, 2)[None])  6.16 us
  transfers between devices with their start and end apart: 8, of which 2 were waited for; matrix products, arithmetic and copies ran while one was open for 10% of the time, Pallas kernels for 47%

profile of v3, /device:TPU:13, one launch (start us, length us, event | category | flops | bytes accessed | tf_op | source)
XLA Modules:
  0.0 169.6 jit_solution(5452246831143113510)
XLA Ops:
  0.6 3.4 %copy.15 = bf16[1,4,256,2,512]{4,2,3,1,0:T(8,128)(2,1)} copy(bf16[1,4,256,2,512]{4,3,2,1,0:T(2,128)(2,1)} %param.6) | data formatting | bytes 4194304 | tf_op args[2]
  4.7 3.1 %slice.12 = bf16[8,256,512]{2,1,0:T(8,128)(2,1)} slice(bf16[14,256,512]{2,1,0:T(8,128)(2,1)} %bitcast.19), slice={[0:8], [0:256], [0:512]} | slice | bytes 4194304 | tf_op jit(solution)/shard_map/slice | solution.py:268
  7.8 3.1 %collective-permute-start.1 = (bf16[8,256,512]{2,1,0:T(8,128)(2,1)}, bf16[8,256,512]{2,1,0:T(8,128)(2,1)}, u32[]{:S(2)}, u32[]{:S(2)}) collective-permute-start(bf16[8,256,512]{2,1,0:T(8,128)(2,1)} %slice.12), channel_id=1, source_target_pairs={{2,0},{4,2},{6,4},{8,6},{10,8},{12,10},{14,12},{16,14},{18,16},{20... | collective-permute-start | bytes 6291464 | tf_op jit(solution)/shard_map/ppermute | solution.py:22
  10.9 2.2 %reshape_squeeze.3.here_ref = bf16[4,512,512]{2,1,0:T(8,128)(2,1)} reshape(bf16[1,4,256,2,512]{4,3,2,1,0:T(2,128)(2,1)S(1)} %copy-done.7) | data formatting | bytes 4194304 | tf_op jit(solution)/shard_map/reshape;squeeze | solution.py:275
  13.2 0.7 reshape.7.bonds_ref
  14.5 30.3 %sweep.1 = (bf16[14,4,512,512]{3,2,1,0:T(8,128)(2,1)S(1)}, f32[8,128]{1,0:T(8,128)}) custom-call(s32[2]{0:T(128)} %pad_add_fusion.places, bf16[28,28]{1,0:T(8,128)(2,1)} %reshape.7.bonds_ref, bf16[14,256,512]{2,1,0:T(8,128)(2,1)} %bitcast.23, bf16[4,2,256,512]{3,2,1,0:T(8,128)(2,1)} %bitcast.18.refs_0_, bf16[4,2,256,512]{3,2,1,0:T(8,128)(2,1)} %collective-permute-done.refs_1_), custom_call_target="tpu_custom_call" | custom-call | flops 22548578304 | bytes 29360128 | tf_op jit(solution)/shard_map/sweep/pallas_call | solution.py:120
  44.8 12.5 %collective-permute-done.1.refs_0_ = bf16[8,256,512]{2,1,0:T(8,128)(2,1)} collective-permute-done((bf16[8,256,512]{2,1,0:T(8,128)(2,1)}, bf16[8,256,512]{2,1,0:T(8,128)(2,1)}, u32[]{:S(2)}, u32[]{:S(2)}) %collective-permute-start.1) | collective-permute-done | bytes 2097184 | tf_op jit(solution)/shard_map/ppermute | solution.py:22
  57.9 0.8 collective-permute-start.2
  58.7 22.9 %env_shares.1 = (bf16[14,256,512]{2,1,0:T(8,128)(2,1)}, bf16[14,256,512]{2,1,0:T(8,128)(2,1)}, bf16[14,4,512,512]{3,2,1,0:T(8,128)(2,1)S(1)}) custom-call(s32[2]{0:T(128)} %pad_add_fusion.places, bf16[4,512,512]{2,1,0:T(8,128)(2,1)} %reshape_squeeze.3.here_ref, ...), custom_call_target="tpu_custom_call", output_to_operand_aliasing={{2}: (2, {})} | custom-call | flops 15032385536 | bytes 29360128 | tf_op jit(solution)/shard_map/env_shares/pallas_call | solution.py:166
  81.6 2.5 %slice.13 = bf16[5,256,512]{2,1,0:T(8,128)(2,1)} slice(bf16[14,256,512]{2,1,0:T(8,128)(2,1)} %bitcast.20), slice={[8:13], [0:256], [0:512]} | slice | bytes 2621440 | tf_op jit(solution)/shard_map/slice | solution.py:268
  84.1 3.9 %collective-permute-start.3 = (bf16[5,256,512]{2,1,0:T(8,128)(2,1)}, bf16[5,256,512]{2,1,0:T(8,128)(2,1)S(1)}, u32[]{:S(2)}, u32[]{:S(2)}) collective-permute-start(bf16[5,256,512]{2,1,0:T(8,128)(2,1)} %slice.13), channel_id=1, source_target_pairs={{2,0},{4,2},{6,4},{8,6},{10,8},{12,10},{14,12},{16,14},{18,16},{20... | collective-permute-start | bytes 3932168 | tf_op jit(solution)/shard_map/ppermute | solution.py:22
  88.1 14.6 %applied_part.3 = (f32[4,512,512]{2,1,0:T(8,128)}, f32[8,128]{1,0:T(8,128)}, bf16[14,4,512,512]{3,2,1,0:T(8,128)(2,1)S(1)}) custom-call(s32[2]{0:T(128)} %pad_add_fusion.places, bf16[14,4,512,512]{3,2,1,0:T(8,128)(2,1)S(1)} %get-tuple-element.15.through_ref, bf16[8,256,512]{2,1,0:T(8,128)(2,1)} %after.3.refs_0_, ...), custom_call_target="tpu_custom_call", output_to_operand_aliasing={{2}: (1, {})} | custom-call | flops 8589934592 | bytes 16777216 | tf_op jit(solution)/shard_map/applied_part/pallas_call | solution.py:229
  102.7 15.2 %collective-permute-done.3.refs_0_ = bf16[5,256,512]{2,1,0:T(8,128)(2,1)S(1)} collective-permute-done((bf16[5,256,512]{2,1,0:T(8,128)(2,1)}, bf16[5,256,512]{2,1,0:T(8,128)(2,1)S(1)}, u32[]{:S(2)}, u32[]{:S(2)}) %collective-permute-start.3) | collective-permute-done | bytes 1310752 | tf_op jit(solution)/shard_map/ppermute | solution.py:22
  118.6 1.0 collective-permute-start.4
  119.6 1.0 slice.14
  120.6 3.3 %collective-permute-start.5 = (bf16[1,256,512]{2,1,0:T(8,128)(2,1)S(1)}, bf16[1,256,512]{2,1,0:T(8,128)(2,1)S(1)}, u32[]{:S(2)}, u32[]{:S(2)}) collective-permute-start(bf16[1,256,512]{2,1,0:T(8,128)(2,1)S(1)} %slice.14), channel_id=1, source_target_pairs={{2,0},{4,2},{6,4},{8,6},{10,8},{12,10},{14,12},{16,14},{18,16},{20... | collective-permute-start | bytes 786440 | tf_op jit(solution)/shard_map/ppermute | solution.py:22
  123.9 1.1 copy-done.8
  125.0 11.7 %applied_part.4 = (f32[4,512,512]{2,1,0:T(8,128)}, f32[8,128]{1,0:T(8,128)}, bf16[14,4,512,512]{3,2,1,0:T(8,128)(2,1)S(1)}) custom-call(s32[2]{0:T(128)} %pad_add_fusion.places, bf16[14,4,512,512]{3,2,1,0:T(8,128)(2,1)S(1)} %get-tuple-element.17.through_ref, bf16[5,256,512]{2,1,0:T(8,128)(2,1)} %copy-done.2, ...), custom_call_target="tpu_custom_call", output_to_operand_aliasing={{2}: (1, {})} | custom-call | flops 5368709120 | bytes 10485760 | tf_op jit(solution)/shard_map/applied_part/pallas_call | solution.py:229
  136.8 9.7 %copy-done = bf16[14,4,512,512]{3,2,1,0:T(8,128)(2,1)} copy-done((bf16[14,4,512,512]{3,2,1,0:T(8,128)(2,1)}, bf16[14,4,512,512]{3,2,1,0:T(8,128)(2,1)S(1)}, u32[]{:S(2)}) %copy-start) | copy-done | bytes 29360152
  146.5 0.7 copy-done.4
  147.6 6.2 %fusion = bf16[1,256,14,512]{3,1,2,0:T(8,128)(2,1)} fusion(bf16[14,256,512]{2,1,0:T(8,128)(2,1)} %collective-permute-done.7, bf16[14,256,512]{2,1,0:T(8,128)(2,1)} %get-tuple-element.24), kind=kLoop, calls=%fused_computation.1 | loop fusion | flops 7340032 | bytes 11010048 | tf_op jit(solution)/shard_map/broadcast_in_dim | solution.py:296
  153.8 0.7 copy-done.9
  154.5 9.3 %copy-done.1 = bf16[14,4,512,512]{3,2,1,0:T(8,128)(2,1)S(1)} copy-done((bf16[14,4,512,512]{3,2,1,0:T(8,128)(2,1)S(1)}, bf16[14,4,512,512]{3,2,1,0:T(8,128)(2,1)}, u32[]{:S(2)}) %copy-start.1) | copy-done | bytes 29360152
  163.8 5.8 %applied_part.5 = (bf16[4,256,2,512]{3,2,1,0:T(2,128)(2,1)}, f32[8,128]{1,0:T(8,128)}) custom-call(s32[2]{0:T(128)} %pad_add_fusion.places, bf16[14,4,512,512]{3,2,1,0:T(8,128)(2,1)S(1)} %copy-done.1, bf16[1,256,512]{2,1,0:T(8,128)(2,1)} %copy-done.3, bf16[1,256,512]{2,1,0:T(8,128)(2,1)} %copy-done.9, f32[4,512,512]{2,1,0:T(8,128)} %get-tuple-element.22.refs_2_), custom_call_target="tpu_custom_call" | custom-call | flops 1073741824 | bytes 2097152 | tf_op jit(solution)/shard_map/applied_part/pallas_call | solution.py:229
  (31 shorter events, 3.2 us)
Async XLA Ops:
  0.6 10.2 %copy-start.7 = (bf16[1,4,256,2,512]{4,3,2,1,0:T(2,128)(2,1)S(1)}, bf16[1,4,256,2,512]{4,3,2,1,0:T(2,128)(2,1)}, u32[]{:S(2)}) copy-start(bf16[1,4,256,2,512]{4,3,2,1,0:T(2,128)(2,1)} %param.6) | copy-start | bytes 6291460
  4.1 10.4 %collective-permute-start = (bf16[4,2,256,512]{3,2,1,0:T(8,128)(2,1)}, bf16[4,2,256,512]{3,2,1,0:T(8,128)(2,1)}, u32[]{:S(2)}, u32[]{:S(2)}) collective-permute-start(bf16[4,2,256,512]{3,2,1,0:T(8,128)(2,1)} %bitcast.18.refs_0_), channel_id=1, source_target_pairs={{0,1},{1,0},{2,3},{3,2},{4,5},{5,4},{6,7},{7,6},{8,9},{9,8},{10,11... | collective-permute-start | bytes 6291464 | tf_op jit(solution)/shard_map/ppermute | solution.py:26
  4.7 8.3 %copy-start.10 = (bf16[14,2,2,14]{3,2,1,0:T(2,128)(2,1)S(1)}, bf16[14,2,2,14]{3,2,1,0:T(2,128)(2,1)}, u32[]{:S(2)}) copy-start(bf16[14,2,2,14]{3,2,1,0:T(2,128)(2,1)} %param.7) | copy-start | bytes 4708
  7.8 49.5 %collective-permute-start.1 = (bf16[8,256,512]{2,1,0:T(8,128)(2,1)}, bf16[8,256,512]{2,1,0:T(8,128)(2,1)}, u32[]{:S(2)}, u32[]{:S(2)}) collective-permute-start(bf16[8,256,512]{2,1,0:T(8,128)(2,1)} %slice.12), channel_id=1, source_target_pairs={{2,0},{4,2},{6,4},{8,6},{10,8},{12,10},{14,12},{16,14},{18,16},{20... | collective-permute-start | bytes 6291464 | tf_op jit(solution)/shard_map/ppermute | solution.py:22
  57.3 0.7 copy-start.6
  57.9 30.1 %collective-permute-start.2 = (bf16[8,256,512]{2,1,0:T(8,128)(2,1)}, bf16[8,256,512]{2,1,0:T(8,128)(2,1)}, u32[]{:S(2)}, u32[]{:S(2)}) collective-permute-start(bf16[8,256,512]{2,1,0:T(8,128)(2,1)} %after.3.refs_0_), channel_id=1, source_target_pairs={{0,1},{1,0},{2,3},{3,2},{4,5},{5,4},{6,7},{7,6},{8,9},{9,8},{10,11... | collective-permute-start | bytes 6291464 | tf_op jit(solution)/shard_map/ppermute | solution.py:26
  81.6 66.0 %collective-permute-start.7 = (bf16[14,256,512]{2,1,0:T(8,128)(2,1)}, bf16[14,256,512]{2,1,0:T(8,128)(2,1)}, u32[]{:S(2)}, u32[]{:S(2)}) collective-permute-start(bf16[14,256,512]{2,1,0:T(8,128)(2,1)} %get-tuple-element.25), channel_id=1, source_target_pairs={{0,1},{1,0},{2,3},{3,2},{4,5},{5,4},{6,7},{7,6},{8,9},{9,8},{10,11... | collective-permute-start | bytes 11010056 | tf_op jit(solution)/shard_map/ppermute | solution.py:26
  84.1 33.8 %collective-permute-start.3 = (bf16[5,256,512]{2,1,0:T(8,128)(2,1)}, bf16[5,256,512]{2,1,0:T(8,128)(2,1)S(1)}, u32[]{:S(2)}, u32[]{:S(2)}) collective-permute-start(bf16[5,256,512]{2,1,0:T(8,128)(2,1)} %slice.13), channel_id=1, source_target_pairs={{2,0},{4,2},{6,4},{8,6},{10,8},{12,10},{14,12},{16,14},{18,16},{20... | collective-permute-start | bytes 3932168 | tf_op jit(solution)/shard_map/ppermute | solution.py:22
  117.9 0.7 copy-start.5
  118.6 6.4 %copy-start.2 = (bf16[5,256,512]{2,1,0:T(8,128)(2,1)}, bf16[5,256,512]{2,1,0:T(8,128)(2,1)S(1)}, u32[]{:S(2)}) copy-start(bf16[5,256,512]{2,1,0:T(8,128)(2,1)S(1)} %after.4.refs_0_) | copy-start | bytes 3932164
  118.6 5.3 %collective-permute-start.4 = (bf16[5,256,512]{2,1,0:T(8,128)(2,1)S(1)}, bf16[5,256,512]{2,1,0:T(8,128)(2,1)S(1)}, u32[]{:S(2)}, u32[]{:S(2)}) collective-permute-start(bf16[5,256,512]{2,1,0:T(8,128)(2,1)S(1)} %after.4.refs_0_), channel_id=1, source_target_pairs={{0,1},{1,0},{2,3},{3,2},{4,5},{5,4},{6,7},{7,6},{8,9},{9,8},{10,11... | collective-permute-start | bytes 3932168 | tf_op jit(solution)/shard_map/ppermute | solution.py:26
  120.6 25.9 %collective-permute-start.5 = (bf16[1,256,512]{2,1,0:T(8,128)(2,1)S(1)}, bf16[1,256,512]{2,1,0:T(8,128)(2,1)S(1)}, u32[]{:S(2)}, u32[]{:S(2)}) collective-permute-start(bf16[1,256,512]{2,1,0:T(8,128)(2,1)S(1)} %slice.14), channel_id=1, source_target_pairs={{2,0},{4,2},{6,4},{8,6},{10,8},{12,10},{14,12},{16,14},{18,16},{20... | collective-permute-start | bytes 786440 | tf_op jit(solution)/shard_map/ppermute | solution.py:22
  123.9 1.1 copy-start.8
  136.8 9.7 %copy-start = (bf16[14,4,512,512]{3,2,1,0:T(8,128)(2,1)}, bf16[14,4,512,512]{3,2,1,0:T(8,128)(2,1)S(1)}, u32[]{:S(2)}) copy-start(bf16[14,4,512,512]{3,2,1,0:T(8,128)(2,1)S(1)} %get-tuple-element.20.through_ref) | copy-start | bytes 88080384
  146.5 0.7 copy-start.4
  147.2 6.6 %copy-start.3 = (bf16[1,256,512]{2,1,0:T(8,128)(2,1)}, bf16[1,256,512]{2,1,0:T(8,128)(2,1)S(1)}, u32[]{:S(2)}) copy-start(bf16[1,256,512]{2,1,0:T(8,128)(2,1)S(1)} %after.5.refs_0_) | copy-start | bytes 786436
  147.2 6.6 %collective-permute-start.6 = (bf16[1,256,512]{2,1,0:T(8,128)(2,1)S(1)}, bf16[1,256,512]{2,1,0:T(8,128)(2,1)S(1)}, u32[]{:S(2)}, u32[]{:S(2)}) collective-permute-start(bf16[1,256,512]{2,1,0:T(8,128)(2,1)S(1)} %after.5.refs_0_), channel_id=1, source_target_pairs={{0,1},{1,0},{2,3},{3,2},{4,5},{5,4},{6,7},{7,6},{8,9},{9,8},{10,11... | collective-permute-start | bytes 786440 | tf_op jit(solution)/shard_map/ppermute | solution.py:26
  153.8 0.7 copy-start.9
  154.5 9.4 %copy-start.1 = (bf16[14,4,512,512]{3,2,1,0:T(8,128)(2,1)S(1)}, bf16[14,4,512,512]{3,2,1,0:T(8,128)(2,1)}, u32[]{:S(2)}) copy-start(bf16[14,4,512,512]{3,2,1,0:T(8,128)(2,1)} %copy-done) | copy-start | bytes 88080384

commit v4 on v3

v4 whole, which is shorter than its diff:
```python
import functools
import math

import jax
import jax.numpy as jnp
from jax import lax
from jax.experimental import pallas as pl
from jax.experimental.pallas import tpu as pltpu
from jax.sharding import PartitionSpec as P

GROUP = 8
MIB = 1 << 20
SWEEP_MIB = 54
APPLIED_MIB = 40
ANY = pl.BlockSpec(memory_space=pl.ANY)


def passed_along(array, axis, by):
    size = lax.axis_size(axis)
    pairs = [(i, i + by) for i in range(size) if 0 <= i + by < size]
    return lax.ppermute(array, axis, pairs)


def swapped(array, axis):
    return lax.ppermute(array, axis, [(0, 1), (1, 0)])


def product(left, right, contract):
    return lax.dot_general(left, right, (contract, ((), ())), preferred_element_type=jnp.float32)


def after(array, *others):
    return pl.pallas_call(
        lambda *refs: None,
        in_specs=[ANY] * (1 + len(others)),
        out_specs=ANY,
        out_shape=jax.ShapeDtypeStruct(array.shape, array.dtype),
        input_output_aliases={0: 0},
        compiler_params=pltpu.CompilerParams(vmem_limit_bytes=MIB),
        name="after",
    )(array, *others)


def block_diagonal(bonds, mw, phys):
    size = mw * phys
    full = size * GROUP
    row = lax.broadcasted_iota(jnp.int32, (full, size), 0)
    which = lax.broadcasted_iota(jnp.int32, (full, size), 1)
    pick_row = (row // (GROUP * phys) * phys + row % phys == which).astype(jnp.bfloat16)
    column = lax.broadcasted_iota(jnp.int32, (size, full), 1)
    which = lax.broadcasted_iota(jnp.int32, (size, full), 0)
    pick_column = (column // GROUP == which).astype(jnp.bfloat16)
    spread = product(pick_row, bonds, ((1,), (0,))).astype(jnp.bfloat16)
    spread = product(spread, pick_column, ((1,), (0,)))
    row = lax.broadcasted_iota(jnp.int32, (full, full), 0)
    column = lax.broadcasted_iota(jnp.int32, (full, full), 1)
    same = row % (GROUP * phys) // phys == column % GROUP
    return jnp.where(same, spread, 0.0).astype(jnp.bfloat16)


TOKEN = jax.ShapeDtypeStruct((8, 128), jnp.float32)
WHOLE = pl.BlockSpec(memory_space=pltpu.VMEM)
SCALARS = pl.BlockSpec(memory_space=pltpu.SMEM)


def own_first(swap, first, second, axis):
    return jnp.concatenate(
        [jnp.where(swap, second, first), jnp.where(swap, first, second)], axis=axis
    )


def sweep_kernel(parts, pieces, scaling, places, bonds_ref, env_hbm, here_hbm, *refs):
    waves_hbm, refs = refs[:parts], refs[parts:]
    throughs_hbm, refs = refs[:pieces], refs[pieces:]
    token_ref, refs = refs[0], refs[1:]
    outs, refs = refs[:parts], refs[parts:]
    env_ref, here_ref, wave_ref, lhs, low, turned, stage, through_ref = refs[:8]
    env_sems, wave_sems, here_sem, out_sems, through_sems = refs[8:]
    mw, rows_all, chi_in = env_ref.shape
    num_states, phys, _, chi = wave_ref.shape
    width = chi_in // parts
    part = mw * GROUP
    groups = lhs.shape[0] // part
    rows = groups * GROUP
    blocks = rows_all // rows

    def env_copy(i):
        here = pl.ds(pl.multiple_of(i * rows, rows), rows)
        return pltpu.make_async_copy(env_hbm.at[:, here], env_ref.at[:, here], env_sems.at[i])

    def wave_copies(k):
        return [
            pltpu.make_async_copy(
                wave.at[k],
                wave_ref.at[k, :, pl.ds(index * width, width)],
                wave_sems.at[k, index],
            )
            for index, wave in enumerate(waves_hbm)
        ]

    def through_copies(i):
        here = pl.ds(pl.multiple_of(i * rows * phys, rows * phys), rows * phys)
        found, first = [], 0
        for index, out in enumerate(throughs_hbm):
            count = out.shape[0]
            found.append(
                pltpu.make_async_copy(
                    through_ref.at[pl.ds(first, count), :, here],
                    out.at[:, :, here],
                    through_sems.at[i, index],
                )
            )
            first += count
        return found

    here_copy = pltpu.make_async_copy(here_hbm, here_ref, here_sem)
    for n in range(max(blocks, num_states)):
        if n < blocks:
            env_copy(n).start()
        if n < num_states:
            for copy in wave_copies(n):
                copy.start()
    here_copy.start()

    table = block_diagonal(bonds_ref[...], mw, phys)
    depth = table.shape[0]
    padded = low.shape[1]
    table = jnp.concatenate([table, jnp.zeros((depth, padded - depth), table.dtype)], axis=1)
    low[:, depth:, :] = jnp.zeros((groups, padded - depth, chi), low.dtype)
    swap = places[0] != 0

    def block(i, _):
        env_copy(i).wait()
        env = env_ref[:, pl.ds(pl.multiple_of(i * rows, rows), rows), :].astype(jnp.float32)
        if parts == 2:
            env = own_first(swap, env[..., :width], env[..., width:], 2)
        env = env.reshape(mw, groups, GROUP, chi_in)
        for g in range(groups):
            lhs[g * part : (g + 1) * part, :] = env[:, g].reshape(part, chi_in).astype(jnp.bfloat16)

        def state(k, _):
            @pl.when(i == 0)
            def _():
                for copy in wave_copies(k):
                    copy.wait()

            for t in range(phys):
                inner = product(lhs[...], wave_ref[k, t], ((1,), (0,))).astype(jnp.bfloat16)
                low[:, t * part : (t + 1) * part, :] = inner.reshape(groups, part, chi)
            for g in range(groups):
                through = product(table, low[g], ((1,), (0,))).astype(jnp.bfloat16)
                size = GROUP * phys
                at = pl.multiple_of(i * rows * phys + g * size, size)
                through_ref[:, k, pl.ds(at, size), :] = through.reshape(mw, size, chi)
            return 0

        lax.fori_loop(0, num_states, state, 0)
        for copy in through_copies(i):
            copy.start()
        return 0

    lax.fori_loop(0, blocks, block, 0)

    here_copy.wait()
    depth = rows_all * phys
    for k in range(num_states):
        turned[:, k * depth : (k + 1) * depth] = here_ref[k].T

    def out_copies(v, slot):
        return [
            pltpu.make_async_copy(
                stage.at[slot, pl.ds(index * (chi // parts), chi // parts)],
                out.at[v],
                out_sems.at[slot, index],
            )
            for index, out in enumerate(outs)
        ]

    def bond(v, _):
        slot = v % 2
        right = through_ref[v].reshape(num_states * depth, chi)
        share = (product(turned[...], right, ((1,), (0,))) * scaling).astype(jnp.bfloat16)
        if parts == 2:
            share = own_first(swap, share[: chi // 2], share[chi // 2 :], 0)

        @pl.when(v >= 2)
        def _():
            for copy in out_copies(v - 2, slot):
                copy.wait()

        stage[slot] = share
        for copy in out_copies(v, slot):
            copy.start()
        return 0

    lax.fori_loop(0, mw, bond, 0)
    for v in range(max(mw - 2, 0), mw):
        for copy in out_copies(v, v % 2):
            copy.wait()
    for i in range(blocks):
        for copy in through_copies(i):
            copy.wait()
    token_ref[...] = jnp.zeros_like(token_ref)


def sweep(bonds, env, here, waves, places, counts, scaling):
    mw, rows_all, chi_in = env.shape
    num_states, phys, _, chi = waves[0].shape
    rows = min(64, rows_all)
    parts = len(waves)
    padded = -(-mw * phys * GROUP // 128) * 128
    bf16 = jnp.bfloat16
    share = jax.ShapeDtypeStruct((mw, chi // parts, chi), bf16)
    out = pl.pallas_call(
        functools.partial(sweep_kernel, parts, len(counts), scaling),
        in_specs=[SCALARS, WHOLE] + [ANY] * (2 + parts),
        out_specs=[ANY] * len(counts) + [WHOLE] + [ANY] * parts,
        scratch_shapes=[
            pltpu.VMEM(env.shape, bf16),
            pltpu.VMEM(here.shape, bf16),
            pltpu.VMEM((num_states, phys, chi_in, chi), bf16),
            pltpu.VMEM((mw * rows, chi_in), bf16),
            pltpu.VMEM((rows // GROUP, padded, chi), bf16),
            pltpu.VMEM((chi, num_states * rows_all * phys), bf16),
            pltpu.VMEM((2, chi, chi), bf16),
            pltpu.VMEM((mw, num_states, rows_all * phys, chi), bf16),
            pltpu.SemaphoreType.DMA((rows_all // rows,)),
            pltpu.SemaphoreType.DMA((num_states, parts)),
            pltpu.SemaphoreType.DMA,
            pltpu.SemaphoreType.DMA((2, parts)),
            pltpu.SemaphoreType.DMA((rows_all // rows, len(counts))),
        ],
        out_shape=[
            jax.ShapeDtypeStruct((count, num_states, rows_all * phys, chi), bf16)
            for count in counts
        ]
        + [TOKEN]
        + [share] * parts,
        compiler_params=pltpu.CompilerParams(vmem_limit_bytes=SWEEP_MIB * MIB),
        cost_estimate=pl.CostEstimate(
            flops=5 * mw * rows_all * chi_in * num_states * phys * chi,
            bytes_accessed=2 * mw * num_states * rows_all * phys * chi,
            transcendentals=0,
        ),
        name="sweep",
    )(places, bonds, env, here, *waves)
    pieces = len(counts)
    return out[:pieces], out[pieces], out[pieces + 1 :]


def applied_kernel(parts, begun, places, through_hbm, *refs):
    rights_hbm, refs = refs[:parts], refs[parts:]
    if begun:
        held_hbm, refs = refs[0], refs[1:]
    out_hbm, token_ref, through_ref, rights, turned, results = refs[:6]
    through_sems, right_sems, out_sems = refs[6:9]
    if begun:
        held, held_sems = refs[9:]
    last = out_hbm.dtype == jnp.bfloat16
    count, num_states, rows, chi = through_hbm.shape
    width = rights_hbm[0].shape[1]

    def right_copies(v):
        return [
            pltpu.make_async_copy(
                right.at[v], rights.at[v, pl.ds(index * width, width)], right_sems.at[v, index]
            )
            for index, right in enumerate(rights_hbm)
        ]

    def through_copies(k):
        return [
            pltpu.make_async_copy(through_hbm.at[v, k], through_ref.at[v, k], through_sems.at[v, k])
            for v in range(count)
        ]

    def held_copy(k):
        return pltpu.make_async_copy(held_hbm.at[k], held.at[k], held_sems.at[k])

    def out_copy(k, slot):
        return pltpu.make_async_copy(results.at[slot], out_hbm.at[k], out_sems.at[slot])

    for v in range(count):
        for copy in right_copies(v):
            copy.start()
    for k in range(num_states):
        for copy in through_copies(k):
            copy.start()
        if begun:
            held_copy(k).start()
    for v in range(count):
        for copy in right_copies(v):
            copy.wait()
        turned[v * chi : (v + 1) * chi, :] = rights[v].T

    def state(k, _):
        for copy in through_copies(k):
            copy.wait()
        left = jnp.concatenate([through_ref[v, k] for v in range(count)], axis=1)
        total = product(left, turned[...], ((1,), (0,)))
        if begun:
            held_copy(k).wait()
            total = total + held[k]
        if last:
            columns = total.shape[1]
            phys = results.shape[2]
            total = total.astype(jnp.bfloat16)
            if parts == 2:
                swap = places[0] != 0
                total = own_first(swap, total[:, : columns // 2], total[:, columns // 2 :], 1)
            total = total.reshape(rows // phys, phys, columns)
        slot = k % 2

        @pl.when(k >= 2)
        def _():
            out_copy(k - 2, slot).wait()

        results[slot] = total
        out_copy(k, slot).start()
        return 0

    lax.fori_loop(0, num_states, state, 0)
    for k in range(max(num_states - 2, 0), num_states):
        out_copy(k, k % 2).wait()
    token_ref[...] = jnp.zeros_like(token_ref)


def applied_part(through, rights, held, places, phys, last):
    count, num_states, rows, chi = through.shape
    width = rights[0].shape[1]
    parts = len(rights)
    begun = held is not None
    columns = width * parts
    if last:
        out_shape = jax.ShapeDtypeStruct((num_states, rows // phys, phys, columns), jnp.bfloat16)
    else:
        out_shape = jax.ShapeDtypeStruct((num_states, rows, columns), jnp.float32)
    operands = [through, *rights] + ([held] if begun else [])
    return pl.pallas_call(
        functools.partial(applied_kernel, parts, begun),
        in_specs=[SCALARS] + [ANY] * len(operands),
        out_specs=[ANY, WHOLE],
        out_shape=[out_shape, TOKEN],
        scratch_shapes=[
            pltpu.VMEM(through.shape, jnp.bfloat16),
            pltpu.VMEM((count, columns, chi), jnp.bfloat16),
            pltpu.VMEM((count * chi, columns), jnp.bfloat16),
            pltpu.VMEM((2,) + out_shape.shape[1:], out_shape.dtype),
            pltpu.SemaphoreType.DMA((count, num_states)),
            pltpu.SemaphoreType.DMA((count, parts)),
            pltpu.SemaphoreType.DMA((2,)),
        ]
        + (
            [
                pltpu.VMEM((num_states, rows, columns), jnp.float32),
                pltpu.SemaphoreType.DMA((num_states,)),
            ]
            if begun
            else []
        ),
        compiler_params=pltpu.CompilerParams(vmem_limit_bytes=APPLIED_MIB * MIB),
        cost_estimate=pl.CostEstimate(
            flops=2 * num_states * rows * columns * count * chi,
            bytes_accessed=2 * count * num_states * rows * chi,
            transcendentals=0,
        ),
        name="applied_part",
    )(places, *operands)


def cuts(size):
    middle = max((size - 1) * 5 // 13, 0)
    sizes = [count for count in (size - 1 - middle, middle, 1) if count > 0]
    found, at = [], 0
    for count in sizes:
        found.append((at, count))
        at += count
    return found


def on_device(left_env, right_env, states, mpo):
    num_states, rows, phys, chi = states.shape[1:]
    mw = mpo.shape[0]
    bonds = lax.axis_size("bond")
    paired = bonds == 2
    me = lax.axis_index("bond").astype(jnp.int32)
    places = jnp.stack([me, 1 - me]) if paired else jnp.stack([me, me]) * 0
    scaling = 1.0 / math.sqrt(num_states * chi)
    left = left_env[0].transpose(1, 0, 2)
    right = right_env[0].transpose(1, 0, 2)

    starts = cuts(mw)
    pieces = [passed_along(right[at : at + count], "seg", -1) for at, count in starts]

    wave_split = states[0].transpose(0, 2, 1, 3)
    if paired:
        waves = [wave_split, swapped(wave_split, "bond")]
    else:
        waves = [lax.all_gather(wave_split, "bond", axis=2, tiled=True)]
    here = states[0].reshape(num_states, rows * phys, chi)
    bond_table = mpo.transpose(3, 1, 2, 0).reshape(mw * phys, phys * mw)
    counts = [count for _, count in starts]
    throughs, token, shares = sweep(bond_table, left, here, waves, places, counts, scaling)
    if paired:
        arrived = swapped(shares[1], "bond")
        new_env = shares[0].astype(jnp.float32) + arrived.astype(jnp.float32)
        new_env = new_env.astype(jnp.bfloat16)
    else:
        new_env = lax.psum_scatter(shares[0], "bond", scatter_dimension=1, tiled=True)

    held = None
    for index, (through, piece) in enumerate(zip(throughs, pieces)):
        if paired:
            piece = after(piece, token)
            rights = [piece, swapped(piece, "bond")]
        else:
            rights = [lax.all_gather(piece, "bond", axis=1, tiled=True)]
        last = index == len(pieces) - 1
        held, token = applied_part(through, rights, held, places, phys, last)
    return (held[None], new_env.transpose(1, 0, 2)[None])


def solution(mesh):
    in_specs = (
        P("seg", "bond", None, None),
        P("seg", "bond", None, None),
        P("seg", None, "bond", None, None),
        P(),
    )
    out_specs = (P("seg", None, "bond", None, None), P("seg", "bond", None, None))
    return jax.shard_map(
        on_device, mesh=mesh, in_specs=in_specs, out_specs=out_specs, check_vma=False
    )
```

time: 173 us -> 126 us (0.73)
  local copies, waits for them, and re-layouts: 35.8 us -> 12.9 us
  waiting for transfers between devices: 27.8 us -> 16.5 us
  Pallas kernels: 85.3 us -> 78.6 us
  other arithmetic: 6.71 us -> 3.67 us
  starting transfers between devices: 13.3 us -> 10.9 us
    unnamed x23 -> x13, local copies, waits for them, and re-layouts: 26.3 us -> 4.11 us
    ppermute x3, waiting for transfers between devices: 27.7 us -> 15.8 us  [passed_along(): return lax.ppermute(array, axis, pairs)]
    pallas_call x5 -> x4, Pallas kernels: 85.3 us -> 78.6 us  [the longest x1 49 us: sweep(): pl.pallas_call(functools.partial(sweep_kernel, parts, len(counts), scalin...]
    broadcast_in_dim x1, other arithmetic: 6.16 us -> 3.08 us  [on_device(): return (held[None], new_env.transpose(1, 0, 2)[None])]
    slice x3, local copies, waits for them, and re-layouts: 6.54 us -> 3.91 us  [on_device(): right[at:at + count]]
    ppermute x3, starting transfers between devices: 10.3 us -> 8.27 us  [passed_along(): return lax.ppermute(array, axis, pairs)]
    another operation x1, local copies, waits for them, and re-layouts: 2.21 us -> 4.1 us  [on_device(): here = states[0].reshape(num_states, rows * phys, chi)]
  transfers between devices with their start and end apart: 8 -> 8, of which waited for: 2 -> 2; matrix products, arithmetic and copies ran while one was open for 10% -> 10% of each run, Pallas kernels for 47% -> 60%
where the time goes in v4:
time: 126 us; the launch traced here: 123 us
  Pallas kernels  78.6 us (62%)
  waiting for transfers between devices  16.5 us (13%)
  local copies, waits for them, and re-layouts  12.9 us (10%)
  starting transfers between devices  10.9 us (9%)
  other arithmetic  3.67 us (3%)
    pallas_call x1, Pallas kernels, sweep(): pl.pallas_call(functools.partial(sweep_kernel, parts, len(counts), scalin...  49 us
    pallas_call x3, Pallas kernels, applied_part(): pl.pallas_call(functools.partial(applied_kernel, parts, begun), in_specs=...  29.6 us
    ppermute x3, waiting for transfers between devices, passed_along(): return lax.ppermute(array, axis, pairs)  15.8 us
    ppermute x3, starting transfers between devices, passed_along(): return lax.ppermute(array, axis, pairs)  8.27 us
    unnamed x13, local copies, waits for them, and re-layouts  4.11 us
    another operation x1, local copies, waits for them, and re-layouts, on_device(): here = states[0].reshape(num_states, rows * phys, chi)  4.1 us
    slice x3, local copies, waits for them, and re-layouts, on_device(): right[at:at + count]  3.91 us
    broadcast_in_dim x1, other arithmetic, on_device(): return (held[None], new_env.transpose(1, 0, 2)[None])  3.08 us
  transfers between devices with their start and end apart: 8, of which 2 were waited for; matrix products, arithmetic and copies ran while one was open for 10% of the time, Pallas kernels for 60%

profile of v4, /device:TPU:13, one launch (start us, length us, event | category | flops | bytes accessed | tf_op | source)
XLA Modules:
  0.0 123.4 jit_solution(126275305873172419)
XLA Ops:
  0.6 3.4 %copy.12 = bf16[1,4,256,2,512]{4,2,3,1,0:T(8,128)(2,1)} copy(bf16[1,4,256,2,512]{4,3,2,1,0:T(2,128)(2,1)} %param.6) | data formatting | bytes 4194304 | tf_op args[2]
  4.1 0.7 collective-permute-start
  4.7 1.5 %slice.14 = bf16[8,256,512]{2,1,0:T(8,128)(2,1)} slice(bf16[14,256,512]{2,1,0:T(8,128)(2,1)S(1)} %bitcast.21), slice={[0:8], [0:256], [0:512]} | slice | bytes 4194304 | tf_op jit(solution)/shard_map/slice | solution.py:393
  6.3 3.0 %collective-permute-start.3 = (bf16[8,256,512]{2,1,0:T(8,128)(2,1)}, bf16[8,256,512]{2,1,0:T(8,128)(2,1)S(1)}, u32[]{:S(2)}, u32[]{:S(2)}) collective-permute-start(bf16[8,256,512]{2,1,0:T(8,128)(2,1)} %slice.14), channel_id=1, source_target_pairs={{2,0},{4,2},{6,4},{8,6},{10,8},{12,10},{14,12},{16,14},{18,16},{20... | collective-permute-start | bytes 6291464 | tf_op jit(solution)/shard_map/ppermute | solution.py:21
  9.3 4.1 %reshape_squeeze.3.here_hbm = bf16[4,512,512]{2,1,0:T(8,128)(2,1)} reshape(bf16[1,4,256,2,512]{4,3,2,1,0:T(2,128)(2,1)} %param.6) | data formatting | bytes 4194304 | tf_op jit(solution)/shard_map/reshape;squeeze | solution.py:400
  13.4 0.1 copy.9
  13.6 0.7 reshape.7.bonds_ref
  14.3 0.6 pad_add_fusion.places
  14.9 49.0 %sweep.1 = (bf16[8,4,512,512]{3,2,1,0:T(8,128)(2,1)}, bf16[5,4,512,512]{3,2,1,0:T(8,128)(2,1)}, bf16[1,4,512,512]{3,2,1,0:T(8,128)(2,1)}, f32[8,128]{1,0:T(8,128...) custom-call(s32[2]{0:T(128)} %pad_add_fusion.places, bf16[28,28]{1,0:T(8,128)(2,1)} %reshape.7.bonds_ref, ...), custom_call_target="tpu_custom_call" | custom-call | flops 37580963840 | bytes 29360128 | tf_op jit(solution)/shard_map/sweep/pallas_call | solution.py:214
  63.9 0.7 copy-done.1
  64.6 0.3 collective-permute-start.4
  64.9 0.2 collective-permute-start.7
  65.1 1.4 %slice.13 = bf16[5,256,512]{2,1,0:T(8,128)(2,1)S(1)} slice(bf16[14,256,512]{2,1,0:T(8,128)(2,1)} %bitcast.19), slice={[8:13], [0:256], [0:512]} | slice | bytes 2621440 | tf_op jit(solution)/shard_map/slice | solution.py:393
  66.5 2.2 %collective-permute-start.2 = (bf16[5,256,512]{2,1,0:T(8,128)(2,1)S(1)}, bf16[5,256,512]{2,1,0:T(8,128)(2,1)S(1)}, u32[]{:S(2)}, u32[]{:S(2)}) collective-permute-start(bf16[5,256,512]{2,1,0:T(8,128)(2,1)S(1)} %slice.13), channel_id=1, source_target_pairs={{2,0},{4,2},{6,4},{8,6},{10,8},{12,10},{14,12},{16,14},{18,16},{20... | collective-permute-start | bytes 3932168 | tf_op jit(solution)/shard_map/ppermute | solution.py:21
  68.7 0.7 collective-permute-done.4.refs_1_
  69.4 13.4 %applied_part.3 = (f32[4,512,512]{2,1,0:T(8,128)S(1)}, f32[8,128]{1,0:T(8,128)S(1)}) custom-call(s32[2]{0:T(128)S(1)} %copy-done.2, bf16[8,4,512,512]{3,2,1,0:T(8,128)(2,1)} %get-tuple-element.15.through_hbm, bf16[8,256,512]{2,1,0:T(8,128)(2,1)S(1)} %after.3.refs_0_, bf16[8,256,512]{2,1,0:T(8,128)(2,1)S(1)} %collective-permute-done.4.refs_1_), custom_call_target="tpu_custom_call" | custom-call | flops 8589934592 | bytes 16777216 | tf_op jit(solution)/shard_map/applied_part/pallas_call | solution.py:339
  82.7 15.8 %collective-permute-done.2.refs_0_ = bf16[5,256,512]{2,1,0:T(8,128)(2,1)S(1)} collective-permute-done((bf16[5,256,512]{2,1,0:T(8,128)(2,1)S(1)}, bf16[5,256,512]{2,1,0:T(8,128)(2,1)S(1)}, u32[]{:S(2)}, u32[]{:S(2)}) %collective-permute-start.2) | collective-permute-done | bytes 1310752 | tf_op jit(solution)/shard_map/ppermute | solution.py:21
  98.5 1.1 collective-permute-start.5
  99.6 1.0 slice.12
  100.6 3.1 %collective-permute-start.1 = (bf16[1,256,512]{2,1,0:T(8,128)(2,1)S(1)}, bf16[1,256,512]{2,1,0:T(8,128)(2,1)S(1)}, u32[]{:S(2)}, u32[]{:S(2)}) collective-permute-start(bf16[1,256,512]{2,1,0:T(8,128)(2,1)S(1)} %slice.12), channel_id=1, source_target_pairs={{2,0},{4,2},{6,4},{8,6},{10,8},{12,10},{14,12},{16,14},{18,16},{20... | collective-permute-start | bytes 786440 | tf_op jit(solution)/shard_map/ppermute | solution.py:21
  103.7 11.1 %applied_part.4 = (f32[4,512,512]{2,1,0:T(8,128)S(1)}, f32[8,128]{1,0:T(8,128)S(1)}) custom-call(s32[2]{0:T(128)S(1)} %copy-done.2, bf16[5,4,512,512]{3,2,1,0:T(8,128)(2,1)} %get-tuple-element.14.through_hbm, bf16[5,256,512]{2,1,0:T(8,128)(2,1)S(1)} %after.4.refs_0_, bf16[5,256,512]{2,1,0:T(8,128)(2,1)S(1)} %collective-permute-done.5.refs_1_, ...), custom_call_target="tpu_custom_call" | custom-call | flops 5368709120 | bytes 10485760 | tf_op jit(solution)/shard_map/applied_part/pallas_call | solution.py:339
  114.8 0.4 collective-permute-start.6
  115.2 3.1 %fusion = bf16[1,256,14,512]{3,1,2,0:T(8,128)(2,1)} fusion(bf16[14,256,512]{2,1,0:T(8,128)(2,1)S(1)} %collective-permute-done.7, bf16[14,256,512]{2,1,0:T(8,128)(2,1)S(1)} %copy-done.4), kind=kLoop, calls=%fused_computation.1 | loop fusion | flops 7340032 | bytes 11010048 | tf_op jit(solution)/shard_map/broadcast_in_dim | solution.py:420
  118.3 5.1 %applied_part.5 = (bf16[4,256,2,512]{3,2,1,0:T(2,128)(2,1)}, f32[8,128]{1,0:T(8,128)}) custom-call(s32[2]{0:T(128)S(1)} %copy-done.2, bf16[1,4,512,512]{3,2,1,0:T(8,128)(2,1)S(1)} %copy-done, bf16[1,256,512]{2,1,0:T(8,128)(2,1)S(1)} %after.5.refs_0_, bf16[1,256,512]{2,1,0:T(8,128)(2,1)S(1)} %collective-permute-done.6.refs_1_, ...), custom_call_target="tpu_custom_call" | custom-call | flops 1073741824 | bytes 2097152 | tf_op jit(solution)/shard_map/applied_part/pallas_call | solution.py:339
  (20 shorter events, 0.0 us)
Async XLA Ops:
  0.6 4.1 %copy-start.3 = (bf16[1,256,14,512]{3,1,2,0:T(8,128)(2,1)S(1)}, bf16[1,256,14,512]{3,1,2,0:T(8,128)(2,1)}, u32[]{:S(2)}) copy-start(bf16[1,256,14,512]{3,1,2,0:T(8,128)(2,1)} %param.5) | copy-start | bytes 11010052
  4.1 10.8 %collective-permute-start = (bf16[4,2,256,512]{3,2,1,0:T(8,128)(2,1)}, bf16[4,2,256,512]{3,2,1,0:T(8,128)(2,1)}, u32[]{:S(2)}, u32[]{:S(2)}) collective-permute-start(bf16[4,2,256,512]{3,2,1,0:T(8,128)(2,1)} %bitcast.18.refs_0_), channel_id=1, source_target_pairs={{0,1},{1,0},{2,3},{3,2},{4,5},{5,4},{6,7},{7,6},{8,9},{9,8},{10,11... | collective-permute-start | bytes 6291464 | tf_op jit(solution)/shard_map/ppermute | solution.py:25
  4.7 8.7 %copy-start.5 = (bf16[14,2,2,14]{3,2,1,0:T(2,128)(2,1)S(1)}, bf16[14,2,2,14]{3,2,1,0:T(2,128)(2,1)}, u32[]{:S(2)}) copy-start(bf16[14,2,2,14]{3,2,1,0:T(2,128)(2,1)} %param.7) | copy-start | bytes 4708
  6.3 57.6 %collective-permute-start.3 = (bf16[8,256,512]{2,1,0:T(8,128)(2,1)}, bf16[8,256,512]{2,1,0:T(8,128)(2,1)S(1)}, u32[]{:S(2)}, u32[]{:S(2)}) collective-permute-start(bf16[8,256,512]{2,1,0:T(8,128)(2,1)} %slice.14), channel_id=1, source_target_pairs={{2,0},{4,2},{6,4},{8,6},{10,8},{12,10},{14,12},{16,14},{18,16},{20... | collective-permute-start | bytes 6291464 | tf_op jit(solution)/shard_map/ppermute | solution.py:21
  63.9 5.5 %copy-start.2 = (s32[2]{0:T(128)S(1)}, s32[2]{0:T(128)}, u32[]{:S(2)}) copy-start(s32[2]{0:T(128)} %pad_add_fusion.places) | copy-start | bytes 28
  63.9 0.7 copy-start.1
  64.6 4.7 %collective-permute-start.4 = (bf16[8,256,512]{2,1,0:T(8,128)(2,1)S(1)}, bf16[8,256,512]{2,1,0:T(8,128)(2,1)S(1)}, u32[]{:S(2)}, u32[]{:S(2)}) collective-permute-start(bf16[8,256,512]{2,1,0:T(8,128)(2,1)S(1)} %after.3.refs_0_), channel_id=1, source_target_pairs={{0,1},{1,0},{2,3},{3,2},{4,5},{5,4},{6,7},{7,6},{8,9},{9,8},{10,11... | collective-permute-start | bytes 6291464 | tf_op jit(solution)/shard_map/ppermute | solution.py:25
  64.9 50.3 %collective-permute-start.7 = (bf16[14,256,512]{2,1,0:T(8,128)(2,1)}, bf16[14,256,512]{2,1,0:T(8,128)(2,1)S(1)}, u32[]{:S(2)}, u32[]{:S(2)}) collective-permute-start(bf16[14,256,512]{2,1,0:T(8,128)(2,1)} %get-tuple-element.23), channel_id=1, source_target_pairs={{0,1},{1,0},{2,3},{3,2},{4,5},{5,4},{6,7},{7,6},{8,9},{9,8},{10,11... | collective-permute-start | bytes 11010056 | tf_op jit(solution)/shard_map/ppermute | solution.py:25
  66.5 32.0 %collective-permute-start.2 = (bf16[5,256,512]{2,1,0:T(8,128)(2,1)S(1)}, bf16[5,256,512]{2,1,0:T(8,128)(2,1)S(1)}, u32[]{:S(2)}, u32[]{:S(2)}) collective-permute-start(bf16[5,256,512]{2,1,0:T(8,128)(2,1)S(1)} %slice.13), channel_id=1, source_target_pairs={{2,0},{4,2},{6,4},{8,6},{10,8},{12,10},{14,12},{16,14},{18,16},{20... | collective-permute-start | bytes 3932168 | tf_op jit(solution)/shard_map/ppermute | solution.py:21
  98.5 5.1 %collective-permute-start.5 = (bf16[5,256,512]{2,1,0:T(8,128)(2,1)S(1)}, bf16[5,256,512]{2,1,0:T(8,128)(2,1)S(1)}, u32[]{:S(2)}, u32[]{:S(2)}) collective-permute-start(bf16[5,256,512]{2,1,0:T(8,128)(2,1)S(1)} %after.4.refs_0_), channel_id=1, source_target_pairs={{0,1},{1,0},{2,3},{3,2},{4,5},{5,4},{6,7},{7,6},{8,9},{9,8},{10,11... | collective-permute-start | bytes 3932168 | tf_op jit(solution)/shard_map/ppermute | solution.py:25
  100.6 14.2 %collective-permute-start.1 = (bf16[1,256,512]{2,1,0:T(8,128)(2,1)S(1)}, bf16[1,256,512]{2,1,0:T(8,128)(2,1)S(1)}, u32[]{:S(2)}, u32[]{:S(2)}) collective-permute-start(bf16[1,256,512]{2,1,0:T(8,128)(2,1)S(1)} %slice.12), channel_id=1, source_target_pairs={{2,0},{4,2},{6,4},{8,6},{10,8},{12,10},{14,12},{16,14},{18,16},{20... | collective-permute-start | bytes 786440 | tf_op jit(solution)/shard_map/ppermute | solution.py:21
  103.7 11.5 %copy-start.4 = (bf16[14,256,512]{2,1,0:T(8,128)(2,1)S(1)}, bf16[14,256,512]{2,1,0:T(8,128)(2,1)}, u32[]{:S(2)}) copy-start(bf16[14,256,512]{2,1,0:T(8,128)(2,1)} %get-tuple-element.22) | copy-start | bytes 11010052
  114.8 3.4 %collective-permute-start.6 = (bf16[1,256,512]{2,1,0:T(8,128)(2,1)S(1)}, bf16[1,256,512]{2,1,0:T(8,128)(2,1)S(1)}, u32[]{:S(2)}, u32[]{:S(2)}) collective-permute-start(bf16[1,256,512]{2,1,0:T(8,128)(2,1)S(1)} %after.5.refs_0_), channel_id=1, source_target_pairs={{0,1},{1,0},{2,3},{3,2},{4,5},{5,4},{6,7},{7,6},{8,9},{9,8},{10,11... | collective-permute-start | bytes 786440 | tf_op jit(solution)/shard_map/ppermute | solution.py:25
  115.2 3.1 %copy-start = (bf16[1,4,512,512]{3,2,1,0:T(8,128)(2,1)S(1)}, bf16[1,4,512,512]{3,2,1,0:T(8,128)(2,1)}, u32[]{:S(2)}) copy-start(bf16[1,4,512,512]{3,2,1,0:T(8,128)(2,1)} %get-tuple-element.13.through_hbm) | copy-start | bytes 6291460

commit v5 on v4

--- a/solution.py
+++ b/solution.py
@@ -11,8 +11,10 @@
 GROUP = 8
 MIB = 1 << 20
 SWEEP_MIB = 54
-APPLIED_MIB = 40
 ANY = pl.BlockSpec(memory_space=pl.ANY)
+TOKEN = pltpu.VMEM((8, 128), jnp.float32)
+WHOLE = pl.BlockSpec(memory_space=pltpu.VMEM)
+SCALARS = pl.BlockSpec(memory_space=pltpu.SMEM)
 
 
 def passed_along(array, axis, by):
@@ -29,16 +31,20 @@
     return lax.dot_general(left, right, (contract, ((), ())), preferred_element_type=jnp.float32)
 
 
-def after(array, *others):
+def near(array):
+    return pltpu.with_memory_space_constraint(array, pltpu.VMEM)
+
+
+def after(array, token):
     return pl.pallas_call(
         lambda *refs: None,
-        in_specs=[ANY] * (1 + len(others)),
+        in_specs=[ANY, WHOLE],
         out_specs=ANY,
         out_shape=jax.ShapeDtypeStruct(array.shape, array.dtype),
         input_output_aliases={0: 0},
         compiler_params=pltpu.CompilerParams(vmem_limit_bytes=MIB),
         name="after",
-    )(array, *others)
+    )(array, near(token))
 
 
 def block_diagonal(bonds, mw, phys):
@@ -58,11 +64,6 @@
     return jnp.where(same, spread, 0.0).astype(jnp.bfloat16)
 
 
-TOKEN = jax.ShapeDtypeStruct((8, 128), jnp.float32)
-WHOLE = pl.BlockSpec(memory_space=pltpu.VMEM)
-SCALARS = pl.BlockSpec(memory_space=pltpu.SMEM)
-
-
 def own_first(swap, first, second, axis):
     return jnp.concatenate(
         [jnp.where(swap, second, first), jnp.where(swap, first, second)], axis=axis
@@ -113,7 +114,7 @@
             first += count
         return found
 
-    here_copy = pltpu.make_async_copy(here_hbm, here_ref, here_sem)
+    here_copy = pltpu.make_async_copy(here_hbm.at[0], here_ref, here_sem)
     for n in range(max(blocks, num_states)):
         if n < blocks:
             env_copy(n).start()
@@ -144,6 +145,13 @@
                 for copy in wave_copies(k):
                     copy.wait()
 
+                @pl.when(k == 0)
+                def _():
+                    here_copy.wait()
+
+            here = here_ref[k, pl.ds(pl.multiple_of(i * rows, rows), rows)]
+            at = pl.multiple_of((k * blocks + i) * rows * phys, rows * phys)
+            turned[:, pl.ds(at, rows * phys)] = here.reshape(rows * phys, chi).T
             for t in range(phys):
                 inner = product(lhs[...], wave_ref[k, t], ((1,), (0,))).astype(jnp.bfloat16)
                 low[:, t * part : (t + 1) * part, :] = inner.reshape(groups, part, chi)
@@ -161,10 +169,7 @@
 
     lax.fori_loop(0, blocks, block, 0)
 
-    here_copy.wait()
     depth = rows_all * phys
-    for k in range(num_states):
-        turned[:, k * depth : (k + 1) * depth] = here_ref[k].T
 
     def out_copies(v, slot):
         return [
@@ -217,7 +222,7 @@
         out_specs=[ANY] * len(counts) + [WHOLE] + [ANY] * parts,
         scratch_shapes=[
             pltpu.VMEM(env.shape, bf16),
-            pltpu.VMEM(here.shape, bf16),
+            pltpu.VMEM(here.shape[1:], bf16),
             pltpu.VMEM((num_states, phys, chi_in, chi), bf16),
             pltpu.VMEM((mw * rows, chi_in), bf16),
             pltpu.VMEM((rows // GROUP, padded, chi), bf16),
@@ -248,80 +253,68 @@
     return out[:pieces], out[pieces], out[pieces + 1 :]
 
 
-def applied_kernel(parts, begun, places, through_hbm, *refs):
-    rights_hbm, refs = refs[:parts], refs[parts:]
+def applied_kernel(parts, begun, close, places, through_in, *refs):
+    rights, refs = refs[:parts], refs[parts:]
     if begun:
-        held_hbm, refs = refs[0], refs[1:]
-    out_hbm, token_ref, through_ref, rights, turned, results = refs[:6]
-    through_sems, right_sems, out_sems = refs[6:9]
-    if begun:
-        held, held_sems = refs[9:]
-    last = out_hbm.dtype == jnp.bfloat16
-    count, num_states, rows, chi = through_hbm.shape
-    width = rights_hbm[0].shape[1]
-
-    def right_copies(v):
-        return [
-            pltpu.make_async_copy(
-                right.at[v], rights.at[v, pl.ds(index * width, width)], right_sems.at[v, index]
-            )
-            for index, right in enumerate(rights_hbm)
-        ]
+        held, refs = refs[0], refs[1:]
+    out, token_ref, turned, refs = refs[0], refs[1], refs[2], refs[3:]
+    last = out.dtype == jnp.bfloat16
+    count, num_states, rows, chi = through_in.shape
+    if last:
+        results, out_sems, refs = refs[0], refs[1], refs[2:]
+    if close:
+        through_ref = through_in
+    else:
+        through_ref, through_sems = refs
 
     def through_copies(k):
         return [
-            pltpu.make_async_copy(through_hbm.at[v, k], through_ref.at[v, k], through_sems.at[v, k])
+            pltpu.make_async_copy(through_in.at[v, k], through_ref.at[v, k], through_sems.at[v, k])
             for v in range(count)
         ]
 
-    def held_copy(k):
-        return pltpu.make_async_copy(held_hbm.at[k], held.at[k], held_sems.at[k])
-
     def out_copy(k, slot):
-        return pltpu.make_async_copy(results.at[slot], out_hbm.at[k], out_sems.at[slot])
-
+        return pltpu.make_async_copy(results.at[slot], out.at[k], out_sems.at[slot])
+
+    if not close:
+        for k in range(num_states):
+            for copy in through_copies(k):
+                copy.start()
     for v in range(count):
-        for copy in right_copies(v):
-            copy.start()
-    for k in range(num_states):
-        for copy in through_copies(k):
-            copy.start()
-        if begun:
-            held_copy(k).start()
-    for v in range(count):
-        for copy in right_copies(v):
-            copy.wait()
-        turned[v * chi : (v + 1) * chi, :] = rights[v].T
+        right = jnp.concatenate([right[v] for right in rights], axis=0)
+        turned[v * chi : (v + 1) * chi, :] = right.T
 
     def state(k, _):
-        for copy in through_copies(k):
-            copy.wait()
+        if not close:
+            for copy in through_copies(k):
+                copy.wait()
         left = jnp.concatenate([through_ref[v, k] for v in range(count)], axis=1)
         total = product(left, turned[...], ((1,), (0,)))
         if begun:
-            held_copy(k).wait()
             total = total + held[k]
-        if last:
-            columns = total.shape[1]
-            phys = results.shape[2]
-            total = total.astype(jnp.bfloat16)
-            if parts == 2:
-                swap = places[0] != 0
-                total = own_first(swap, total[:, : columns // 2], total[:, columns // 2 :], 1)
-            total = total.reshape(rows // phys, phys, columns)
+        if not last:
+            out[k] = total
+            return 0
+        columns = total.shape[1]
+        phys = results.shape[2]
+        total = total.astype(jnp.bfloat16)
+        if parts == 2:
+            swap = places[0] != 0
+            total = own_first(swap, total[:, : columns // 2], total[:, columns // 2 :], 1)
         slot = k % 2
 
         @pl.when(k >= 2)
         def _():
             out_copy(k - 2, slot).wait()
 
-        results[slot] = total
+        results[slot] = total.reshape(rows // phys, phys, columns)
         out_copy(k, slot).start()
         return 0
 
     lax.fori_loop(0, num_states, state, 0)
-    for k in range(max(num_states - 2, 0), num_states):
-        out_copy(k, k % 2).wait()
+    if last:
+        for k in range(max(num_states - 2, 0), num_states):
+            out_copy(k, k % 2).wait()
     token_ref[...] = jnp.zeros_like(token_ref)
 
 
@@ -330,35 +323,29 @@
     width = rights[0].shape[1]
     parts = len(rights)
     begun = held is not None
+    close = count <= 4
     columns = width * parts
+    scratch = [pltpu.VMEM((count * chi, columns), jnp.bfloat16)]
     if last:
-        out_shape = jax.ShapeDtypeStruct((num_states, rows // phys, phys, columns), jnp.bfloat16)
+        shape = (num_states, rows // phys, phys, columns)
+        out_shape, out_spec = jax.ShapeDtypeStruct(shape, jnp.bfloat16), ANY
+        scratch += [pltpu.VMEM((2,) + shape[1:], jnp.bfloat16), pltpu.SemaphoreType.DMA((2,))]
     else:
-        out_shape = jax.ShapeDtypeStruct((num_states, rows, columns), jnp.float32)
-    operands = [through, *rights] + ([held] if begun else [])
+        out_shape, out_spec = pltpu.VMEM((num_states, rows, columns), jnp.float32), WHOLE
+    if not close:
+        scratch += [
+            pltpu.VMEM(through.shape, jnp.bfloat16),
+            pltpu.SemaphoreType.DMA((count, num_states)),
+        ]
+    operands = [near(through) if close else through]
+    operands += [near(right) for right in rights] + ([near(held)] if begun else [])
     return pl.pallas_call(
-        functools.partial(applied_kernel, parts, begun),
-        in_specs=[SCALARS] + [ANY] * len(operands),
-        out_specs=[ANY, WHOLE],
+        functools.partial(applied_kernel, parts, begun, close),
+        in_specs=[SCALARS, WHOLE if close else ANY] + [WHOLE] * (len(operands) - 1),
+        out_specs=[out_spec, WHOLE],
         out_shape=[out_shape, TOKEN],
-        scratch_shapes=[
-            pltpu.VMEM(through.shape, jnp.bfloat16),
-            pltpu.VMEM((count, columns, chi), jnp.bfloat16),
-            pltpu.VMEM((count * chi, columns), jnp.bfloat16),
-            pltpu.VMEM((2,) + out_shape.shape[1:], out_shape.dtype),
-            pltpu.SemaphoreType.DMA((count, num_states)),
-            pltpu.SemaphoreType.DMA((count, parts)),
-            pltpu.SemaphoreType.DMA((2,)),
-        ]
-        + (
-            [
-                pltpu.VMEM((num_states, rows, columns), jnp.float32),
-                pltpu.SemaphoreType.DMA((num_states,)),
-            ]
-            if begun
-            else []
-        ),
-        compiler_params=pltpu.CompilerParams(vmem_limit_bytes=APPLIED_MIB * MIB),
+        scratch_shapes=scratch,
+        compiler_params=pltpu.CompilerParams(vmem_limit_bytes=(16 if close else 34) * MIB),
         cost_estimate=pl.CostEstimate(
             flops=2 * num_states * rows * columns * count * chi,
             bytes_accessed=2 * count * num_states * rows * chi,
@@ -369,7 +356,7 @@
 
 
 def cuts(size):
-    middle = max((size - 1) * 5 // 13, 0)
+    middle = max((size - 1) * 3 // 13, 0)
     sizes = [count for count in (size - 1 - middle, middle, 1) if count > 0]
     found, at = [], 0
     for count in sizes:
@@ -397,10 +384,9 @@
         waves = [wave_split, swapped(wave_split, "bond")]
     else:
         waves = [lax.all_gather(wave_split, "bond", axis=2, tiled=True)]
-    here = states[0].reshape(num_states, rows * phys, chi)
     bond_table = mpo.transpose(3, 1, 2, 0).reshape(mw * phys, phys * mw)
     counts = [count for _, count in starts]
-    throughs, token, shares = sweep(bond_table, left, here, waves, places, counts, scaling)
+    throughs, token, shares = sweep(bond_table, left, states, waves, places, counts, scaling)
     if paired:
         arrived = swapped(shares[1], "bond")
         new_env = shares[0].astype(jnp.float32) + arrived.astype(jnp.float32)

time: 126 us -> 116 us (0.921)
  local copies, waits for them, and re-layouts: 12.9 us -> 8.21 us
  Pallas kernels: 78.6 us -> 74.1 us
  waiting for transfers between devices: 16.5 us -> 13 us
  starting transfers between devices: 10.9 us -> 13.5 us
    ppermute x3, waiting for transfers between devices: 15.8 us -> 10.2 us  [passed_along(): return lax.ppermute(array, axis, pairs)]
    pallas_call x6, Pallas kernels: 29.6 us -> 24.4 us  [the longest x3 24.4 us: applied_part(): pl.pallas_call(functools.partial(applied_kernel, parts, begun, close), in...]
    another operation x1 -> x0, local copies, waits for them, and re-layouts: 4.1 us -> none  [on_device(): here = states[0].reshape(num_states, rows * phys, chi)]
    ppermute x3, starting transfers between devices: 8.27 us -> 10.4 us  [passed_along(): return lax.ppermute(array, axis, pairs)]
    ppermute x5, waiting for transfers between devices: 0.68 us -> 2.81 us  [swapped(): return lax.ppermute(array, axis, [(0, 1), (1, 0)])]
    unnamed x13 -> x15, local copies, waits for them, and re-layouts: 4.11 us -> 3.47 us
  transfers between devices with their start and end apart: 8 -> 8, of which waited for: 2 -> 4; matrix products, arithmetic and copies ran while one was open for 10% -> 8% of each run, Pallas kernels for 60% -> 62%
where the time goes in v5:
time: 116 us; the launch traced here: 113 us
  Pallas kernels  74.1 us (64%)
  starting transfers between devices  13.5 us (12%)
  waiting for transfers between devices  13 us (11%)
  local copies, waits for them, and re-layouts  8.21 us (7%)
  other arithmetic  3.79 us (3%)
    pallas_call x1, Pallas kernels, sweep(): pl.pallas_call(functools.partial(sweep_kernel, parts, len(counts), scalin...  49.8 us
    pallas_call x3, Pallas kernels, applied_part(): pl.pallas_call(functools.partial(applied_kernel, parts, begun, close), in...  24.4 us
    ppermute x3, starting transfers between devices, passed_along(): return lax.ppermute(array, axis, pairs)  10.4 us
    ppermute x3, waiting for transfers between devices, passed_along(): return lax.ppermute(array, axis, pairs)  10.2 us
    slice x3, local copies, waits for them, and re-layouts, on_device(): right[at:at + count]  3.93 us
    unnamed x15, local copies, waits for them, and re-layouts  3.47 us
    broadcast_in_dim x1, other arithmetic, on_device(): return (held[None], new_env.transpose(1, 0, 2)[None])  3.13 us
    ppermute x5, starting transfers between devices, swapped(): return lax.ppermute(array, axis, [(0, 1), (1, 0)])  3.09 us
  transfers between devices with their start and end apart: 8, of which 4 were waited for; matrix products, arithmetic and copies ran while one was open for 8% of the time, Pallas kernels for 62%

profile of v5, /device:TPU:13, one launch (start us, length us, event | category | flops | bytes accessed | tf_op | source)
XLA Modules:
  0.0 113.5 jit_solution(13884640570558251333)
XLA Ops:
  0.6 0.0 copy-start.2
  0.6 3.4 %copy.12 = bf16[1,4,256,2,512]{4,2,3,1,0:T(8,128)(2,1)} copy(bf16[1,4,256,2,512]{4,3,2,1,0:T(2,128)(2,1)} %here_hbm.1) | data formatting | bytes 4194304 | tf_op args[2]
  4.1 0.7 collective-permute-start
  4.8 1.6 %slice.14 = bf16[10,256,512]{2,1,0:T(8,128)(2,1)} slice(bf16[14,256,512]{2,1,0:T(8,128)(2,1)S(1)} %bitcast.23), slice={[0:10], [0:256], [0:512]} | slice | bytes 5242880 | tf_op jit(solution)/shard_map/slice | solution.py:380
  6.4 3.0 %collective-permute-start.3 = (bf16[10,256,512]{2,1,0:T(8,128)(2,1)}, bf16[10,256,512]{2,1,0:T(8,128)(2,1)S(1)}, u32[]{:S(2)}, u32[]{:S(2)}) collective-permute-start(bf16[10,256,512]{2,1,0:T(8,128)(2,1)} %slice.14), channel_id=1, source_target_pairs={{2,0},{4,2},{6,4},{8,6},{10,8},{12,10},{14,12},{16,14},{18,16},{20... | collective-permute-start | bytes 7864328 | tf_op jit(solution)/shard_map/ppermute | solution.py:23
  9.5 0.1 copy.9
  9.6 0.7 reshape.7.bonds_ref
  10.3 0.7 pad_add_fusion.places
  10.9 49.8 %sweep.1 = (bf16[10,4,512,512]{3,2,1,0:T(8,128)(2,1)}, bf16[3,4,512,512]{3,2,1,0:T(8,128)(2,1)}, bf16[1,4,512,512]{3,2,1,0:T(8,128)(2,1)}, f32[8,128]{1,0:T(8,12...) custom-call(s32[2]{0:T(128)} %pad_add_fusion.places, bf16[28,28]{1,0:T(8,128)(2,1)} %reshape.7.bonds_ref, ...), custom_call_target="tpu_custom_call" | custom-call | flops 37580963840 | bytes 29360128 | tf_op jit(solution)/shard_map/sweep/pallas_call | solution.py:219
  60.7 6.3 %collective-permute-done.3.refs_0_ = bf16[10,256,512]{2,1,0:T(8,128)(2,1)S(1)} collective-permute-done((bf16[10,256,512]{2,1,0:T(8,128)(2,1)}, bf16[10,256,512]{2,1,0:T(8,128)(2,1)S(1)}, u32[]{:S(2)}, u32[]{:S(2)}) %collective-permute-start.3) | collective-permute-done | bytes 2621472 | tf_op jit(solution)/shard_map/ppermute | solution.py:23
  67.0 0.8 collective-permute-start.4
  67.8 1.3 %slice.13 = bf16[3,256,512]{2,1,0:T(8,128)(2,1)S(1)} slice(bf16[14,256,512]{2,1,0:T(8,128)(2,1)} %bitcast.21), slice={[10:13], [0:256], [0:512]} | slice | bytes 1572864 | tf_op jit(solution)/shard_map/slice | solution.py:380
  69.1 4.1 %collective-permute-start.2 = (bf16[3,256,512]{2,1,0:T(8,128)(2,1)S(1)}, bf16[3,256,512]{2,1,0:T(8,128)(2,1)S(1)}, u32[]{:S(2)}, u32[]{:S(2)}) collective-permute-start(bf16[3,256,512]{2,1,0:T(8,128)(2,1)S(1)} %slice.13), channel_id=1, source_target_pairs={{2,0},{4,2},{6,4},{8,6},{10,8},{12,10},{14,12},{16,14},{18,16},{20... | collective-permute-start | bytes 2359304 | tf_op jit(solution)/shard_map/ppermute | solution.py:23
  73.2 2.8 %collective-permute-done.4.refs_1_ = bf16[10,256,512]{2,1,0:T(8,128)(2,1)S(1)} collective-permute-done((bf16[10,256,512]{2,1,0:T(8,128)(2,1)S(1)}, bf16[10,256,512]{2,1,0:T(8,128)(2,1)S(1)}, u32[]{:S(2)}, u32[]{:S(2)}) %collective-permute-start.4) | collective-permute-done | bytes 2621472 | tf_op jit(solution)/shard_map/ppermute | solution.py:27
  76.0 15.2 %applied_part.3 = (f32[4,512,512]{2,1,0:T(8,128)S(1)}, f32[8,128]{1,0:T(8,128)S(1)}) custom-call(s32[2]{0:T(128)S(1)} %copy-done.1, bf16[10,4,512,512]{3,2,1,0:T(8,128)(2,1)} %get-tuple-element.15.through_in, bf16[10,256,512]{2,1,0:T(8,128)(2,1)S(1)} %after.3.refs_0_, bf16[10,256,512]{2,1,0:T(8,128)(2,1)S(1)} %collective-permute-done.4.refs_1_), custom_call_target="tpu_custom_call" | custom-call | flops 10737418240 | bytes 20971520 | tf_op jit(solution)/shard_map/applied_part/pallas_call | solution.py:342
  91.2 0.4 collective-permute-done.2.refs_0_
  91.6 1.0 collective-permute-start.5
  92.7 1.0 slice.12
  93.6 3.3 %collective-permute-start.1 = (bf16[1,256,512]{2,1,0:T(8,128)(2,1)S(1)}, bf16[1,256,512]{2,1,0:T(8,128)(2,1)S(1)}, u32[]{:S(2)}, u32[]{:S(2)}) collective-permute-start(bf16[1,256,512]{2,1,0:T(8,128)(2,1)S(1)} %slice.12), channel_id=1, source_target_pairs={{2,0},{4,2},{6,4},{8,6},{10,8},{12,10},{14,12},{16,14},{18,16},{20... | collective-permute-start | bytes 786440 | tf_op jit(solution)/shard_map/ppermute | solution.py:23
  97.0 4.9 %applied_part.4 = (f32[4,512,512]{2,1,0:T(8,128)S(1)}, f32[8,128]{1,0:T(8,128)S(1)}) custom-call(s32[2]{0:T(128)S(1)} %copy-done.1, bf16[3,4,512,512]{3,2,1,0:T(8,128)(2,1)S(1)} %bitcast.20, bf16[3,256,512]{2,1,0:T(8,128)(2,1)S(1)} %after.4.refs_0_, bf16[3,256,512]{2,1,0:T(8,128)(2,1)S(1)} %collective-permute-done.5.refs_1_, ...), custom_call_target="tpu_custom_call" | custom-call | flops 3221225472 | bytes 6291456 | tf_op jit(solution)/shard_map/applied_part/pallas_call | solution.py:342
  101.9 3.6 %collective-permute-done.1.refs_0_ = bf16[1,256,512]{2,1,0:T(8,128)(2,1)S(1)} collective-permute-done((bf16[1,256,512]{2,1,0:T(8,128)(2,1)S(1)}, bf16[1,256,512]{2,1,0:T(8,128)(2,1)S(1)}, u32[]{:S(2)}, u32[]{:S(2)}) %collective-permute-start.1) | collective-permute-done | bytes 262176 | tf_op jit(solution)/shard_map/ppermute | solution.py:23
  105.5 0.6 collective-permute-start.6
  106.0 3.1 %fusion = bf16[1,256,14,512]{3,1,2,0:T(8,128)(2,1)} fusion(bf16[14,256,512]{2,1,0:T(8,128)(2,1)S(1)} %collective-permute-done.7, bf16[14,256,512]{2,1,0:T(8,128)(2,1)S(1)} %copy-done.3), kind=kLoop, calls=%fused_computation.1 | loop fusion | flops 7340032 | bytes 11010048 | tf_op jit(solution)/shard_map/broadcast_in_dim | solution.py:406
  109.2 4.3 %applied_part.5 = (bf16[4,256,2,512]{3,2,1,0:T(2,128)(2,1)}, f32[8,128]{1,0:T(8,128)}) custom-call(s32[2]{0:T(128)S(1)} %copy-done.1, bf16[1,4,512,512]{3,2,1,0:T(8,128)(2,1)S(1)} %copy-done, bf16[1,256,512]{2,1,0:T(8,128)(2,1)S(1)} %after.5.refs_0_, bf16[1,256,512]{2,1,0:T(8,128)(2,1)S(1)} %collective-permute-done.6.refs_1_, ...), custom_call_target="tpu_custom_call" | custom-call | flops 1073741824 | bytes 2097152 | tf_op jit(solution)/shard_map/applied_part/pallas_call | solution.py:342
  (22 shorter events, 0.0 us)
Async XLA Ops:
  0.6 4.1 %copy-start.2 = (bf16[1,256,14,512]{3,1,2,0:T(8,128)(2,1)S(1)}, bf16[1,256,14,512]{3,1,2,0:T(8,128)(2,1)}, u32[]{:S(2)}) copy-start(bf16[1,256,14,512]{3,1,2,0:T(8,128)(2,1)} %param.5) | copy-start | bytes 11010052
  4.1 5.4 %copy-start.4 = (bf16[14,2,2,14]{3,2,1,0:T(2,128)(2,1)S(1)}, bf16[14,2,2,14]{3,2,1,0:T(2,128)(2,1)}, u32[]{:S(2)}) copy-start(bf16[14,2,2,14]{3,2,1,0:T(2,128)(2,1)} %param.7) | copy-start | bytes 4708
  4.1 6.9 %collective-permute-start = (bf16[4,2,256,512]{3,2,1,0:T(8,128)(2,1)}, bf16[4,2,256,512]{3,2,1,0:T(8,128)(2,1)}, u32[]{:S(2)}, u32[]{:S(2)}) collective-permute-start(bf16[4,2,256,512]{3,2,1,0:T(8,128)(2,1)} %bitcast.18.refs_0_), channel_id=1, source_target_pairs={{0,1},{1,0},{2,3},{3,2},{4,5},{5,4},{6,7},{7,6},{8,9},{9,8},{10,11... | collective-permute-start | bytes 6291464 | tf_op jit(solution)/shard_map/ppermute | solution.py:27
  6.4 60.6 %collective-permute-start.3 = (bf16[10,256,512]{2,1,0:T(8,128)(2,1)}, bf16[10,256,512]{2,1,0:T(8,128)(2,1)S(1)}, u32[]{:S(2)}, u32[]{:S(2)}) collective-permute-start(bf16[10,256,512]{2,1,0:T(8,128)(2,1)} %slice.14), channel_id=1, source_target_pairs={{2,0},{4,2},{6,4},{8,6},{10,8},{12,10},{14,12},{16,14},{18,16},{20... | collective-permute-start | bytes 7864328 | tf_op jit(solution)/shard_map/ppermute | solution.py:23
  60.7 15.3 %copy-start.1 = (s32[2]{0:T(128)S(1)}, s32[2]{0:T(128)}, u32[]{:S(2)}) copy-start(s32[2]{0:T(128)} %pad_add_fusion.places) | copy-start | bytes 28
  67.0 9.0 %collective-permute-start.4 = (bf16[10,256,512]{2,1,0:T(8,128)(2,1)S(1)}, bf16[10,256,512]{2,1,0:T(8,128)(2,1)S(1)}, u32[]{:S(2)}, u32[]{:S(2)}) collective-permute-start(bf16[10,256,512]{2,1,0:T(8,128)(2,1)S(1)} %after.3.refs_0_), channel_id=1, source_target_pairs={{0,1},{1,0},{2,3},{3,2},{4,5},{5,4},{6,7},{7,6},{8,9},{9,8},{10,11... | collective-permute-start | bytes 7864328 | tf_op jit(solution)/shard_map/ppermute | solution.py:27
  67.8 38.3 %collective-permute-start.7 = (bf16[14,256,512]{2,1,0:T(8,128)(2,1)}, bf16[14,256,512]{2,1,0:T(8,128)(2,1)S(1)}, u32[]{:S(2)}, u32[]{:S(2)}) collective-permute-start(bf16[14,256,512]{2,1,0:T(8,128)(2,1)} %get-tuple-element.23), channel_id=1, source_target_pairs={{0,1},{1,0},{2,3},{3,2},{4,5},{5,4},{6,7},{7,6},{8,9},{9,8},{10,11... | collective-permute-start | bytes 11010056 | tf_op jit(solution)/shard_map/ppermute | solution.py:27
  67.8 29.2 %slice-start = ((s8[6291456]{0:T(1024)(128)(4,1)}), s8[4194304]{0:T(1024)(128)(4,1)S(1)}, s32[]{:S(2)}) async-start(s8[6291456]{0:T(1024)(128)(4,1)} %bitcast.19), calls=%async_computation | async-start | bytes 8388608
  69.1 22.5 %collective-permute-start.2 = (bf16[3,256,512]{2,1,0:T(8,128)(2,1)S(1)}, bf16[3,256,512]{2,1,0:T(8,128)(2,1)S(1)}, u32[]{:S(2)}, u32[]{:S(2)}) collective-permute-start(bf16[3,256,512]{2,1,0:T(8,128)(2,1)S(1)} %slice.13), channel_id=1, source_target_pairs={{2,0},{4,2},{6,4},{8,6},{10,8},{12,10},{14,12},{16,14},{18,16},{20... | collective-permute-start | bytes 2359304 | tf_op jit(solution)/shard_map/ppermute | solution.py:23
  76.0 20.9 %slice-start.1 = ((s8[6291456]{0:T(1024)(128)(4,1)}), s8[2097152]{0:T(1024)(128)(4,1)S(1)}, s32[]{:S(2)}) async-start(s8[6291456]{0:T(1024)(128)(4,1)} %bitcast.19), calls=%async_computation.1 | async-start | bytes 4194304
  91.6 5.3 %collective-permute-start.5 = (bf16[3,256,512]{2,1,0:T(8,128)(2,1)S(1)}, bf16[3,256,512]{2,1,0:T(8,128)(2,1)S(1)}, u32[]{:S(2)}, u32[]{:S(2)}) collective-permute-start(bf16[3,256,512]{2,1,0:T(8,128)(2,1)S(1)} %after.4.refs_0_), channel_id=1, source_target_pairs={{0,1},{1,0},{2,3},{3,2},{4,5},{5,4},{6,7},{7,6},{8,9},{9,8},{10,11... | collective-permute-start | bytes 2359304 | tf_op jit(solution)/shard_map/ppermute | solution.py:27
  93.6 11.8 %collective-permute-start.1 = (bf16[1,256,512]{2,1,0:T(8,128)(2,1)S(1)}, bf16[1,256,512]{2,1,0:T(8,128)(2,1)S(1)}, u32[]{:S(2)}, u32[]{:S(2)}) collective-permute-start(bf16[1,256,512]{2,1,0:T(8,128)(2,1)S(1)} %slice.12), channel_id=1, source_target_pairs={{2,0},{4,2},{6,4},{8,6},{10,8},{12,10},{14,12},{16,14},{18,16},{20... | collective-permute-start | bytes 786440 | tf_op jit(solution)/shard_map/ppermute | solution.py:23
  97.0 9.1 %copy-start.3 = (bf16[14,256,512]{2,1,0:T(8,128)(2,1)S(1)}, bf16[14,256,512]{2,1,0:T(8,128)(2,1)}, u32[]{:S(2)}) copy-start(bf16[14,256,512]{2,1,0:T(8,128)(2,1)} %get-tuple-element.22) | copy-start | bytes 11010052
  105.5 3.7 %collective-permute-start.6 = (bf16[1,256,512]{2,1,0:T(8,128)(2,1)S(1)}, bf16[1,256,512]{2,1,0:T(8,128)(2,1)S(1)}, u32[]{:S(2)}, u32[]{:S(2)}) collective-permute-start(bf16[1,256,512]{2,1,0:T(8,128)(2,1)S(1)} %after.5.refs_0_), channel_id=1, source_target_pairs={{0,1},{1,0},{2,3},{3,2},{4,5},{5,4},{6,7},{7,6},{8,9},{9,8},{10,11... | collective-permute-start | bytes 786440 | tf_op jit(solution)/shard_map/ppermute | solution.py:27
  106.0 3.1 %copy-start = (bf16[1,4,512,512]{3,2,1,0:T(8,128)(2,1)S(1)}, bf16[1,4,512,512]{3,2,1,0:T(8,128)(2,1)}, u32[]{:S(2)}) copy-start(bf16[1,4,512,512]{3,2,1,0:T(8,128)(2,1)} %get-tuple-element.13.through_in) | copy-start | bytes 6291460

commit v6 on v5

--- a/solution.py
+++ b/solution.py
@@ -33,6 +33,10 @@
 
 def near(array):
     return pltpu.with_memory_space_constraint(array, pltpu.VMEM)
+
+
+def far(array):
+    return pltpu.with_memory_space_constraint(array, pltpu.HBM)
 
 
 def after(array, token):
@@ -253,8 +257,8 @@
     return out[:pieces], out[pieces], out[pieces + 1 :]
 
 
-def applied_kernel(parts, begun, close, places, through_in, *refs):
-    rights, refs = refs[:parts], refs[parts:]
+def applied_kernel(parts, pieces, begun, close, places, through_in, *refs):
+    rights, refs = refs[: parts * pieces], refs[parts * pieces :]
     if begun:
         held, refs = refs[0], refs[1:]
     out, token_ref, turned, refs = refs[0], refs[1], refs[2], refs[3:]
@@ -280,9 +284,13 @@
         for k in range(num_states):
             for copy in through_copies(k):
                 copy.start()
-    for v in range(count):
-        right = jnp.concatenate([right[v] for right in rights], axis=0)
-        turned[v * chi : (v + 1) * chi, :] = right.T
+    v = 0
+    for piece in range(pieces):
+        blocks = rights[piece * parts : (piece + 1) * parts]
+        for n in range(blocks[0].shape[0]):
+            right = jnp.concatenate([block[n] for block in blocks], axis=0)
+            turned[v * chi : (v + 1) * chi, :] = right.T
+            v += 1
 
     def state(k, _):
         if not close:
@@ -320,8 +328,8 @@
 
 def applied_part(through, rights, held, places, phys, last):
     count, num_states, rows, chi = through.shape
-    width = rights[0].shape[1]
-    parts = len(rights)
+    width = rights[0][0].shape[1]
+    parts = len(rights[0])
     begun = held is not None
     close = count <= 4
     columns = width * parts
@@ -337,18 +345,18 @@
             pltpu.VMEM(through.shape, jnp.bfloat16),
             pltpu.SemaphoreType.DMA((count, num_states)),
         ]
-    operands = [near(through) if close else through]
-    operands += [near(right) for right in rights] + ([near(held)] if begun else [])
+    operands = [near(through) if close else far(through)]
+    operands += [near(block) for blocks in rights for block in blocks] + ([near(held)] if begun else [])
     return pl.pallas_call(
-        functools.partial(applied_kernel, parts, begun, close),
+        functools.partial(applied_kernel, parts, len(rights), begun, close),
         in_specs=[SCALARS, WHOLE if close else ANY] + [WHOLE] * (len(operands) - 1),
         out_specs=[out_spec, WHOLE],
         out_shape=[out_shape, TOKEN],
         scratch_shapes=scratch,
         compiler_params=pltpu.CompilerParams(vmem_limit_bytes=(16 if close else 34) * MIB),
         cost_estimate=pl.CostEstimate(
-            flops=2 * num_states * rows * columns * count * chi,
-            bytes_accessed=2 * count * num_states * rows * chi,
+            flops=0,
+            bytes_accessed=0,
             transcendentals=0,
         ),
         name="applied_part",
@@ -356,13 +364,8 @@
 
 
 def cuts(size):
-    middle = max((size - 1) * 3 // 13, 0)
-    sizes = [count for count in (size - 1 - middle, middle, 1) if count > 0]
-    found, at = [], 0
-    for count in sizes:
-        found.append((at, count))
-        at += count
-    return found
+    first = (size - 1) * 6 // 13
+    return [[count] for count in (first, size - 1 - first, 1) if count > 0]
 
 
 def on_device(left_env, right_env, states, mpo):
@@ -376,8 +379,14 @@
     left = left_env[0].transpose(1, 0, 2)
     right = right_env[0].transpose(1, 0, 2)
 
-    starts = cuts(mw)
-    pieces = [passed_along(right[at : at + count], "seg", -1) for at, count in starts]
+    stages = cuts(mw)
+    pieces, first = [], 0
+    for stage in stages:
+        pieces.append([])
+        for count in stage:
+            piece = passed_along(right[first : first + count], "seg", -1)
+            pieces[-1].append(piece)
+            first += count
 
     wave_split = states[0].transpose(0, 2, 1, 3)
     if paired:
@@ -385,7 +394,7 @@
     else:
         waves = [lax.all_gather(wave_split, "bond", axis=2, tiled=True)]
     bond_table = mpo.transpose(3, 1, 2, 0).reshape(mw * phys, phys * mw)
-    counts = [count for _, count in starts]
+    counts = [sum(stage) for stage in stages]
     throughs, token, shares = sweep(bond_table, left, states, waves, places, counts, scaling)
     if paired:
         arrived = swapped(shares[1], "bond")
@@ -395,12 +404,14 @@
         new_env = lax.psum_scatter(shares[0], "bond", scatter_dimension=1, tiled=True)
 
     held = None
-    for index, (through, piece) in enumerate(zip(throughs, pieces)):
-        if paired:
-            piece = after(piece, token)
-            rights = [piece, swapped(piece, "bond")]
-        else:
-            rights = [lax.all_gather(piece, "bond", axis=1, tiled=True)]
+    for index, (through, stage) in enumerate(zip(throughs, pieces)):
+        rights = []
+        for piece in stage:
+            if paired:
+                piece = after(piece, token)
+                rights.append([piece, swapped(piece, "bond")])
+            else:
+                rights.append([lax.all_gather(piece, "bond", axis=1, tiled=True)])
         last = index == len(pieces) - 1
         held, token = applied_part(through, rights, held, places, phys, last)
     return (held[None], new_env.transpose(1, 0, 2)[None])

time: 116 us -> 111 us (0.957)
  waiting for transfers between devices: 13 us -> 8.42 us
  Pallas kernels: 74.1 us -> 76.3 us
  starting transfers between devices: 13.5 us -> 11.7 us
    ppermute x3, waiting for transfers between devices: 10.2 us -> 0.36 us  [passed_along(): return lax.ppermute(array, axis, pairs)]
    ppermute x5, waiting for transfers between devices: 2.81 us -> 8.07 us  [swapped(): return lax.ppermute(array, axis, [(0, 1), (1, 0)])]
    pallas_call x3, Pallas kernels: 24.4 us -> 26.4 us  [applied_part(): pl.pallas_call(functools.partial(applied_kernel, parts, len(rights), begu...]
    ppermute x3, starting transfers between devices: 10.4 us -> 9.16 us  [passed_along(): return lax.ppermute(array, axis, pairs)]
    unnamed x15 -> x11, local copies, waits for them, and re-layouts: 3.47 us -> 3.46 us
  transfers between devices with their start and end apart: 8 -> 8, of which waited for: 4 -> 2; matrix products, arithmetic and copies ran while one was open for 8% -> 7% of each run, Pallas kernels for 62% -> 66%
where the time goes in v6:
time: 111 us; the launch traced here: 109 us
  Pallas kernels  76.3 us (69%)
  starting transfers between devices  11.7 us (11%)
  waiting for transfers between devices  8.42 us (8%)
  local copies, waits for them, and re-layouts  7.94 us (7%)
  other arithmetic  3.66 us (3%)
    pallas_call x1, Pallas kernels, sweep(): pl.pallas_call(functools.partial(sweep_kernel, parts, len(counts), scalin...  49.8 us
    pallas_call x3, Pallas kernels, applied_part(): pl.pallas_call(functools.partial(applied_kernel, parts, len(rights), begu...  26.4 us
    ppermute x3, starting transfers between devices, passed_along(): return lax.ppermute(array, axis, pairs)  9.16 us
    ppermute x5, waiting for transfers between devices, swapped(): return lax.ppermute(array, axis, [(0, 1), (1, 0)])  8.07 us
    slice x3, local copies, waits for them, and re-layouts, on_device(): piece = passed_along(right[first:first + count], 'seg', -1)  3.67 us
    unnamed x11, local copies, waits for them, and re-layouts  3.46 us
    broadcast_in_dim x1, other arithmetic, on_device(): return (held[None], new_env.transpose(1, 0, 2)[None])  3 us
    ppermute x5, starting transfers between devices, swapped(): return lax.ppermute(array, axis, [(0, 1), (1, 0)])  2.54 us
  transfers between devices with their start and end apart: 8, of which 2 were waited for; matrix products, arithmetic and copies ran while one was open for 7% of the time, Pallas kernels for 66%

profile of v6, /device:TPU:13, one launch (start us, length us, event | category | flops | bytes accessed | tf_op | source)
XLA Modules:
  0.0 108.7 jit_solution(4234707589465047427)
XLA Ops:
  0.6 0.0 copy-start.2
  0.6 3.4 %copy.12 = bf16[1,4,256,2,512]{4,2,3,1,0:T(8,128)(2,1)} copy(bf16[1,4,256,2,512]{4,3,2,1,0:T(2,128)(2,1)} %here_hbm.1) | data formatting | bytes 4194304 | tf_op args[2]
  4.1 0.7 collective-permute-start
  4.8 1.3 %slice.14 = bf16[6,256,512]{2,1,0:T(8,128)(2,1)} slice(bf16[14,256,512]{2,1,0:T(8,128)(2,1)S(1)} %bitcast.20), slice={[0:6], [0:256], [0:512]} | slice | bytes 3145728 | tf_op jit(solution)/shard_map/slice | solution.py:387
  6.1 3.0 %collective-permute-start.3 = (bf16[6,256,512]{2,1,0:T(8,128)(2,1)}, bf16[6,256,512]{2,1,0:T(8,128)(2,1)S(1)}, u32[]{:S(2)}, u32[]{:S(2)}) collective-permute-start(bf16[6,256,512]{2,1,0:T(8,128)(2,1)} %slice.14), channel_id=1, source_target_pairs={{2,0},{4,2},{6,4},{8,6},{10,8},{12,10},{14,12},{16,14},{18,16},{20... | collective-permute-start | bytes 4718600 | tf_op jit(solution)/shard_map/ppermute | solution.py:23
  9.2 1.4 %slice.13 = bf16[7,256,512]{2,1,0:T(8,128)(2,1)} slice(bf16[14,256,512]{2,1,0:T(8,128)(2,1)S(1)} %bitcast.21), slice={[6:13], [0:256], [0:512]} | slice | bytes 3670016 | tf_op jit(solution)/shard_map/slice | solution.py:387
  10.5 2.2 %collective-permute-start.2 = (bf16[7,256,512]{2,1,0:T(8,128)(2,1)}, bf16[7,256,512]{2,1,0:T(8,128)(2,1)S(1)}, u32[]{:S(2)}, u32[]{:S(2)}) collective-permute-start(bf16[7,256,512]{2,1,0:T(8,128)(2,1)} %slice.13), channel_id=1, source_target_pairs={{2,0},{4,2},{6,4},{8,6},{10,8},{12,10},{14,12},{16,14},{18,16},{20... | collective-permute-start | bytes 5505032 | tf_op jit(solution)/shard_map/ppermute | solution.py:23
  12.7 0.1 copy.9
  12.8 0.7 reshape.7.bonds_ref
  13.5 0.7 pad_add_fusion.places
  14.2 49.8 %sweep.1 = (bf16[6,4,512,512]{3,2,1,0:T(8,128)(2,1)}, bf16[7,4,512,512]{3,2,1,0:T(8,128)(2,1)}, bf16[1,4,512,512]{3,2,1,0:T(8,128)(2,1)}, f32[8,128]{1,0:T(8,128...) custom-call(s32[2]{0:T(128)} %pad_add_fusion.places, bf16[28,28]{1,0:T(8,128)(2,1)} %reshape.7.bonds_ref, ...), custom_call_target="tpu_custom_call" | custom-call | flops 37580963840 | bytes 29360128 | tf_op jit(solution)/shard_map/sweep/pallas_call | solution.py:223
  64.0 0.6 collective-permute-start.7
  64.7 0.1 collective-permute-start.4
  64.8 8.1 %collective-permute-done.4.refs_1_ = bf16[6,256,512]{2,1,0:T(8,128)(2,1)S(1)} collective-permute-done((bf16[6,256,512]{2,1,0:T(8,128)(2,1)S(1)}, bf16[6,256,512]{2,1,0:T(8,128)(2,1)S(1)}, u32[]{:S(2)}, u32[]{:S(2)}) %collective-permute-start.4) | collective-permute-done | bytes 1572896 | tf_op jit(solution)/shard_map/ppermute | solution.py:27
  72.8 10.4 %applied_part.3 = (f32[4,512,512]{2,1,0:T(8,128)S(1)}, f32[8,128]{1,0:T(8,128)S(1)}) custom-call(s32[2]{0:T(128)S(1)} %copy-done.1, bf16[6,4,512,512]{3,2,1,0:T(8,128)(2,1)} %get-tuple-element.15.through_in, bf16[6,256,512]{2,1,0:T(8,128)(2,1)S(1)} %after.3.refs_0_, bf16[6,256,512]{2,1,0:T(8,128)(2,1)S(1)} %collective-permute-done.4.refs_1_), custom_call_target="tpu_custom_call" | custom-call | tf_op jit(solution)/shard_map/applied_part/pallas_call | solution.py:350
  83.2 0.3 collective-permute-done.2.refs_0_
  83.5 0.8 collective-permute-start.5
  84.3 1.0 slice.12
  85.3 4.0 %collective-permute-start.1 = (bf16[1,256,512]{2,1,0:T(8,128)(2,1)S(1)}, bf16[1,256,512]{2,1,0:T(8,128)(2,1)S(1)}, u32[]{:S(2)}, u32[]{:S(2)}) collective-permute-start(bf16[1,256,512]{2,1,0:T(8,128)(2,1)S(1)} %slice.12), channel_id=1, source_target_pairs={{2,0},{4,2},{6,4},{8,6},{10,8},{12,10},{14,12},{16,14},{18,16},{20... | collective-permute-start | bytes 786440 | tf_op jit(solution)/shard_map/ppermute | solution.py:23
  89.3 0.0 copy-start.3
  89.3 11.8 %applied_part.4 = (f32[4,512,512]{2,1,0:T(8,128)S(1)}, f32[8,128]{1,0:T(8,128)S(1)}) custom-call(s32[2]{0:T(128)S(1)} %copy-done.1, bf16[7,4,512,512]{3,2,1,0:T(8,128)(2,1)} %get-tuple-element.14.through_in, bf16[7,256,512]{2,1,0:T(8,128)(2,1)S(1)} %after.4.refs_0_, bf16[7,256,512]{2,1,0:T(8,128)(2,1)S(1)} %collective-permute-done.5.refs_1_, ...), custom_call_target="tpu_custom_call" | custom-call | tf_op jit(solution)/shard_map/applied_part/pallas_call | solution.py:350
  101.1 0.3 collective-permute-start.6
  101.5 3.0 %fusion = bf16[1,256,14,512]{3,1,2,0:T(8,128)(2,1)} fusion(bf16[14,256,512]{2,1,0:T(8,128)(2,1)S(1)} %collective-permute-done.7, bf16[14,256,512]{2,1,0:T(8,128)(2,1)S(1)} %copy-done.3), kind=kLoop, calls=%fused_computation.1 | loop fusion | flops 7340032 | bytes 11010048 | tf_op jit(solution)/shard_map/broadcast_in_dim | solution.py:417
  104.5 4.3 %applied_part.5 = (bf16[4,256,2,512]{3,2,1,0:T(2,128)(2,1)}, f32[8,128]{1,0:T(8,128)}) custom-call(s32[2]{0:T(128)S(1)} %copy-done.1, bf16[1,4,512,512]{3,2,1,0:T(8,128)(2,1)S(1)} %copy-done, bf16[1,256,512]{2,1,0:T(8,128)(2,1)S(1)} %after.5.refs_0_, bf16[1,256,512]{2,1,0:T(8,128)(2,1)S(1)} %collective-permute-done.6.refs_1_, ...), custom_call_target="tpu_custom_call" | custom-call | tf_op jit(solution)/shard_map/applied_part/pallas_call | solution.py:350
  (17 shorter events, 0.0 us)
Async XLA Ops:
  0.6 4.1 %copy-start.2 = (bf16[1,256,14,512]{3,1,2,0:T(8,128)(2,1)S(1)}, bf16[1,256,14,512]{3,1,2,0:T(8,128)(2,1)}, u32[]{:S(2)}) copy-start(bf16[1,256,14,512]{3,1,2,0:T(8,128)(2,1)} %param.5) | copy-start | bytes 11010052
  4.1 8.6 %copy-start.4 = (bf16[14,2,2,14]{3,2,1,0:T(2,128)(2,1)S(1)}, bf16[14,2,2,14]{3,2,1,0:T(2,128)(2,1)}, u32[]{:S(2)}) copy-start(bf16[14,2,2,14]{3,2,1,0:T(2,128)(2,1)} %param.7) | copy-start | bytes 4708
  4.1 10.1 %collective-permute-start = (bf16[4,2,256,512]{3,2,1,0:T(8,128)(2,1)}, bf16[4,2,256,512]{3,2,1,0:T(8,128)(2,1)}, u32[]{:S(2)}, u32[]{:S(2)}) collective-permute-start(bf16[4,2,256,512]{3,2,1,0:T(8,128)(2,1)} %bitcast.18.refs_0_), channel_id=1, source_target_pairs={{0,1},{1,0},{2,3},{3,2},{4,5},{5,4},{6,7},{7,6},{8,9},{9,8},{10,11... | collective-permute-start | bytes 6291464 | tf_op jit(solution)/shard_map/ppermute | solution.py:27
  6.1 58.6 %collective-permute-start.3 = (bf16[6,256,512]{2,1,0:T(8,128)(2,1)}, bf16[6,256,512]{2,1,0:T(8,128)(2,1)S(1)}, u32[]{:S(2)}, u32[]{:S(2)}) collective-permute-start(bf16[6,256,512]{2,1,0:T(8,128)(2,1)} %slice.14), channel_id=1, source_target_pairs={{2,0},{4,2},{6,4},{8,6},{10,8},{12,10},{14,12},{16,14},{18,16},{20... | collective-permute-start | bytes 4718600 | tf_op jit(solution)/shard_map/ppermute | solution.py:23
  10.5 73.0 %collective-permute-start.2 = (bf16[7,256,512]{2,1,0:T(8,128)(2,1)}, bf16[7,256,512]{2,1,0:T(8,128)(2,1)S(1)}, u32[]{:S(2)}, u32[]{:S(2)}) collective-permute-start(bf16[7,256,512]{2,1,0:T(8,128)(2,1)} %slice.13), channel_id=1, source_target_pairs={{2,0},{4,2},{6,4},{8,6},{10,8},{12,10},{14,12},{16,14},{18,16},{20... | collective-permute-start | bytes 5505032 | tf_op jit(solution)/shard_map/ppermute | solution.py:23
  14.2 58.7 %copy-start.1 = (s32[2]{0:T(128)S(1)}, s32[2]{0:T(128)}, u32[]{:S(2)}) copy-start(s32[2]{0:T(128)} %pad_add_fusion.places) | copy-start | bytes 28
  64.0 37.4 %collective-permute-start.7 = (bf16[14,256,512]{2,1,0:T(8,128)(2,1)}, bf16[14,256,512]{2,1,0:T(8,128)(2,1)S(1)}, u32[]{:S(2)}, u32[]{:S(2)}) collective-permute-start(bf16[14,256,512]{2,1,0:T(8,128)(2,1)} %get-tuple-element.23), channel_id=1, source_target_pairs={{0,1},{1,0},{2,3},{3,2},{4,5},{5,4},{6,7},{7,6},{8,9},{9,8},{10,11... | collective-permute-start | bytes 11010056 | tf_op jit(solution)/shard_map/ppermute | solution.py:27
  64.7 8.1 %collective-permute-start.4 = (bf16[6,256,512]{2,1,0:T(8,128)(2,1)S(1)}, bf16[6,256,512]{2,1,0:T(8,128)(2,1)S(1)}, u32[]{:S(2)}, u32[]{:S(2)}) collective-permute-start(bf16[6,256,512]{2,1,0:T(8,128)(2,1)S(1)} %after.3.refs_0_), channel_id=1, source_target_pairs={{0,1},{1,0},{2,3},{3,2},{4,5},{5,4},{6,7},{7,6},{8,9},{9,8},{10,11... | collective-permute-start | bytes 4718600 | tf_op jit(solution)/shard_map/ppermute | solution.py:27
  83.5 5.7 %collective-permute-start.5 = (bf16[7,256,512]{2,1,0:T(8,128)(2,1)S(1)}, bf16[7,256,512]{2,1,0:T(8,128)(2,1)S(1)}, u32[]{:S(2)}, u32[]{:S(2)}) collective-permute-start(bf16[7,256,512]{2,1,0:T(8,128)(2,1)S(1)} %after.4.refs_0_), channel_id=1, source_target_pairs={{0,1},{1,0},{2,3},{3,2},{4,5},{5,4},{6,7},{7,6},{8,9},{9,8},{10,11... | collective-permute-start | bytes 5505032 | tf_op jit(solution)/shard_map/ppermute | solution.py:27
  85.3 15.8 %collective-permute-start.1 = (bf16[1,256,512]{2,1,0:T(8,128)(2,1)S(1)}, bf16[1,256,512]{2,1,0:T(8,128)(2,1)S(1)}, u32[]{:S(2)}, u32[]{:S(2)}) collective-permute-start(bf16[1,256,512]{2,1,0:T(8,128)(2,1)S(1)} %slice.12), channel_id=1, source_target_pairs={{2,0},{4,2},{6,4},{8,6},{10,8},{12,10},{14,12},{16,14},{18,16},{20... | collective-permute-start | bytes 786440 | tf_op jit(solution)/shard_map/ppermute | solution.py:23
  89.3 12.2 %copy-start.3 = (bf16[14,256,512]{2,1,0:T(8,128)(2,1)S(1)}, bf16[14,256,512]{2,1,0:T(8,128)(2,1)}, u32[]{:S(2)}) copy-start(bf16[14,256,512]{2,1,0:T(8,128)(2,1)} %get-tuple-element.22) | copy-start | bytes 11010052
  101.1 3.4 %collective-permute-start.6 = (bf16[1,256,512]{2,1,0:T(8,128)(2,1)S(1)}, bf16[1,256,512]{2,1,0:T(8,128)(2,1)S(1)}, u32[]{:S(2)}, u32[]{:S(2)}) collective-permute-start(bf16[1,256,512]{2,1,0:T(8,128)(2,1)S(1)} %after.5.refs_0_), channel_id=1, source_target_pairs={{0,1},{1,0},{2,3},{3,2},{4,5},{5,4},{6,7},{7,6},{8,9},{9,8},{10,11... | collective-permute-start | bytes 786440 | tf_op jit(solution)/shard_map/ppermute | solution.py:27
  101.5 3.0 %copy-start = (bf16[1,4,512,512]{3,2,1,0:T(8,128)(2,1)S(1)}, bf16[1,4,512,512]{3,2,1,0:T(8,128)(2,1)}, u32[]{:S(2)}) copy-start(bf16[1,4,512,512]{3,2,1,0:T(8,128)(2,1)} %get-tuple-element.13.through_in) | copy-start | bytes 6291460

commit v7 on v6

--- a/solution.py
+++ b/solution.py
@@ -74,8 +74,8 @@
     )
 
 
-def sweep_kernel(parts, pieces, scaling, places, bonds_ref, env_hbm, here_hbm, *refs):
-    waves_hbm, refs = refs[:parts], refs[parts:]
+def sweep_kernel(parts, turns, pieces, scaling, places, bonds_ref, env_hbm, here_hbm, *refs):
+    waves_hbm, refs = refs[: parts * turns], refs[parts * turns :]
     throughs_hbm, refs = refs[:pieces], refs[pieces:]
     token_ref, refs = refs[0], refs[1:]
     outs, refs = refs[:parts], refs[parts:]
@@ -93,14 +93,25 @@
         here = pl.ds(pl.multiple_of(i * rows, rows), rows)
         return pltpu.make_async_copy(env_hbm.at[:, here], env_ref.at[:, here], env_sems.at[i])
 
+    def wave_starts(k):
+        turn, inside = divmod(k, waves_hbm[0].shape[0])
+        return [
+            pltpu.make_async_copy(
+                waves_hbm[turn * parts + index].at[inside],
+                wave_ref.at[k, :, pl.ds(index * width, width)],
+                wave_sems.at[k, index],
+            )
+            for index in range(parts)
+        ]
+
     def wave_copies(k):
         return [
             pltpu.make_async_copy(
-                wave.at[k],
+                waves_hbm[index].at[0],
                 wave_ref.at[k, :, pl.ds(index * width, width)],
                 wave_sems.at[k, index],
             )
-            for index, wave in enumerate(waves_hbm)
+            for index in range(parts)
         ]
 
     def through_copies(i):
@@ -123,7 +134,7 @@
         if n < blocks:
             env_copy(n).start()
         if n < num_states:
-            for copy in wave_copies(n):
+            for copy in wave_starts(n):
                 copy.start()
     here_copy.start()
 
@@ -214,15 +225,16 @@
 
 def sweep(bonds, env, here, waves, places, counts, scaling):
     mw, rows_all, chi_in = env.shape
-    num_states, phys, _, chi = waves[0].shape
+    phys, _, chi = waves[0][0].shape[1:]
+    num_states = here.shape[1]
     rows = min(64, rows_all)
-    parts = len(waves)
+    parts = len(waves[0])
     padded = -(-mw * phys * GROUP // 128) * 128
     bf16 = jnp.bfloat16
     share = jax.ShapeDtypeStruct((mw, chi // parts, chi), bf16)
     out = pl.pallas_call(
-        functools.partial(sweep_kernel, parts, len(counts), scaling),
-        in_specs=[SCALARS, WHOLE] + [ANY] * (2 + parts),
+        functools.partial(sweep_kernel, parts, len(waves), len(counts), scaling),
+        in_specs=[SCALARS, WHOLE] + [ANY] * (2 + parts * len(waves)),
         out_specs=[ANY] * len(counts) + [WHOLE] + [ANY] * parts,
         scratch_shapes=[
             pltpu.VMEM(env.shape, bf16),
@@ -247,12 +259,12 @@
         + [share] * parts,
         compiler_params=pltpu.CompilerParams(vmem_limit_bytes=SWEEP_MIB * MIB),
         cost_estimate=pl.CostEstimate(
-            flops=5 * mw * rows_all * chi_in * num_states * phys * chi,
-            bytes_accessed=2 * mw * num_states * rows_all * phys * chi,
+            flops=0,
+            bytes_accessed=0,
             transcendentals=0,
         ),
         name="sweep",
-    )(places, bonds, env, here, *waves)
+    )(places, bonds, env, here, *[wave for turn in waves for wave in turn])
     pieces = len(counts)
     return out[:pieces], out[pieces], out[pieces + 1 :]
 
@@ -284,20 +296,30 @@
         for k in range(num_states):
             for copy in through_copies(k):
                 copy.start()
-    v = 0
-    for piece in range(pieces):
-        blocks = rights[piece * parts : (piece + 1) * parts]
-        for n in range(blocks[0].shape[0]):
-            right = jnp.concatenate([block[n] for block in blocks], axis=0)
-            turned[v * chi : (v + 1) * chi, :] = right.T
-            v += 1
+    def turn(v):
+        for piece in range(pieces):
+            blocks = rights[piece * parts : (piece + 1) * parts]
+            n = v - sum(rights[before * parts].shape[0] for before in range(piece))
+            if 0 <= n < blocks[0].shape[0]:
+                right = jnp.concatenate([block[n] for block in blocks], axis=0)
+                turned[v * chi : (v + 1) * chi, :] = right.T
 
     def state(k, _):
         if not close:
             for copy in through_copies(k):
                 copy.wait()
-        left = jnp.concatenate([through_ref[v, k] for v in range(count)], axis=1)
-        total = product(left, turned[...], ((1,), (0,)))
+        if isinstance(k, int) and k == 0:
+            total = None
+            for v in range(0, count, 2):
+                most = min(v + 2, count)
+                for n in range(v, most):
+                    turn(n)
+                left = jnp.concatenate([through_ref[n, k] for n in range(v, most)], axis=1)
+                term = product(left, turned[v * chi : most * chi, :], ((1,), (0,)))
+                total = term if total is None else total + term
+        else:
+            left = jnp.concatenate([through_ref[v, k] for v in range(count)], axis=1)
+            total = product(left, turned[...], ((1,), (0,)))
         if begun:
             total = total + held[k]
         if not last:
@@ -311,15 +333,18 @@
             total = own_first(swap, total[:, : columns // 2], total[:, columns // 2 :], 1)
         slot = k % 2
 
-        @pl.when(k >= 2)
-        def _():
+        if k >= 2:
             out_copy(k - 2, slot).wait()
-
         results[slot] = total.reshape(rows // phys, phys, columns)
         out_copy(k, slot).start()
         return 0
 
-    lax.fori_loop(0, num_states, state, 0)
+    state(0, 0)
+    if last:
+        for k in range(1, num_states):
+            state(k, 0)
+    else:
+        lax.fori_loop(1, num_states, state, 0)
     if last:
         for k in range(max(num_states - 2, 0), num_states):
             out_copy(k, k % 2).wait()
@@ -388,11 +413,14 @@
             pieces[-1].append(piece)
             first += count
 
-    wave_split = states[0].transpose(0, 2, 1, 3)
-    if paired:
-        waves = [wave_split, swapped(wave_split, "bond")]
-    else:
-        waves = [lax.all_gather(wave_split, "bond", axis=2, tiled=True)]
+    half = max(num_states // 2, 1)
+    waves = []
+    for start in range(0, num_states, half):
+        wave = states[0, start : start + half].transpose(0, 2, 1, 3)
+        if paired:
+            waves.append([wave, swapped(wave, "bond")])
+        else:
+            waves.append([lax.all_gather(wave, "bond", axis=2, tiled=True)])
     bond_table = mpo.transpose(3, 1, 2, 0).reshape(mw * phys, phys * mw)
     counts = [sum(stage) for stage in stages]
     throughs, token, shares = sweep(bond_table, left, states, waves, places, counts, scaling)

time: 111 us -> 110 us (level); the launches traced: 109 us -> 110 us
  local copies, waits for them, and re-layouts: 7.94 us -> 9.94 us
  Pallas kernels: 76.3 us -> 75 us
    slice x3, local copies, waits for them, and re-layouts: 3.67 us -> 5.24 us  [on_device(): piece = passed_along(right[first:first + count], 'seg', -1)]
    slice x0 -> x1, local copies, waits for them, and re-layouts: none -> 1.49 us  [on_device(): wave = states[0, start:start + half].transpose(0, 2, 1, 3)]
    pallas_call x3, Pallas kernels: 26.4 us -> 25.2 us  [applied_part(): pl.pallas_call(functools.partial(applied_kernel, parts, len(rights), begu...]
    unnamed x11 -> x14, local copies, waits for them, and re-layouts: 3.46 us -> 2.4 us
    ppermute x5 -> x6, starting transfers between devices: 2.54 us -> 2.83 us  [swapped(): return lax.ppermute(array, axis, [(0, 1), (1, 0)])]
    ppermute x5 -> x6, waiting for transfers between devices: 8.07 us -> 8.07 us  [swapped(): return lax.ppermute(array, axis, [(0, 1), (1, 0)])]
  transfers between devices with their start and end apart: 8 -> 9, of which waited for: 2 -> 1; matrix products, arithmetic and copies ran while one was open for 7% -> 10% of each run, Pallas kernels for 66% -> 65%
where the time goes in v7:
time: 110 us
  Pallas kernels  75 us (68%)
  starting transfers between devices  12.4 us (11%)
  local copies, waits for them, and re-layouts  9.94 us (9%)
  waiting for transfers between devices  8.08 us (7%)
  other arithmetic  3.68 us (3%)
    pallas_call x1, Pallas kernels, sweep(): pl.pallas_call(functools.partial(sweep_kernel, parts, len(waves), len(cou...  49.8 us
    pallas_call x3, Pallas kernels, applied_part(): pl.pallas_call(functools.partial(applied_kernel, parts, len(rights), begu...  25.2 us
    ppermute x3, starting transfers between devices, passed_along(): return lax.ppermute(array, axis, pairs)  9.61 us
    ppermute x6, waiting for transfers between devices, swapped(): return lax.ppermute(array, axis, [(0, 1), (1, 0)])  8.07 us
    slice x3, local copies, waits for them, and re-layouts, on_device(): piece = passed_along(right[first:first + count], 'seg', -1)  5.24 us
    broadcast_in_dim x1, other arithmetic, on_device(): return (held[None], new_env.transpose(1, 0, 2)[None])  3.02 us
    ppermute x6, starting transfers between devices, swapped(): return lax.ppermute(array, axis, [(0, 1), (1, 0)])  2.83 us
    unnamed x14, local copies, waits for them, and re-layouts  2.4 us
  transfers between devices with their start and end apart: 9, of which 1 were waited for; matrix products, arithmetic and copies ran while one was open for 10% of the time, Pallas kernels for 65%

profile of v7, /device:TPU:13, one launch (start us, length us, event | category | flops | bytes accessed | tf_op | source)
XLA Modules:
  0.0 110.1 jit_solution(4059004785956946133)
XLA Ops:
  0.6 2.9 %slice.22 = bf16[6,256,512]{2,1,0:T(8,128)(2,1)} slice(bf16[14,256,512]{2,1,0:T(8,128)(2,1)} %bitcast.24), slice={[0:6], [0:256], [0:512]} | slice | bytes 3145728 | tf_op jit(solution)/shard_map/slice | solution.py:412
  3.5 3.3 %collective-permute-start.4 = (bf16[6,256,512]{2,1,0:T(8,128)(2,1)}, bf16[6,256,512]{2,1,0:T(8,128)(2,1)S(1)}, u32[]{:S(2)}, u32[]{:S(2)}) collective-permute-start(bf16[6,256,512]{2,1,0:T(8,128)(2,1)} %slice.22), channel_id=1, source_target_pairs={{2,0},{4,2},{6,4},{8,6},{10,8},{12,10},{14,12},{16,14},{18,16},{20... | collective-permute-start | bytes 4718600 | tf_op jit(solution)/shard_map/ppermute | solution.py:23
  6.9 1.5 %fusion.1 = (bf16[1,2,256,2,512]{4,3,2,1,0:T(2,128)(2,1)S(1)}, bf16[1,2,256,2,512]{4,3,2,1,0:T(2,128)(2,1)S(1)}) fusion(bf16[1,4,256,2,512]{4,3,2,1,0:T(2,128)(2,1)S(1)} %copy-done.2), kind=kLoop, calls=%fused_computation.5 | loop fusion | bytes 4194304 | tf_op jit(solution)/shard_map/slice | solution.py:419
  8.4 0.0 copy-start.5
  8.4 1.2 %copy.17 = bf16[1,2,256,2,512]{4,2,3,1,0:T(8,128)(2,1)} copy(bf16[1,2,256,2,512]{4,3,2,1,0:T(2,128)(2,1)S(1)} %get-tuple-element.25) | data formatting | bytes 2097152
  9.6 1.0 collective-permute-start
  10.5 1.2 %copy.16 = bf16[1,2,256,2,512]{4,2,3,1,0:T(8,128)(2,1)} copy(bf16[1,2,256,2,512]{4,3,2,1,0:T(2,128)(2,1)S(1)} %get-tuple-element.24) | data formatting | bytes 2097152
  11.7 1.4 %slice.21 = bf16[7,256,512]{2,1,0:T(8,128)(2,1)} slice(bf16[14,256,512]{2,1,0:T(8,128)(2,1)S(1)} %bitcast.26), slice={[6:13], [0:256], [0:512]} | slice | bytes 3670016 | tf_op jit(solution)/shard_map/slice | solution.py:412
  13.1 2.2 %collective-permute-start.3 = (bf16[7,256,512]{2,1,0:T(8,128)(2,1)}, bf16[7,256,512]{2,1,0:T(8,128)(2,1)S(1)}, u32[]{:S(2)}, u32[]{:S(2)}) collective-permute-start(bf16[7,256,512]{2,1,0:T(8,128)(2,1)} %slice.21), channel_id=1, source_target_pairs={{2,0},{4,2},{6,4},{8,6},{10,8},{12,10},{14,12},{16,14},{18,16},{20... | collective-permute-start | bytes 5505032 | tf_op jit(solution)/shard_map/ppermute | solution.py:23
  15.3 0.7 pad_add_fusion.places
  15.9 0.1 copy.9
  16.0 0.7 reshape.7.bonds_ref
  16.7 49.8 %sweep.1 = (bf16[6,4,512,512]{3,2,1,0:T(8,128)(2,1)}, bf16[7,4,512,512]{3,2,1,0:T(8,128)(2,1)}, bf16[1,4,512,512]{3,2,1,0:T(8,128)(2,1)}, f32[8,128]{1,0:T(8,128...) custom-call(s32[2]{0:T(128)} %pad_add_fusion.places, bf16[28,28]{1,0:T(8,128)(2,1)} %reshape.7.bonds_ref, ...), custom_call_target="tpu_custom_call" | custom-call | tf_op jit(solution)/shard_map/sweep/pallas_call | solution.py:235
  66.5 0.9 collective-permute-start.8
  67.4 0.1 collective-permute-start.5
  67.5 8.1 %collective-permute-done.5.refs_1_ = bf16[6,256,512]{2,1,0:T(8,128)(2,1)S(1)} collective-permute-done((bf16[6,256,512]{2,1,0:T(8,128)(2,1)S(1)}, bf16[6,256,512]{2,1,0:T(8,128)(2,1)S(1)}, u32[]{:S(2)}, u32[]{:S(2)}) %collective-permute-start.5) | collective-permute-done | bytes 1572896 | tf_op jit(solution)/shard_map/ppermute | solution.py:27
  75.6 9.8 %applied_part.3 = (f32[4,512,512]{2,1,0:T(8,128)S(1)}, f32[8,128]{1,0:T(8,128)S(1)}) custom-call(s32[2]{0:T(128)S(1)} %copy-done.1, bf16[6,4,512,512]{3,2,1,0:T(8,128)(2,1)} %get-tuple-element.15.through_in, bf16[6,256,512]{2,1,0:T(8,128)(2,1)S(1)} %after.3.refs_0_, bf16[6,256,512]{2,1,0:T(8,128)(2,1)S(1)} %collective-permute-done.5.refs_1_), custom_call_target="tpu_custom_call" | custom-call | tf_op jit(solution)/shard_map/applied_part/pallas_call | solution.py:375
  85.4 0.2 collective-permute-start.6
  85.6 1.0 slice.20
  86.6 4.1 %collective-permute-start.2 = (bf16[1,256,512]{2,1,0:T(8,128)(2,1)S(1)}, bf16[1,256,512]{2,1,0:T(8,128)(2,1)S(1)}, u32[]{:S(2)}, u32[]{:S(2)}) collective-permute-start(bf16[1,256,512]{2,1,0:T(8,128)(2,1)S(1)} %slice.20), channel_id=1, source_target_pairs={{2,0},{4,2},{6,4},{8,6},{10,8},{12,10},{14,12},{16,14},{18,16},{20... | collective-permute-start | bytes 786440 | tf_op jit(solution)/shard_map/ppermute | solution.py:23
  90.8 11.4 %applied_part.4 = (f32[4,512,512]{2,1,0:T(8,128)S(1)}, f32[8,128]{1,0:T(8,128)S(1)}) custom-call(s32[2]{0:T(128)S(1)} %copy-done.1, bf16[7,4,512,512]{3,2,1,0:T(8,128)(2,1)} %get-tuple-element.14.through_in, bf16[7,256,512]{2,1,0:T(8,128)(2,1)S(1)} %after.4.refs_0_, bf16[7,256,512]{2,1,0:T(8,128)(2,1)S(1)} %collective-permute-done.6.refs_1_, ...), custom_call_target="tpu_custom_call" | custom-call | tf_op jit(solution)/shard_map/applied_part/pallas_call | solution.py:375
  102.2 0.7 collective-permute-start.7
  102.9 3.0 %fusion = bf16[1,256,14,512]{3,1,2,0:T(8,128)(2,1)} fusion(bf16[14,256,512]{2,1,0:T(8,128)(2,1)S(1)} %collective-permute-done.8, bf16[14,256,512]{2,1,0:T(8,128)(2,1)S(1)} %copy-done.4), kind=kLoop, calls=%fused_computation.1 | loop fusion | flops 7340032 | bytes 11010048 | tf_op jit(solution)/shard_map/broadcast_in_dim | solution.py:445
  105.9 4.0 %applied_part.5 = (bf16[4,256,2,512]{3,2,1,0:T(2,128)(2,1)}, f32[8,128]{1,0:T(8,128)}) custom-call(s32[2]{0:T(128)S(1)} %copy-done.1, bf16[1,4,512,512]{3,2,1,0:T(8,128)(2,1)S(1)} %copy-done, bf16[1,256,512]{2,1,0:T(8,128)(2,1)S(1)} %after.5.refs_0_, bf16[1,256,512]{2,1,0:T(8,128)(2,1)S(1)} %collective-permute-done.7.refs_1_, ...), custom_call_target="tpu_custom_call" | custom-call | tf_op jit(solution)/shard_map/applied_part/pallas_call | solution.py:375
  (23 shorter events, 0.1 us)
Async XLA Ops:
  0.6 6.2 %copy-start.2 = (bf16[1,4,256,2,512]{4,3,2,1,0:T(2,128)(2,1)S(1)}, bf16[1,4,256,2,512]{4,3,2,1,0:T(2,128)(2,1)}, u32[]{:S(2)}) copy-start(bf16[1,4,256,2,512]{4,3,2,1,0:T(2,128)(2,1)} %here_hbm.1) | copy-start | bytes 6291460
  3.5 8.2 %copy-start.3 = (bf16[1,256,14,512]{3,1,2,0:T(8,128)(2,1)S(1)}, bf16[1,256,14,512]{3,1,2,0:T(8,128)(2,1)}, u32[]{:S(2)}) copy-start(bf16[1,256,14,512]{3,1,2,0:T(8,128)(2,1)} %param.5) | copy-start | bytes 11010052
  3.5 63.9 %collective-permute-start.4 = (bf16[6,256,512]{2,1,0:T(8,128)(2,1)}, bf16[6,256,512]{2,1,0:T(8,128)(2,1)S(1)}, u32[]{:S(2)}, u32[]{:S(2)}) collective-permute-start(bf16[6,256,512]{2,1,0:T(8,128)(2,1)} %slice.22), channel_id=1, source_target_pairs={{2,0},{4,2},{6,4},{8,6},{10,8},{12,10},{14,12},{16,14},{18,16},{20... | collective-permute-start | bytes 4718600 | tf_op jit(solution)/shard_map/ppermute | solution.py:23
  8.4 7.6 %copy-start.5 = (bf16[14,2,2,14]{3,2,1,0:T(2,128)(2,1)S(1)}, bf16[14,2,2,14]{3,2,1,0:T(2,128)(2,1)}, u32[]{:S(2)}) copy-start(bf16[14,2,2,14]{3,2,1,0:T(2,128)(2,1)} %param.7) | copy-start | bytes 4708
  9.6 7.2 %collective-permute-start = (bf16[2,2,256,512]{3,2,1,0:T(8,128)(2,1)}, bf16[2,2,256,512]{3,2,1,0:T(8,128)(2,1)}, u32[]{:S(2)}, u32[]{:S(2)}) collective-permute-start(bf16[2,2,256,512]{3,2,1,0:T(8,128)(2,1)} %bitcast.23.refs_0_), channel_id=1, source_target_pairs={{0,1},{1,0},{2,3},{3,2},{4,5},{5,4},{6,7},{7,6},{8,9},{9,8},{10,11... | collective-permute-start | bytes 3145736 | tf_op jit(solution)/shard_map/ppermute | solution.py:27
  11.7 5.0 %collective-permute-start.1 = (bf16[2,2,256,512]{3,2,1,0:T(8,128)(2,1)}, bf16[2,2,256,512]{3,2,1,0:T(8,128)(2,1)}, u32[]{:S(2)}, u32[]{:S(2)}) collective-permute-start(bf16[2,2,256,512]{3,2,1,0:T(8,128)(2,1)} %bitcast.22.refs_2_), channel_id=1, source_target_pairs={{0,1},{1,0},{2,3},{3,2},{4,5},{5,4},{6,7},{7,6},{8,9},{9,8},{10,11... | collective-permute-start | bytes 3145736 | tf_op jit(solution)/shard_map/ppermute | solution.py:27
  13.1 72.3 %collective-permute-start.3 = (bf16[7,256,512]{2,1,0:T(8,128)(2,1)}, bf16[7,256,512]{2,1,0:T(8,128)(2,1)S(1)}, u32[]{:S(2)}, u32[]{:S(2)}) collective-permute-start(bf16[7,256,512]{2,1,0:T(8,128)(2,1)} %slice.21), channel_id=1, source_target_pairs={{2,0},{4,2},{6,4},{8,6},{10,8},{12,10},{14,12},{16,14},{18,16},{20... | collective-permute-start | bytes 5505032 | tf_op jit(solution)/shard_map/ppermute | solution.py:23
  16.7 58.8 %copy-start.1 = (s32[2]{0:T(128)S(1)}, s32[2]{0:T(128)}, u32[]{:S(2)}) copy-start(s32[2]{0:T(128)} %pad_add_fusion.places) | copy-start | bytes 28
  66.5 36.4 %collective-permute-start.8 = (bf16[14,256,512]{2,1,0:T(8,128)(2,1)}, bf16[14,256,512]{2,1,0:T(8,128)(2,1)S(1)}, u32[]{:S(2)}, u32[]{:S(2)}) collective-permute-start(bf16[14,256,512]{2,1,0:T(8,128)(2,1)} %get-tuple-element.23), channel_id=1, source_target_pairs={{0,1},{1,0},{2,3},{3,2},{4,5},{5,4},{6,7},{7,6},{8,9},{9,8},{10,11... | collective-permute-start | bytes 11010056 | tf_op jit(solution)/shard_map/ppermute | solution.py:27
  67.4 8.1 %collective-permute-start.5 = (bf16[6,256,512]{2,1,0:T(8,128)(2,1)S(1)}, bf16[6,256,512]{2,1,0:T(8,128)(2,1)S(1)}, u32[]{:S(2)}, u32[]{:S(2)}) collective-permute-start(bf16[6,256,512]{2,1,0:T(8,128)(2,1)S(1)} %after.3.refs_0_), channel_id=1, source_target_pairs={{0,1},{1,0},{2,3},{3,2},{4,5},{5,4},{6,7},{7,6},{8,9},{9,8},{10,11... | collective-permute-start | bytes 4718600 | tf_op jit(solution)/shard_map/ppermute | solution.py:27
  85.4 5.3 %collective-permute-start.6 = (bf16[7,256,512]{2,1,0:T(8,128)(2,1)S(1)}, bf16[7,256,512]{2,1,0:T(8,128)(2,1)S(1)}, u32[]{:S(2)}, u32[]{:S(2)}) collective-permute-start(bf16[7,256,512]{2,1,0:T(8,128)(2,1)S(1)} %after.4.refs_0_), channel_id=1, source_target_pairs={{0,1},{1,0},{2,3},{3,2},{4,5},{5,4},{6,7},{7,6},{8,9},{9,8},{10,11... | collective-permute-start | bytes 5505032 | tf_op jit(solution)/shard_map/ppermute | solution.py:27
  86.6 15.6 %collective-permute-start.2 = (bf16[1,256,512]{2,1,0:T(8,128)(2,1)S(1)}, bf16[1,256,512]{2,1,0:T(8,128)(2,1)S(1)}, u32[]{:S(2)}, u32[]{:S(2)}) collective-permute-start(bf16[1,256,512]{2,1,0:T(8,128)(2,1)S(1)} %slice.20), channel_id=1, source_target_pairs={{2,0},{4,2},{6,4},{8,6},{10,8},{12,10},{14,12},{16,14},{18,16},{20... | collective-permute-start | bytes 786440 | tf_op jit(solution)/shard_map/ppermute | solution.py:23
  90.8 12.2 %copy-start.4 = (bf16[14,256,512]{2,1,0:T(8,128)(2,1)S(1)}, bf16[14,256,512]{2,1,0:T(8,128)(2,1)}, u32[]{:S(2)}) copy-start(bf16[14,256,512]{2,1,0:T(8,128)(2,1)} %get-tuple-element.22) | copy-start | bytes 11010052
  102.2 3.7 %collective-permute-start.7 = (bf16[1,256,512]{2,1,0:T(8,128)(2,1)S(1)}, bf16[1,256,512]{2,1,0:T(8,128)(2,1)S(1)}, u32[]{:S(2)}, u32[]{:S(2)}) collective-permute-start(bf16[1,256,512]{2,1,0:T(8,128)(2,1)S(1)} %after.5.refs_0_), channel_id=1, source_target_pairs={{0,1},{1,0},{2,3},{3,2},{4,5},{5,4},{6,7},{7,6},{8,9},{9,8},{10,11... | collective-permute-start | bytes 786440 | tf_op jit(solution)/shard_map/ppermute | solution.py:27
  102.9 3.0 %copy-start = (bf16[1,4,512,512]{3,2,1,0:T(8,128)(2,1)S(1)}, bf16[1,4,512,512]{3,2,1,0:T(8,128)(2,1)}, u32[]{:S(2)}) copy-start(bf16[1,4,512,512]{3,2,1,0:T(8,128)(2,1)} %get-tuple-element.13.through_in) | copy-start | bytes 6291460

commit v8 on v7

--- a/solution.py
+++ b/solution.py
@@ -14,7 +14,6 @@
 ANY = pl.BlockSpec(memory_space=pl.ANY)
 TOKEN = pltpu.VMEM((8, 128), jnp.float32)
 WHOLE = pl.BlockSpec(memory_space=pltpu.VMEM)
-SCALARS = pl.BlockSpec(memory_space=pltpu.SMEM)
 
 
 def passed_along(array, axis, by):
@@ -49,6 +48,28 @@
         compiler_params=pltpu.CompilerParams(vmem_limit_bytes=MIB),
         name="after",
     )(array, near(token))
+
+
+def cut(array, at, count):
+    def kernel(in_ref, out_ref, sems):
+        copies = [
+            pltpu.make_async_copy(in_ref.at[at + n], out_ref.at[n], sems.at[n])
+            for n in range(count)
+        ]
+        for copy in copies:
+            copy.start()
+        for copy in copies:
+            copy.wait()
+
+    return pl.pallas_call(
+        kernel,
+        in_specs=[ANY],
+        out_specs=ANY,
+        out_shape=jax.ShapeDtypeStruct((count,) + array.shape[1:], array.dtype),
+        scratch_shapes=[pltpu.SemaphoreType.DMA((count,))],
+        compiler_params=pltpu.CompilerParams(vmem_limit_bytes=MIB),
+        name="cut",
+    )(far(array))
 
 
 def block_diagonal(bonds, mw, phys):
@@ -74,7 +95,7 @@
     )
 
 
-def sweep_kernel(parts, turns, pieces, scaling, places, bonds_ref, env_hbm, here_hbm, *refs):
+def sweep_kernel(parts, turns, pieces, scaling, bonds_ref, env_hbm, here_hbm, *refs):
     waves_hbm, refs = refs[: parts * turns], refs[parts * turns :]
     throughs_hbm, refs = refs[:pieces], refs[pieces:]
     token_ref, refs = refs[0], refs[1:]
@@ -143,7 +164,7 @@
     padded = low.shape[1]
     table = jnp.concatenate([table, jnp.zeros((depth, padded - depth), table.dtype)], axis=1)
     low[:, depth:, :] = jnp.zeros((groups, padded - depth, chi), low.dtype)
-    swap = places[0] != 0
+    swap = lax.axis_index("bond") != 0
 
     def block(i, _):
         env_copy(i).wait()
@@ -223,7 +244,7 @@
     token_ref[...] = jnp.zeros_like(token_ref)
 
 
-def sweep(bonds, env, here, waves, places, counts, scaling):
+def sweep(bonds, env, here, waves, counts, scaling):
     mw, rows_all, chi_in = env.shape
     phys, _, chi = waves[0][0].shape[1:]
     num_states = here.shape[1]
@@ -234,7 +255,7 @@
     share = jax.ShapeDtypeStruct((mw, chi // parts, chi), bf16)
     out = pl.pallas_call(
         functools.partial(sweep_kernel, parts, len(waves), len(counts), scaling),
-        in_specs=[SCALARS, WHOLE] + [ANY] * (2 + parts * len(waves)),
+        in_specs=[WHOLE] + [ANY] * (2 + parts * len(waves)),
         out_specs=[ANY] * len(counts) + [WHOLE] + [ANY] * parts,
         scratch_shapes=[
             pltpu.VMEM(env.shape, bf16),
@@ -264,12 +285,12 @@
             transcendentals=0,
         ),
         name="sweep",
-    )(places, bonds, env, here, *[wave for turn in waves for wave in turn])
+    )(bonds, env, here, *[wave for turn in waves for wave in turn])
     pieces = len(counts)
     return out[:pieces], out[pieces], out[pieces + 1 :]
 
 
-def applied_kernel(parts, pieces, begun, close, places, through_in, *refs):
+def applied_kernel(parts, pieces, begun, close, through_in, *refs):
     rights, refs = refs[: parts * pieces], refs[parts * pieces :]
     if begun:
         held, refs = refs[0], refs[1:]
@@ -329,7 +350,7 @@
         phys = results.shape[2]
         total = total.astype(jnp.bfloat16)
         if parts == 2:
-            swap = places[0] != 0
+            swap = lax.axis_index("bond") != 0
             total = own_first(swap, total[:, : columns // 2], total[:, columns // 2 :], 1)
         slot = k % 2
 
@@ -351,7 +372,7 @@
     token_ref[...] = jnp.zeros_like(token_ref)
 
 
-def applied_part(through, rights, held, places, phys, last):
+def applied_part(through, rights, held, phys, last):
     count, num_states, rows, chi = through.shape
     width = rights[0][0].shape[1]
     parts = len(rights[0])
@@ -374,7 +395,7 @@
     operands += [near(block) for blocks in rights for block in blocks] + ([near(held)] if begun else [])
     return pl.pallas_call(
         functools.partial(applied_kernel, parts, len(rights), begun, close),
-        in_specs=[SCALARS, WHOLE if close else ANY] + [WHOLE] * (len(operands) - 1),
+        in_specs=[WHOLE if close else ANY] + [WHOLE] * (len(operands) - 1),
         out_specs=[out_spec, WHOLE],
         out_shape=[out_shape, TOKEN],
         scratch_shapes=scratch,
@@ -385,7 +406,7 @@
             transcendentals=0,
         ),
         name="applied_part",
-    )(places, *operands)
+    )(*operands)
 
 
 def cuts(size):
@@ -398,8 +419,6 @@
     mw = mpo.shape[0]
     bonds = lax.axis_size("bond")
     paired = bonds == 2
-    me = lax.axis_index("bond").astype(jnp.int32)
-    places = jnp.stack([me, 1 - me]) if paired else jnp.stack([me, me]) * 0
     scaling = 1.0 / math.sqrt(num_states * chi)
     left = left_env[0].transpose(1, 0, 2)
     right = right_env[0].transpose(1, 0, 2)
@@ -409,7 +428,7 @@
     for stage in stages:
         pieces.append([])
         for count in stage:
-            piece = passed_along(right[first : first + count], "seg", -1)
+            piece = passed_along(cut(right, first, count), "seg", -1)
             pieces[-1].append(piece)
             first += count
 
@@ -423,7 +442,7 @@
             waves.append([lax.all_gather(wave, "bond", axis=2, tiled=True)])
     bond_table = mpo.transpose(3, 1, 2, 0).reshape(mw * phys, phys * mw)
     counts = [sum(stage) for stage in stages]
-    throughs, token, shares = sweep(bond_table, left, states, waves, places, counts, scaling)
+    throughs, token, shares = sweep(bond_table, left, states, waves, counts, scaling)
     if paired:
         arrived = swapped(shares[1], "bond")
         new_env = shares[0].astype(jnp.float32) + arrived.astype(jnp.float32)
@@ -441,7 +460,7 @@
             else:
                 rights.append([lax.all_gather(piece, "bond", axis=1, tiled=True)])
         last = index == len(pieces) - 1
-        held, token = applied_part(through, rights, held, places, phys, last)
+        held, token = applied_part(through, rights, held, phys, last)
     return (held[None], new_env.transpose(1, 0, 2)[None])
 
 

time: 110 us -> 209 us (1.90)
  Pallas kernels: 75 us -> 180 us
  local copies, waits for them, and re-layouts: 9.94 us -> 4.67 us
    pallas_call x0 -> x3, Pallas kernels: none -> 107 us  [cut(): pl.pallas_call(kernel, in_specs=[ANY], out_specs=ANY, out_shape=jax.Shape...]
    slice x3 -> x0, local copies, waits for them, and re-layouts: 5.24 us -> none  [on_device(): piece = passed_along(right[first:first + count], 'seg', -1)]
  transfers between devices with their start and end apart: 9 -> 9, of which waited for: 1 -> 1; matrix products, arithmetic and copies ran while one was open for 10% -> 4% of each run, Pallas kernels for 65% -> 61%
where the time goes in v8:
time: 209 us
  Pallas kernels  180 us (86%)
  starting transfers between devices  12.2 us (6%)
  waiting for transfers between devices  8.08 us (4%)
  local copies, waits for them, and re-layouts  4.67 us (2%)
  other arithmetic  3.02 us (1%)
    pallas_call x3, Pallas kernels, cut(): pl.pallas_call(kernel, in_specs=[ANY], out_specs=ANY, out_shape=jax.Shape...  107 us
    pallas_call x1, Pallas kernels, sweep(): pl.pallas_call(functools.partial(sweep_kernel, parts, len(waves), len(cou...  49.8 us
    pallas_call x3, Pallas kernels, applied_part(): pl.pallas_call(functools.partial(applied_kernel, parts, len(rights), begu...  23.5 us
    ppermute x3, starting transfers between devices, passed_along(): return lax.ppermute(array, axis, pairs)  9.37 us
    ppermute x6, waiting for transfers between devices, swapped(): return lax.ppermute(array, axis, [(0, 1), (1, 0)])  8.07 us
  transfers between devices with their start and end apart: 9, of which 1 were waited for; matrix products, arithmetic and copies ran while one was open for 4% of the time, Pallas kernels for 61%

profile of v8, /device:TPU:13, one launch (start us, length us, event | category | flops | bytes accessed | tf_op | source)
XLA Modules:
  0.0 208.7 jit_solution(11619851890871352708)
XLA Ops:
  0.6 0.0 copy-start.1
  0.6 48.8 %cut.5 = bf16[6,256,512]{2,1,0:T(8,128)(2,1)} custom-call(bf16[14,256,512]{2,1,0:T(8,128)(2,1)} %bitcast.22), custom_call_target="tpu_custom_call" | custom-call | tf_op jit(solution)/shard_map/cut/pallas_call | solution.py:64
  49.5 3.1 %collective-permute-start.4 = (bf16[6,256,512]{2,1,0:T(8,128)(2,1)}, bf16[6,256,512]{2,1,0:T(8,128)(2,1)S(1)}, u32[]{:S(2)}, u32[]{:S(2)}) collective-permute-start(bf16[6,256,512]{2,1,0:T(8,128)(2,1)} %cut.5), channel_id=1, source_target_pairs={{2,0},{4,2},{6,4},{8,6},{10,8},{12,10},{14,12},{16,14},{18,16},{20... | collective-permute-start | bytes 4718600 | tf_op jit(solution)/shard_map/ppermute | solution.py:22
  52.5 1.5 fusion.1
  54.0 1.2 copy.17
  55.2 1.0 collective-permute-start
  56.2 1.2 copy.16
  57.3 56.7 %cut.4 = bf16[7,256,512]{2,1,0:T(8,128)(2,1)} custom-call(bf16[14,256,512]{2,1,0:T(8,128)(2,1)} %bitcast.23), custom_call_target="tpu_custom_call" | custom-call | tf_op jit(solution)/shard_map/cut/pallas_call | solution.py:64
  114.1 2.2 %collective-permute-start.3 = (bf16[7,256,512]{2,1,0:T(8,128)(2,1)}, bf16[7,256,512]{2,1,0:T(8,128)(2,1)S(1)}, u32[]{:S(2)}, u32[]{:S(2)}) collective-permute-start(bf16[7,256,512]{2,1,0:T(8,128)(2,1)} %cut.4), channel_id=1, source_target_pairs={{2,0},{4,2},{6,4},{8,6},{10,8},{12,10},{14,12},{16,14},{18,16},{20... | collective-permute-start | bytes 5505032 | tf_op jit(solution)/shard_map/ppermute | solution.py:22
  116.3 0.1 copy.9
  116.4 0.7 reshape.7.bonds_ref
  117.1 49.8 %sweep.1 = (bf16[6,4,512,512]{3,2,1,0:T(8,128)(2,1)}, bf16[7,4,512,512]{3,2,1,0:T(8,128)(2,1)}, bf16[1,4,512,512]{3,2,1,0:T(8,128)(2,1)}, f32[8,128]{1,0:T(8,128...) custom-call(bf16[28,28]{1,0:T(8,128)(2,1)} %reshape.7.bonds_ref, bf16[14,256,512]{2,1,0:T(8,128)(2,1)} %bitcast.25, ...), custom_call_target="tpu_custom_call" | custom-call | tf_op jit(solution)/shard_map/sweep/pallas_call | solution.py:256
  166.9 0.9 collective-permute-start.8
  167.7 0.1 collective-permute-start.5
  167.8 8.1 %collective-permute-done.5.refs_1_ = bf16[6,256,512]{2,1,0:T(8,128)(2,1)S(1)} collective-permute-done((bf16[6,256,512]{2,1,0:T(8,128)(2,1)S(1)}, bf16[6,256,512]{2,1,0:T(8,128)(2,1)S(1)}, u32[]{:S(2)}, u32[]{:S(2)}) %collective-permute-start.5) | collective-permute-done | bytes 1572896 | tf_op jit(solution)/shard_map/ppermute | solution.py:26
  175.9 9.3 %applied_part.3 = (f32[4,512,512]{2,1,0:T(8,128)S(1)}, f32[8,128]{1,0:T(8,128)S(1)}) custom-call(bf16[6,4,512,512]{3,2,1,0:T(8,128)(2,1)} %get-tuple-element.15.through_in, bf16[6,256,512]{2,1,0:T(8,128)(2,1)S(1)} %after.3.refs_0_, bf16[6,256,512]{2,1,0:T(8,128)(2,1)S(1)} %collective-permute-done.5.refs_1_), custom_call_target="tpu_custom_call" | custom-call | tf_op jit(solution)/shard_map/applied_part/pallas_call | solution.py:396
  185.2 0.2 collective-permute-start.6
  185.4 1.0 cut.3
  186.4 4.1 %collective-permute-start.2 = (bf16[1,256,512]{2,1,0:T(8,128)(2,1)S(1)}, bf16[1,256,512]{2,1,0:T(8,128)(2,1)S(1)}, u32[]{:S(2)}, u32[]{:S(2)}) collective-permute-start(bf16[1,256,512]{2,1,0:T(8,128)(2,1)S(1)} %cut.3), channel_id=1, source_target_pairs={{2,0},{4,2},{6,4},{8,6},{10,8},{12,10},{14,12},{16,14},{18,16},{20... | collective-permute-start | bytes 786440 | tf_op jit(solution)/shard_map/ppermute | solution.py:22
  190.5 0.0 copy-start.2
  190.5 10.7 %applied_part.4 = (f32[4,512,512]{2,1,0:T(8,128)S(1)}, f32[8,128]{1,0:T(8,128)S(1)}) custom-call(bf16[7,4,512,512]{3,2,1,0:T(8,128)(2,1)} %get-tuple-element.14.through_in, bf16[7,256,512]{2,1,0:T(8,128)(2,1)S(1)} %after.4.refs_0_, bf16[7,256,512]{2,1,0:T(8,128)(2,1)S(1)} %collective-permute-done.6.refs_1_, f32[4,512,512]{2,1,0:T(8,128)S(1)} %get-tuple-element.18.refs_2_), custom_call_target="tpu_custom_call" | custom-call | tf_op jit(solution)/shard_map/applied_part/pallas_call | solution.py:396
  201.3 0.7 collective-permute-start.7
  202.0 3.0 %fusion = bf16[1,256,14,512]{3,1,2,0:T(8,128)(2,1)} fusion(bf16[14,256,512]{2,1,0:T(8,128)(2,1)S(1)} %collective-permute-done.8, bf16[14,256,512]{2,1,0:T(8,128)(2,1)S(1)} %copy-done.2), kind=kLoop, calls=%fused_computation.1 | loop fusion | flops 7340032 | bytes 11010048 | tf_op jit(solution)/shard_map/broadcast_in_dim | solution.py:464
  205.1 3.4 %applied_part.5 = (bf16[4,256,2,512]{3,2,1,0:T(2,128)(2,1)}, f32[8,128]{1,0:T(8,128)}) custom-call(bf16[1,4,512,512]{3,2,1,0:T(8,128)(2,1)S(1)} %copy-done, bf16[1,256,512]{2,1,0:T(8,128)(2,1)S(1)} %after.5.refs_0_, bf16[1,256,512]{2,1,0:T(8,128)(2,1)S(1)} %collective-permute-done.7.refs_1_, f32[4,512,512]{2,1,0:T(8,128)S(1)} %get-tuple-element.20.refs_2_), custom_call_target="tpu_custom_call" | custom-call | tf_op jit(solution)/shard_map/applied_part/pallas_call | solution.py:396
  (18 shorter events, 0.0 us)
Async XLA Ops:
  0.6 51.9 %copy-start.1 = (bf16[1,4,256,2,512]{4,3,2,1,0:T(2,128)(2,1)S(1)}, bf16[1,4,256,2,512]{4,3,2,1,0:T(2,128)(2,1)}, u32[]{:S(2)}) copy-start(bf16[1,4,256,2,512]{4,3,2,1,0:T(2,128)(2,1)} %here_hbm.1) | copy-start | bytes 6291460
  49.5 118.3 %collective-permute-start.4 = (bf16[6,256,512]{2,1,0:T(8,128)(2,1)}, bf16[6,256,512]{2,1,0:T(8,128)(2,1)S(1)}, u32[]{:S(2)}, u32[]{:S(2)}) collective-permute-start(bf16[6,256,512]{2,1,0:T(8,128)(2,1)} %cut.5), channel_id=1, source_target_pairs={{2,0},{4,2},{6,4},{8,6},{10,8},{12,10},{14,12},{16,14},{18,16},{20... | collective-permute-start | bytes 4718600 | tf_op jit(solution)/shard_map/ppermute | solution.py:22
  55.2 61.9 %collective-permute-start = (bf16[2,2,256,512]{3,2,1,0:T(8,128)(2,1)}, bf16[2,2,256,512]{3,2,1,0:T(8,128)(2,1)}, u32[]{:S(2)}, u32[]{:S(2)}) collective-permute-start(bf16[2,2,256,512]{3,2,1,0:T(8,128)(2,1)} %bitcast.21.refs_0_), channel_id=1, source_target_pairs={{0,1},{1,0},{2,3},{3,2},{4,5},{5,4},{6,7},{7,6},{8,9},{9,8},{10,11... | collective-permute-start | bytes 3145736 | tf_op jit(solution)/shard_map/ppermute | solution.py:26
  56.2 60.1 %copy-start.3 = (bf16[14,2,2,14]{3,2,1,0:T(2,128)(2,1)S(1)}, bf16[14,2,2,14]{3,2,1,0:T(2,128)(2,1)}, u32[]{:S(2)}) copy-start(bf16[14,2,2,14]{3,2,1,0:T(2,128)(2,1)} %param.7) | copy-start | bytes 4708
  57.3 59.8 %collective-permute-start.1 = (bf16[2,2,256,512]{3,2,1,0:T(8,128)(2,1)}, bf16[2,2,256,512]{3,2,1,0:T(8,128)(2,1)}, u32[]{:S(2)}, u32[]{:S(2)}) collective-permute-start(bf16[2,2,256,512]{3,2,1,0:T(8,128)(2,1)} %bitcast.20.refs_2_), channel_id=1, source_target_pairs={{0,1},{1,0},{2,3},{3,2},{4,5},{5,4},{6,7},{7,6},{8,9},{9,8},{10,11... | collective-permute-start | bytes 3145736 | tf_op jit(solution)/shard_map/ppermute | solution.py:26
  114.1 71.1 %collective-permute-start.3 = (bf16[7,256,512]{2,1,0:T(8,128)(2,1)}, bf16[7,256,512]{2,1,0:T(8,128)(2,1)S(1)}, u32[]{:S(2)}, u32[]{:S(2)}) collective-permute-start(bf16[7,256,512]{2,1,0:T(8,128)(2,1)} %cut.4), channel_id=1, source_target_pairs={{2,0},{4,2},{6,4},{8,6},{10,8},{12,10},{14,12},{16,14},{18,16},{20... | collective-permute-start | bytes 5505032 | tf_op jit(solution)/shard_map/ppermute | solution.py:22
  166.9 35.2 %collective-permute-start.8 = (bf16[14,256,512]{2,1,0:T(8,128)(2,1)}, bf16[14,256,512]{2,1,0:T(8,128)(2,1)S(1)}, u32[]{:S(2)}, u32[]{:S(2)}) collective-permute-start(bf16[14,256,512]{2,1,0:T(8,128)(2,1)} %get-tuple-element.23), channel_id=1, source_target_pairs={{0,1},{1,0},{2,3},{3,2},{4,5},{5,4},{6,7},{7,6},{8,9},{9,8},{10,11... | collective-permute-start | bytes 11010056 | tf_op jit(solution)/shard_map/ppermute | solution.py:26
  167.7 8.1 %collective-permute-start.5 = (bf16[6,256,512]{2,1,0:T(8,128)(2,1)S(1)}, bf16[6,256,512]{2,1,0:T(8,128)(2,1)S(1)}, u32[]{:S(2)}, u32[]{:S(2)}) collective-permute-start(bf16[6,256,512]{2,1,0:T(8,128)(2,1)S(1)} %after.3.refs_0_), channel_id=1, source_target_pairs={{0,1},{1,0},{2,3},{3,2},{4,5},{5,4},{6,7},{7,6},{8,9},{9,8},{10,11... | collective-permute-start | bytes 4718600 | tf_op jit(solution)/shard_map/ppermute | solution.py:26
  185.2 5.3 %collective-permute-start.6 = (bf16[7,256,512]{2,1,0:T(8,128)(2,1)S(1)}, bf16[7,256,512]{2,1,0:T(8,128)(2,1)S(1)}, u32[]{:S(2)}, u32[]{:S(2)}) collective-permute-start(bf16[7,256,512]{2,1,0:T(8,128)(2,1)S(1)} %after.4.refs_0_), channel_id=1, source_target_pairs={{0,1},{1,0},{2,3},{3,2},{4,5},{5,4},{6,7},{7,6},{8,9},{9,8},{10,11... | collective-permute-start | bytes 5505032 | tf_op jit(solution)/shard_map/ppermute | solution.py:26
  186.4 14.9 %collective-permute-start.2 = (bf16[1,256,512]{2,1,0:T(8,128)(2,1)S(1)}, bf16[1,256,512]{2,1,0:T(8,128)(2,1)S(1)}, u32[]{:S(2)}, u32[]{:S(2)}) collective-permute-start(bf16[1,256,512]{2,1,0:T(8,128)(2,1)S(1)} %cut.3), channel_id=1, source_target_pairs={{2,0},{4,2},{6,4},{8,6},{10,8},{12,10},{14,12},{16,14},{18,16},{20... | collective-permute-start | bytes 786440 | tf_op jit(solution)/shard_map/ppermute | solution.py:22
  190.5 11.5 %copy-start.2 = (bf16[14,256,512]{2,1,0:T(8,128)(2,1)S(1)}, bf16[14,256,512]{2,1,0:T(8,128)(2,1)}, u32[]{:S(2)}) copy-start(bf16[14,256,512]{2,1,0:T(8,128)(2,1)} %get-tuple-element.22) | copy-start | bytes 11010052
  201.3 3.7 %collective-permute-start.7 = (bf16[1,256,512]{2,1,0:T(8,128)(2,1)S(1)}, bf16[1,256,512]{2,1,0:T(8,128)(2,1)S(1)}, u32[]{:S(2)}, u32[]{:S(2)}) collective-permute-start(bf16[1,256,512]{2,1,0:T(8,128)(2,1)S(1)} %after.5.refs_0_), channel_id=1, source_target_pairs={{0,1},{1,0},{2,3},{3,2},{4,5},{5,4},{6,7},{7,6},{8,9},{9,8},{10,11... | collective-permute-start | bytes 786440 | tf_op jit(solution)/shard_map/ppermute | solution.py:26
  202.0 3.0 %copy-start = (bf16[1,4,512,512]{3,2,1,0:T(8,128)(2,1)S(1)}, bf16[1,4,512,512]{3,2,1,0:T(8,128)(2,1)}, u32[]{:S(2)}) copy-start(bf16[1,4,512,512]{3,2,1,0:T(8,128)(2,1)} %get-tuple-element.13.through_in) | copy-start | bytes 6291460

commit v9 on v8

--- a/solution.py
+++ b/solution.py
@@ -64,10 +64,10 @@
     return pl.pallas_call(
         kernel,
         in_specs=[ANY],
-        out_specs=ANY,
-        out_shape=jax.ShapeDtypeStruct((count,) + array.shape[1:], array.dtype),
+        out_specs=WHOLE,
+        out_shape=pltpu.VMEM((count,) + array.shape[1:], array.dtype),
         scratch_shapes=[pltpu.SemaphoreType.DMA((count,))],
-        compiler_params=pltpu.CompilerParams(vmem_limit_bytes=MIB),
+        compiler_params=pltpu.CompilerParams(vmem_limit_bytes=8 * MIB),
         name="cut",
     )(far(array))
 
@@ -428,7 +428,8 @@
     for stage in stages:
         pieces.append([])
         for count in stage:
-            piece = passed_along(cut(right, first, count), "seg", -1)
+            sent = right[first : first + count] if first else cut(right, first, count)
+            piece = passed_along(sent, "seg", -1)
             pieces[-1].append(piece)
             first += count
 

time: 209 us -> 108 us (0.52)
  Pallas kernels: 180 us -> 75.9 us
  local copies, waits for them, and re-layouts: 4.67 us -> 7.04 us
    pallas_call x3 -> x1, Pallas kernels: 107 us -> 2.7 us  [cut(): pl.pallas_call(kernel, in_specs=[ANY], out_specs=WHOLE, out_shape=pltpu.V...]
    slice x0 -> x2, local copies, waits for them, and re-layouts: none -> 2.36 us  [on_device(): sent = right[first:first + count] if first else cut(right, first, count)]
  transfers between devices with their start and end apart: 9 -> 9, of which waited for: 1 -> 1; matrix products, arithmetic and copies ran while one was open for 4% -> 9% of each run, Pallas kernels for 61% -> 65%
where the time goes in v9:
time: 108 us; the launch traced here: 107 us
  Pallas kernels  75.9 us (70%)
  starting transfers between devices  12.4 us (11%)
  waiting for transfers between devices  8.08 us (7%)
  local copies, waits for them, and re-layouts  7.04 us (7%)
  other arithmetic  3.02 us (3%)
    pallas_call x1, Pallas kernels, sweep(): pl.pallas_call(functools.partial(sweep_kernel, parts, len(waves), len(cou...  49.8 us
    pallas_call x3, Pallas kernels, applied_part(): pl.pallas_call(functools.partial(applied_kernel, parts, len(rights), begu...  23.5 us
    ppermute x3, starting transfers between devices, passed_along(): return lax.ppermute(array, axis, pairs)  9.62 us
    ppermute x6, waiting for transfers between devices, swapped(): return lax.ppermute(array, axis, [(0, 1), (1, 0)])  8.07 us
    broadcast_in_dim x1, other arithmetic, on_device(): return (held[None], new_env.transpose(1, 0, 2)[None])  3.02 us
    ppermute x6, starting transfers between devices, swapped(): return lax.ppermute(array, axis, [(0, 1), (1, 0)])  2.83 us
    pallas_call x1, Pallas kernels, cut(): pl.pallas_call(kernel, in_specs=[ANY], out_specs=WHOLE, out_shape=pltpu.V...  2.7 us
    unnamed x12, local copies, waits for them, and re-layouts  2.39 us
  transfers between devices with their start and end apart: 9, of which 1 were waited for; matrix products, arithmetic and copies ran while one was open for 9% of the time, Pallas kernels for 65%

profile of v9, /device:TPU:13, one launch (start us, length us, event | category | flops | bytes accessed | tf_op | source)
XLA Modules:
  0.0 107.5 jit_solution(1229920071195970692)
XLA Ops:
  0.6 2.7 %cut.1 = bf16[6,256,512]{2,1,0:T(8,128)(2,1)} custom-call(bf16[14,256,512]{2,1,0:T(8,128)(2,1)} %bitcast.22), custom_call_target="tpu_custom_call" | custom-call | tf_op jit(solution)/shard_map/cut/pallas_call | solution.py:64
  3.3 0.0 copy-start.1
  3.4 3.3 %collective-permute-start.4 = (bf16[6,256,512]{2,1,0:T(8,128)(2,1)}, bf16[6,256,512]{2,1,0:T(8,128)(2,1)S(1)}, u32[]{:S(2)}, u32[]{:S(2)}) collective-permute-start(bf16[6,256,512]{2,1,0:T(8,128)(2,1)} %cut.1), channel_id=1, source_target_pairs={{2,0},{4,2},{6,4},{8,6},{10,8},{12,10},{14,12},{16,14},{18,16},{20... | collective-permute-start | bytes 4718600 | tf_op jit(solution)/shard_map/ppermute | solution.py:22
  6.7 1.5 %fusion.1 = (bf16[1,2,256,2,512]{4,3,2,1,0:T(2,128)(2,1)S(1)}, bf16[1,2,256,2,512]{4,3,2,1,0:T(2,128)(2,1)S(1)}) fusion(bf16[1,4,256,2,512]{4,3,2,1,0:T(2,128)(2,1)S(1)} %copy-done.2), kind=kLoop, calls=%fused_computation.4 | loop fusion | bytes 4194304 | tf_op jit(solution)/shard_map/slice | solution.py:439
  8.2 1.2 %copy.17 = bf16[1,2,256,2,512]{4,2,3,1,0:T(8,128)(2,1)} copy(bf16[1,2,256,2,512]{4,3,2,1,0:T(2,128)(2,1)S(1)} %get-tuple-element.25) | data formatting | bytes 2097152
  9.4 1.0 collective-permute-start
  10.3 1.2 %copy.16 = bf16[1,2,256,2,512]{4,2,3,1,0:T(8,128)(2,1)} copy(bf16[1,2,256,2,512]{4,3,2,1,0:T(2,128)(2,1)S(1)} %get-tuple-element.24) | data formatting | bytes 2097152
  11.5 1.4 %slice.17 = bf16[7,256,512]{2,1,0:T(8,128)(2,1)} slice(bf16[14,256,512]{2,1,0:T(8,128)(2,1)S(1)} %bitcast.24), slice={[6:13], [0:256], [0:512]} | slice | bytes 3670016 | tf_op jit(solution)/shard_map/slice | solution.py:431
  12.9 2.2 %collective-permute-start.3 = (bf16[7,256,512]{2,1,0:T(8,128)(2,1)}, bf16[7,256,512]{2,1,0:T(8,128)(2,1)S(1)}, u32[]{:S(2)}, u32[]{:S(2)}) collective-permute-start(bf16[7,256,512]{2,1,0:T(8,128)(2,1)} %slice.17), channel_id=1, source_target_pairs={{2,0},{4,2},{6,4},{8,6},{10,8},{12,10},{14,12},{16,14},{18,16},{20... | collective-permute-start | bytes 5505032 | tf_op jit(solution)/shard_map/ppermute | solution.py:22
  15.1 0.1 copy.9
  15.2 0.7 reshape.7.bonds_ref
  15.9 49.8 %sweep.1 = (bf16[6,4,512,512]{3,2,1,0:T(8,128)(2,1)}, bf16[7,4,512,512]{3,2,1,0:T(8,128)(2,1)}, bf16[1,4,512,512]{3,2,1,0:T(8,128)(2,1)}, f32[8,128]{1,0:T(8,128...) custom-call(bf16[28,28]{1,0:T(8,128)(2,1)} %reshape.7.bonds_ref, bf16[14,256,512]{2,1,0:T(8,128)(2,1)} %bitcast.25, ...), custom_call_target="tpu_custom_call" | custom-call | tf_op jit(solution)/shard_map/sweep/pallas_call | solution.py:256
  65.7 0.9 collective-permute-start.8
  66.5 0.1 collective-permute-start.5
  66.6 8.1 %collective-permute-done.5.refs_1_ = bf16[6,256,512]{2,1,0:T(8,128)(2,1)S(1)} collective-permute-done((bf16[6,256,512]{2,1,0:T(8,128)(2,1)S(1)}, bf16[6,256,512]{2,1,0:T(8,128)(2,1)S(1)}, u32[]{:S(2)}, u32[]{:S(2)}) %collective-permute-start.5) | collective-permute-done | bytes 1572896 | tf_op jit(solution)/shard_map/ppermute | solution.py:26
  74.7 9.3 %applied_part.3 = (f32[4,512,512]{2,1,0:T(8,128)S(1)}, f32[8,128]{1,0:T(8,128)S(1)}) custom-call(bf16[6,4,512,512]{3,2,1,0:T(8,128)(2,1)} %get-tuple-element.15.through_in, bf16[6,256,512]{2,1,0:T(8,128)(2,1)S(1)} %after.3.refs_0_, bf16[6,256,512]{2,1,0:T(8,128)(2,1)S(1)} %collective-permute-done.5.refs_1_), custom_call_target="tpu_custom_call" | custom-call | tf_op jit(solution)/shard_map/applied_part/pallas_call | solution.py:396
  84.0 0.2 collective-permute-start.6
  84.2 1.0 slice.16
  85.2 4.1 %collective-permute-start.2 = (bf16[1,256,512]{2,1,0:T(8,128)(2,1)S(1)}, bf16[1,256,512]{2,1,0:T(8,128)(2,1)S(1)}, u32[]{:S(2)}, u32[]{:S(2)}) collective-permute-start(bf16[1,256,512]{2,1,0:T(8,128)(2,1)S(1)} %slice.16), channel_id=1, source_target_pairs={{2,0},{4,2},{6,4},{8,6},{10,8},{12,10},{14,12},{16,14},{18,16},{20... | collective-permute-start | bytes 786440 | tf_op jit(solution)/shard_map/ppermute | solution.py:22
  89.3 0.0 copy-start.3
  89.4 10.7 %applied_part.4 = (f32[4,512,512]{2,1,0:T(8,128)S(1)}, f32[8,128]{1,0:T(8,128)S(1)}) custom-call(bf16[7,4,512,512]{3,2,1,0:T(8,128)(2,1)} %get-tuple-element.14.through_in, bf16[7,256,512]{2,1,0:T(8,128)(2,1)S(1)} %after.4.refs_0_, bf16[7,256,512]{2,1,0:T(8,128)(2,1)S(1)} %collective-permute-done.6.refs_1_, f32[4,512,512]{2,1,0:T(8,128)S(1)} %get-tuple-element.18.refs_2_), custom_call_target="tpu_custom_call" | custom-call | tf_op jit(solution)/shard_map/applied_part/pallas_call | solution.py:396
  100.1 0.7 collective-permute-start.7
  100.8 3.0 %fusion = bf16[1,256,14,512]{3,1,2,0:T(8,128)(2,1)} fusion(bf16[14,256,512]{2,1,0:T(8,128)(2,1)S(1)} %collective-permute-done.8, bf16[14,256,512]{2,1,0:T(8,128)(2,1)S(1)} %copy-done.3), kind=kLoop, calls=%fused_computation.1 | loop fusion | flops 7340032 | bytes 11010048 | tf_op jit(solution)/shard_map/broadcast_in_dim | solution.py:465
  103.9 3.4 %applied_part.5 = (bf16[4,256,2,512]{3,2,1,0:T(2,128)(2,1)}, f32[8,128]{1,0:T(8,128)}) custom-call(bf16[1,4,512,512]{3,2,1,0:T(8,128)(2,1)S(1)} %copy-done, bf16[1,256,512]{2,1,0:T(8,128)(2,1)S(1)} %after.5.refs_0_, bf16[1,256,512]{2,1,0:T(8,128)(2,1)S(1)} %collective-permute-done.7.refs_1_, f32[4,512,512]{2,1,0:T(8,128)S(1)} %get-tuple-element.20.refs_2_), custom_call_target="tpu_custom_call" | custom-call | tf_op jit(solution)/shard_map/applied_part/pallas_call | solution.py:396
  (20 shorter events, 0.0 us)
Async XLA Ops:
  0.6 6.1 %copy-start.2 = (bf16[1,4,256,2,512]{4,3,2,1,0:T(2,128)(2,1)S(1)}, bf16[1,4,256,2,512]{4,3,2,1,0:T(2,128)(2,1)}, u32[]{:S(2)}) copy-start(bf16[1,4,256,2,512]{4,3,2,1,0:T(2,128)(2,1)} %here_hbm.1) | copy-start | bytes 6291460
  3.3 8.2 %copy-start.1 = (bf16[1,256,14,512]{3,1,2,0:T(8,128)(2,1)S(1)}, bf16[1,256,14,512]{3,1,2,0:T(8,128)(2,1)}, u32[]{:S(2)}) copy-start(bf16[1,256,14,512]{3,1,2,0:T(8,128)(2,1)} %param.5) | copy-start | bytes 11010052
  3.4 63.2 %collective-permute-start.4 = (bf16[6,256,512]{2,1,0:T(8,128)(2,1)}, bf16[6,256,512]{2,1,0:T(8,128)(2,1)S(1)}, u32[]{:S(2)}, u32[]{:S(2)}) collective-permute-start(bf16[6,256,512]{2,1,0:T(8,128)(2,1)} %cut.1), channel_id=1, source_target_pairs={{2,0},{4,2},{6,4},{8,6},{10,8},{12,10},{14,12},{16,14},{18,16},{20... | collective-permute-start | bytes 4718600 | tf_op jit(solution)/shard_map/ppermute | solution.py:22
  8.2 6.9 %copy-start.4 = (bf16[14,2,2,14]{3,2,1,0:T(2,128)(2,1)S(1)}, bf16[14,2,2,14]{3,2,1,0:T(2,128)(2,1)}, u32[]{:S(2)}) copy-start(bf16[14,2,2,14]{3,2,1,0:T(2,128)(2,1)} %param.7) | copy-start | bytes 4708
  9.4 6.5 %collective-permute-start = (bf16[2,2,256,512]{3,2,1,0:T(8,128)(2,1)}, bf16[2,2,256,512]{3,2,1,0:T(8,128)(2,1)}, u32[]{:S(2)}, u32[]{:S(2)}) collective-permute-start(bf16[2,2,256,512]{3,2,1,0:T(8,128)(2,1)} %bitcast.21.refs_0_), channel_id=1, source_target_pairs={{0,1},{1,0},{2,3},{3,2},{4,5},{5,4},{6,7},{7,6},{8,9},{9,8},{10,11... | collective-permute-start | bytes 3145736 | tf_op jit(solution)/shard_map/ppermute | solution.py:26
  11.5 4.4 %collective-permute-start.1 = (bf16[2,2,256,512]{3,2,1,0:T(8,128)(2,1)}, bf16[2,2,256,512]{3,2,1,0:T(8,128)(2,1)}, u32[]{:S(2)}, u32[]{:S(2)}) collective-permute-start(bf16[2,2,256,512]{3,2,1,0:T(8,128)(2,1)} %bitcast.20.refs_2_), channel_id=1, source_target_pairs={{0,1},{1,0},{2,3},{3,2},{4,5},{5,4},{6,7},{7,6},{8,9},{9,8},{10,11... | collective-permute-start | bytes 3145736 | tf_op jit(solution)/shard_map/ppermute | solution.py:26
  12.9 71.1 %collective-permute-start.3 = (bf16[7,256,512]{2,1,0:T(8,128)(2,1)}, bf16[7,256,512]{2,1,0:T(8,128)(2,1)S(1)}, u32[]{:S(2)}, u32[]{:S(2)}) collective-permute-start(bf16[7,256,512]{2,1,0:T(8,128)(2,1)} %slice.17), channel_id=1, source_target_pairs={{2,0},{4,2},{6,4},{8,6},{10,8},{12,10},{14,12},{16,14},{18,16},{20... | collective-permute-start | bytes 5505032 | tf_op jit(solution)/shard_map/ppermute | solution.py:22
  65.7 35.2 %collective-permute-start.8 = (bf16[14,256,512]{2,1,0:T(8,128)(2,1)}, bf16[14,256,512]{2,1,0:T(8,128)(2,1)S(1)}, u32[]{:S(2)}, u32[]{:S(2)}) collective-permute-start(bf16[14,256,512]{2,1,0:T(8,128)(2,1)} %get-tuple-element.23), channel_id=1, source_target_pairs={{0,1},{1,0},{2,3},{3,2},{4,5},{5,4},{6,7},{7,6},{8,9},{9,8},{10,11... | collective-permute-start | bytes 11010056 | tf_op jit(solution)/shard_map/ppermute | solution.py:26
  66.5 8.1 %collective-permute-start.5 = (bf16[6,256,512]{2,1,0:T(8,128)(2,1)S(1)}, bf16[6,256,512]{2,1,0:T(8,128)(2,1)S(1)}, u32[]{:S(2)}, u32[]{:S(2)}) collective-permute-start(bf16[6,256,512]{2,1,0:T(8,128)(2,1)S(1)} %after.3.refs_0_), channel_id=1, source_target_pairs={{0,1},{1,0},{2,3},{3,2},{4,5},{5,4},{6,7},{7,6},{8,9},{9,8},{10,11... | collective-permute-start | bytes 4718600 | tf_op jit(solution)/shard_map/ppermute | solution.py:26
  84.0 5.3 %collective-permute-start.6 = (bf16[7,256,512]{2,1,0:T(8,128)(2,1)S(1)}, bf16[7,256,512]{2,1,0:T(8,128)(2,1)S(1)}, u32[]{:S(2)}, u32[]{:S(2)}) collective-permute-start(bf16[7,256,512]{2,1,0:T(8,128)(2,1)S(1)} %after.4.refs_0_), channel_id=1, source_target_pairs={{0,1},{1,0},{2,3},{3,2},{4,5},{5,4},{6,7},{7,6},{8,9},{9,8},{10,11... | collective-permute-start | bytes 5505032 | tf_op jit(solution)/shard_map/ppermute | solution.py:26
  85.2 14.9 %collective-permute-start.2 = (bf16[1,256,512]{2,1,0:T(8,128)(2,1)S(1)}, bf16[1,256,512]{2,1,0:T(8,128)(2,1)S(1)}, u32[]{:S(2)}, u32[]{:S(2)}) collective-permute-start(bf16[1,256,512]{2,1,0:T(8,128)(2,1)S(1)} %slice.16), channel_id=1, source_target_pairs={{2,0},{4,2},{6,4},{8,6},{10,8},{12,10},{14,12},{16,14},{18,16},{20... | collective-permute-start | bytes 786440 | tf_op jit(solution)/shard_map/ppermute | solution.py:22
  89.3 11.5 %copy-start.3 = (bf16[14,256,512]{2,1,0:T(8,128)(2,1)S(1)}, bf16[14,256,512]{2,1,0:T(8,128)(2,1)}, u32[]{:S(2)}) copy-start(bf16[14,256,512]{2,1,0:T(8,128)(2,1)} %get-tuple-element.22) | copy-start | bytes 11010052
  100.1 3.8 %collective-permute-start.7 = (bf16[1,256,512]{2,1,0:T(8,128)(2,1)S(1)}, bf16[1,256,512]{2,1,0:T(8,128)(2,1)S(1)}, u32[]{:S(2)}, u32[]{:S(2)}) collective-permute-start(bf16[1,256,512]{2,1,0:T(8,128)(2,1)S(1)} %after.5.refs_0_), channel_id=1, source_target_pairs={{0,1},{1,0},{2,3},{3,2},{4,5},{5,4},{6,7},{7,6},{8,9},{9,8},{10,11... | collective-permute-start | bytes 786440 | tf_op jit(solution)/shard_map/ppermute | solution.py:26
  100.8 3.0 %copy-start = (bf16[1,4,512,512]{3,2,1,0:T(8,128)(2,1)S(1)}, bf16[1,4,512,512]{3,2,1,0:T(8,128)(2,1)}, u32[]{:S(2)}) copy-start(bf16[1,4,512,512]{3,2,1,0:T(8,128)(2,1)} %get-tuple-element.13.through_in) | copy-start | bytes 6291460

commit v10 on v9

--- a/solution.py
+++ b/solution.py
@@ -10,7 +10,7 @@
 
 GROUP = 8
 MIB = 1 << 20
-SWEEP_MIB = 54
+SWEEP_MIB = 56
 ANY = pl.BlockSpec(memory_space=pl.ANY)
 TOKEN = pltpu.VMEM((8, 128), jnp.float32)
 WHOLE = pl.BlockSpec(memory_space=pltpu.VMEM)
@@ -248,7 +248,7 @@
     mw, rows_all, chi_in = env.shape
     phys, _, chi = waves[0][0].shape[1:]
     num_states = here.shape[1]
-    rows = min(64, rows_all)
+    rows = min(128, rows_all)
     parts = len(waves[0])
     padded = -(-mw * phys * GROUP // 128) * 128
     bf16 = jnp.bfloat16

time: 108 us -> 108 us (level)
  no operation moved by 1% of the time
where the time goes in v10:
time: 108 us; the launch traced here: 107 us
  Pallas kernels  75.9 us (70%)
  starting transfers between devices  12.5 us (12%)
  waiting for transfers between devices  8.08 us (7%)
  local copies, waits for them, and re-layouts  7.04 us (7%)
  other arithmetic  3.02 us (3%)
    pallas_call x1, Pallas kernels, sweep(): pl.pallas_call(functools.partial(sweep_kernel, parts, len(waves), len(cou...  49.7 us
    pallas_call x3, Pallas kernels, applied_part(): pl.pallas_call(functools.partial(applied_kernel, parts, len(rights), begu...  23.5 us
    ppermute x3, starting transfers between devices, passed_along(): return lax.ppermute(array, axis, pairs)  9.61 us
    ppermute x6, waiting for transfers between devices, swapped(): return lax.ppermute(array, axis, [(0, 1), (1, 0)])  8.07 us
    broadcast_in_dim x1, other arithmetic, on_device(): return (held[None], new_env.transpose(1, 0, 2)[None])  3.02 us
    ppermute x6, starting transfers between devices, swapped(): return lax.ppermute(array, axis, [(0, 1), (1, 0)])  2.85 us
    pallas_call x1, Pallas kernels, cut(): pl.pallas_call(kernel, in_specs=[ANY], out_specs=WHOLE, out_shape=pltpu.V...  2.7 us
    unnamed x12, local copies, waits for them, and re-layouts  2.39 us
  transfers between devices with their start and end apart: 9, of which 1 were waited for; matrix products, arithmetic and copies ran while one was open for 9% of the time, Pallas kernels for 65%

profile of v10, /device:TPU:13, one launch (start us, length us, event | category | flops | bytes accessed | tf_op | source)
XLA Modules:
  0.0 107.4 jit_solution(12687687110614369639)
XLA Ops:
  0.6 0.0 copy-start.2
  0.6 2.7 %cut.1 = bf16[6,256,512]{2,1,0:T(8,128)(2,1)} custom-call(bf16[14,256,512]{2,1,0:T(8,128)(2,1)} %bitcast.22), custom_call_target="tpu_custom_call" | custom-call | tf_op jit(solution)/shard_map/cut/pallas_call | solution.py:64
  3.3 0.0 copy-start.1
  3.4 3.3 %collective-permute-start.4 = (bf16[6,256,512]{2,1,0:T(8,128)(2,1)}, bf16[6,256,512]{2,1,0:T(8,128)(2,1)S(1)}, u32[]{:S(2)}, u32[]{:S(2)}) collective-permute-start(bf16[6,256,512]{2,1,0:T(8,128)(2,1)} %cut.1), channel_id=1, source_target_pairs={{2,0},{4,2},{6,4},{8,6},{10,8},{12,10},{14,12},{16,14},{18,16},{20... | collective-permute-start | bytes 4718600 | tf_op jit(solution)/shard_map/ppermute | solution.py:22
  6.7 1.5 %fusion.1 = (bf16[1,2,256,2,512]{4,3,2,1,0:T(2,128)(2,1)S(1)}, bf16[1,2,256,2,512]{4,3,2,1,0:T(2,128)(2,1)S(1)}) fusion(bf16[1,4,256,2,512]{4,3,2,1,0:T(2,128)(2,1)S(1)} %copy-done.2), kind=kLoop, calls=%fused_computation.4 | loop fusion | bytes 4194304 | tf_op jit(solution)/shard_map/slice | solution.py:439
  8.2 1.2 %copy.17 = bf16[1,2,256,2,512]{4,2,3,1,0:T(8,128)(2,1)} copy(bf16[1,2,256,2,512]{4,3,2,1,0:T(2,128)(2,1)S(1)} %get-tuple-element.25) | data formatting | bytes 2097152
  9.4 1.0 collective-permute-start
  10.3 1.2 %copy.16 = bf16[1,2,256,2,512]{4,2,3,1,0:T(8,128)(2,1)} copy(bf16[1,2,256,2,512]{4,3,2,1,0:T(2,128)(2,1)S(1)} %get-tuple-element.24) | data formatting | bytes 2097152
  11.5 1.4 %slice.17 = bf16[7,256,512]{2,1,0:T(8,128)(2,1)} slice(bf16[14,256,512]{2,1,0:T(8,128)(2,1)S(1)} %bitcast.24), slice={[6:13], [0:256], [0:512]} | slice | bytes 3670016 | tf_op jit(solution)/shard_map/slice | solution.py:431
  12.9 2.2 %collective-permute-start.3 = (bf16[7,256,512]{2,1,0:T(8,128)(2,1)}, bf16[7,256,512]{2,1,0:T(8,128)(2,1)S(1)}, u32[]{:S(2)}, u32[]{:S(2)}) collective-permute-start(bf16[7,256,512]{2,1,0:T(8,128)(2,1)} %slice.17), channel_id=1, source_target_pairs={{2,0},{4,2},{6,4},{8,6},{10,8},{12,10},{14,12},{16,14},{18,16},{20... | collective-permute-start | bytes 5505032 | tf_op jit(solution)/shard_map/ppermute | solution.py:22
  15.1 0.1 copy.9
  15.2 0.7 reshape.7.bonds_ref
  15.9 49.7 %sweep.1 = (bf16[6,4,512,512]{3,2,1,0:T(8,128)(2,1)}, bf16[7,4,512,512]{3,2,1,0:T(8,128)(2,1)}, bf16[1,4,512,512]{3,2,1,0:T(8,128)(2,1)}, f32[8,128]{1,0:T(8,128...) custom-call(bf16[28,28]{1,0:T(8,128)(2,1)} %reshape.7.bonds_ref, bf16[14,256,512]{2,1,0:T(8,128)(2,1)} %bitcast.25, ...), custom_call_target="tpu_custom_call" | custom-call | tf_op jit(solution)/shard_map/sweep/pallas_call | solution.py:256
  65.6 0.9 collective-permute-start.8
  66.5 0.1 collective-permute-start.5
  66.6 8.1 %collective-permute-done.5.refs_1_ = bf16[6,256,512]{2,1,0:T(8,128)(2,1)S(1)} collective-permute-done((bf16[6,256,512]{2,1,0:T(8,128)(2,1)S(1)}, bf16[6,256,512]{2,1,0:T(8,128)(2,1)S(1)}, u32[]{:S(2)}, u32[]{:S(2)}) %collective-permute-start.5) | collective-permute-done | bytes 1572896 | tf_op jit(solution)/shard_map/ppermute | solution.py:26
  74.7 9.3 %applied_part.3 = (f32[4,512,512]{2,1,0:T(8,128)S(1)}, f32[8,128]{1,0:T(8,128)S(1)}) custom-call(bf16[6,4,512,512]{3,2,1,0:T(8,128)(2,1)} %get-tuple-element.15.through_in, bf16[6,256,512]{2,1,0:T(8,128)(2,1)S(1)} %after.3.refs_0_, bf16[6,256,512]{2,1,0:T(8,128)(2,1)S(1)} %collective-permute-done.5.refs_1_), custom_call_target="tpu_custom_call" | custom-call | tf_op jit(solution)/shard_map/applied_part/pallas_call | solution.py:396
  84.0 0.2 collective-permute-start.6
  84.2 1.0 slice.16
  85.2 4.1 %collective-permute-start.2 = (bf16[1,256,512]{2,1,0:T(8,128)(2,1)S(1)}, bf16[1,256,512]{2,1,0:T(8,128)(2,1)S(1)}, u32[]{:S(2)}, u32[]{:S(2)}) collective-permute-start(bf16[1,256,512]{2,1,0:T(8,128)(2,1)S(1)} %slice.16), channel_id=1, source_target_pairs={{2,0},{4,2},{6,4},{8,6},{10,8},{12,10},{14,12},{16,14},{18,16},{20... | collective-permute-start | bytes 786440 | tf_op jit(solution)/shard_map/ppermute | solution.py:22
  89.3 10.7 %applied_part.4 = (f32[4,512,512]{2,1,0:T(8,128)S(1)}, f32[8,128]{1,0:T(8,128)S(1)}) custom-call(bf16[7,4,512,512]{3,2,1,0:T(8,128)(2,1)} %get-tuple-element.14.through_in, bf16[7,256,512]{2,1,0:T(8,128)(2,1)S(1)} %after.4.refs_0_, bf16[7,256,512]{2,1,0:T(8,128)(2,1)S(1)} %collective-permute-done.6.refs_1_, f32[4,512,512]{2,1,0:T(8,128)S(1)} %get-tuple-element.18.refs_2_), custom_call_target="tpu_custom_call" | custom-call | tf_op jit(solution)/shard_map/applied_part/pallas_call | solution.py:396
  100.1 0.7 collective-permute-start.7
  100.8 3.0 %fusion = bf16[1,256,14,512]{3,1,2,0:T(8,128)(2,1)} fusion(bf16[14,256,512]{2,1,0:T(8,128)(2,1)S(1)} %collective-permute-done.8, bf16[14,256,512]{2,1,0:T(8,128)(2,1)S(1)} %copy-done.3), kind=kLoop, calls=%fused_computation.1 | loop fusion | flops 7340032 | bytes 11010048 | tf_op jit(solution)/shard_map/broadcast_in_dim | solution.py:465
  103.8 3.4 %applied_part.5 = (bf16[4,256,2,512]{3,2,1,0:T(2,128)(2,1)}, f32[8,128]{1,0:T(8,128)}) custom-call(bf16[1,4,512,512]{3,2,1,0:T(8,128)(2,1)S(1)} %copy-done, bf16[1,256,512]{2,1,0:T(8,128)(2,1)S(1)} %after.5.refs_0_, bf16[1,256,512]{2,1,0:T(8,128)(2,1)S(1)} %collective-permute-done.7.refs_1_, f32[4,512,512]{2,1,0:T(8,128)S(1)} %get-tuple-element.20.refs_2_), custom_call_target="tpu_custom_call" | custom-call | tf_op jit(solution)/shard_map/applied_part/pallas_call | solution.py:396
  (20 shorter events, 0.0 us)
Async XLA Ops:
  0.6 6.1 %copy-start.2 = (bf16[1,4,256,2,512]{4,3,2,1,0:T(2,128)(2,1)S(1)}, bf16[1,4,256,2,512]{4,3,2,1,0:T(2,128)(2,1)}, u32[]{:S(2)}) copy-start(bf16[1,4,256,2,512]{4,3,2,1,0:T(2,128)(2,1)} %here_hbm.1) | copy-start | bytes 6291460
  3.3 8.2 %copy-start.1 = (bf16[1,256,14,512]{3,1,2,0:T(8,128)(2,1)S(1)}, bf16[1,256,14,512]{3,1,2,0:T(8,128)(2,1)}, u32[]{:S(2)}) copy-start(bf16[1,256,14,512]{3,1,2,0:T(8,128)(2,1)} %param.5) | copy-start | bytes 11010052
  3.4 63.2 %collective-permute-start.4 = (bf16[6,256,512]{2,1,0:T(8,128)(2,1)}, bf16[6,256,512]{2,1,0:T(8,128)(2,1)S(1)}, u32[]{:S(2)}, u32[]{:S(2)}) collective-permute-start(bf16[6,256,512]{2,1,0:T(8,128)(2,1)} %cut.1), channel_id=1, source_target_pairs={{2,0},{4,2},{6,4},{8,6},{10,8},{12,10},{14,12},{16,14},{18,16},{20... | collective-permute-start | bytes 4718600 | tf_op jit(solution)/shard_map/ppermute | solution.py:22
  8.2 6.9 %copy-start.4 = (bf16[14,2,2,14]{3,2,1,0:T(2,128)(2,1)S(1)}, bf16[14,2,2,14]{3,2,1,0:T(2,128)(2,1)}, u32[]{:S(2)}) copy-start(bf16[14,2,2,14]{3,2,1,0:T(2,128)(2,1)} %param.7) | copy-start | bytes 4708
  9.4 6.5 %collective-permute-start = (bf16[2,2,256,512]{3,2,1,0:T(8,128)(2,1)}, bf16[2,2,256,512]{3,2,1,0:T(8,128)(2,1)}, u32[]{:S(2)}, u32[]{:S(2)}) collective-permute-start(bf16[2,2,256,512]{3,2,1,0:T(8,128)(2,1)} %bitcast.21.refs_0_), channel_id=1, source_target_pairs={{0,1},{1,0},{2,3},{3,2},{4,5},{5,4},{6,7},{7,6},{8,9},{9,8},{10,11... | collective-permute-start | bytes 3145736 | tf_op jit(solution)/shard_map/ppermute | solution.py:26
  11.5 4.4 %collective-permute-start.1 = (bf16[2,2,256,512]{3,2,1,0:T(8,128)(2,1)}, bf16[2,2,256,512]{3,2,1,0:T(8,128)(2,1)}, u32[]{:S(2)}, u32[]{:S(2)}) collective-permute-start(bf16[2,2,256,512]{3,2,1,0:T(8,128)(2,1)} %bitcast.20.refs_2_), channel_id=1, source_target_pairs={{0,1},{1,0},{2,3},{3,2},{4,5},{5,4},{6,7},{7,6},{8,9},{9,8},{10,11... | collective-permute-start | bytes 3145736 | tf_op jit(solution)/shard_map/ppermute | solution.py:26
  12.9 71.0 %collective-permute-start.3 = (bf16[7,256,512]{2,1,0:T(8,128)(2,1)}, bf16[7,256,512]{2,1,0:T(8,128)(2,1)S(1)}, u32[]{:S(2)}, u32[]{:S(2)}) collective-permute-start(bf16[7,256,512]{2,1,0:T(8,128)(2,1)} %slice.17), channel_id=1, source_target_pairs={{2,0},{4,2},{6,4},{8,6},{10,8},{12,10},{14,12},{16,14},{18,16},{20... | collective-permute-start | bytes 5505032 | tf_op jit(solution)/shard_map/ppermute | solution.py:22
  65.6 35.2 %collective-permute-start.8 = (bf16[14,256,512]{2,1,0:T(8,128)(2,1)}, bf16[14,256,512]{2,1,0:T(8,128)(2,1)S(1)}, u32[]{:S(2)}, u32[]{:S(2)}) collective-permute-start(bf16[14,256,512]{2,1,0:T(8,128)(2,1)} %get-tuple-element.23), channel_id=1, source_target_pairs={{0,1},{1,0},{2,3},{3,2},{4,5},{5,4},{6,7},{7,6},{8,9},{9,8},{10,11... | collective-permute-start | bytes 11010056 | tf_op jit(solution)/shard_map/ppermute | solution.py:26
  66.5 8.1 %collective-permute-start.5 = (bf16[6,256,512]{2,1,0:T(8,128)(2,1)S(1)}, bf16[6,256,512]{2,1,0:T(8,128)(2,1)S(1)}, u32[]{:S(2)}, u32[]{:S(2)}) collective-permute-start(bf16[6,256,512]{2,1,0:T(8,128)(2,1)S(1)} %after.3.refs_0_), channel_id=1, source_target_pairs={{0,1},{1,0},{2,3},{3,2},{4,5},{5,4},{6,7},{7,6},{8,9},{9,8},{10,11... | collective-permute-start | bytes 4718600 | tf_op jit(solution)/shard_map/ppermute | solution.py:26
  84.0 5.3 %collective-permute-start.6 = (bf16[7,256,512]{2,1,0:T(8,128)(2,1)S(1)}, bf16[7,256,512]{2,1,0:T(8,128)(2,1)S(1)}, u32[]{:S(2)}, u32[]{:S(2)}) collective-permute-start(bf16[7,256,512]{2,1,0:T(8,128)(2,1)S(1)} %after.4.refs_0_), channel_id=1, source_target_pairs={{0,1},{1,0},{2,3},{3,2},{4,5},{5,4},{6,7},{7,6},{8,9},{9,8},{10,11... | collective-permute-start | bytes 5505032 | tf_op jit(solution)/shard_map/ppermute | solution.py:26
  85.2 14.9 %collective-permute-start.2 = (bf16[1,256,512]{2,1,0:T(8,128)(2,1)S(1)}, bf16[1,256,512]{2,1,0:T(8,128)(2,1)S(1)}, u32[]{:S(2)}, u32[]{:S(2)}) collective-permute-start(bf16[1,256,512]{2,1,0:T(8,128)(2,1)S(1)} %slice.16), channel_id=1, source_target_pairs={{2,0},{4,2},{6,4},{8,6},{10,8},{12,10},{14,12},{16,14},{18,16},{20... | collective-permute-start | bytes 786440 | tf_op jit(solution)/shard_map/ppermute | solution.py:22
  89.3 11.5 %copy-start.3 = (bf16[14,256,512]{2,1,0:T(8,128)(2,1)S(1)}, bf16[14,256,512]{2,1,0:T(8,128)(2,1)}, u32[]{:S(2)}) copy-start(bf16[14,256,512]{2,1,0:T(8,128)(2,1)} %get-tuple-element.22) | copy-start | bytes 11010052
  100.1 3.7 %collective-permute-start.7 = (bf16[1,256,512]{2,1,0:T(8,128)(2,1)S(1)}, bf16[1,256,512]{2,1,0:T(8,128)(2,1)S(1)}, u32[]{:S(2)}, u32[]{:S(2)}) collective-permute-start(bf16[1,256,512]{2,1,0:T(8,128)(2,1)S(1)} %after.5.refs_0_), channel_id=1, source_target_pairs={{0,1},{1,0},{2,3},{3,2},{4,5},{5,4},{6,7},{7,6},{8,9},{9,8},{10,11... | collective-permute-start | bytes 786440 | tf_op jit(solution)/shard_map/ppermute | solution.py:26
  100.8 3.0 %copy-start = (bf16[1,4,512,512]{3,2,1,0:T(8,128)(2,1)S(1)}, bf16[1,4,512,512]{3,2,1,0:T(8,128)(2,1)}, u32[]{:S(2)}) copy-start(bf16[1,4,512,512]{3,2,1,0:T(8,128)(2,1)} %get-tuple-element.13.through_in) | copy-start | bytes 6291460

commit v11 on v9

--- a/solution.py
+++ b/solution.py
@@ -361,11 +361,8 @@
         return 0
 
     state(0, 0)
-    if last:
-        for k in range(1, num_states):
-            state(k, 0)
-    else:
-        lax.fori_loop(1, num_states, state, 0)
+    for k in range(1, num_states):
+        state(k, 0)
     if last:
         for k in range(max(num_states - 2, 0), num_states):
             out_copy(k, k % 2).wait()

time: 108 us -> 108 us (level)
  no operation moved by 1% of the time
where the time goes in v11:
time: 108 us; the launch traced here: 107 us
  Pallas kernels  75.9 us (70%)
  starting transfers between devices  12.4 us (11%)
  waiting for transfers between devices  8.08 us (7%)
  local copies, waits for them, and re-layouts  7.04 us (7%)
  other arithmetic  3.02 us (3%)
    pallas_call x1, Pallas kernels, sweep(): pl.pallas_call(functools.partial(sweep_kernel, parts, len(waves), len(cou...  49.8 us
    pallas_call x3, Pallas kernels, applied_part(): pl.pallas_call(functools.partial(applied_kernel, parts, len(rights), begu...  23.5 us
    ppermute x3, starting transfers between devices, passed_along(): return lax.ppermute(array, axis, pairs)  9.62 us
    ppermute x6, waiting for transfers between devices, swapped(): return lax.ppermute(array, axis, [(0, 1), (1, 0)])  8.07 us
    broadcast_in_dim x1, other arithmetic, on_device(): return (held[None], new_env.transpose(1, 0, 2)[None])  3.02 us
    ppermute x6, starting transfers between devices, swapped(): return lax.ppermute(array, axis, [(0, 1), (1, 0)])  2.83 us
    pallas_call x1, Pallas kernels, cut(): pl.pallas_call(kernel, in_specs=[ANY], out_specs=WHOLE, out_shape=pltpu.V...  2.7 us
    unnamed x12, local copies, waits for them, and re-layouts  2.39 us
  transfers between devices with their start and end apart: 9, of which 1 were waited for; matrix products, arithmetic and copies ran while one was open for 9% of the time, Pallas kernels for 65%

profile of v11, /device:TPU:13, one launch (start us, length us, event | category | flops | bytes accessed | tf_op | source)
XLA Modules:
  0.0 107.5 jit_solution(12886743207387844384)
XLA Ops:
  0.6 2.7 %cut.1 = bf16[6,256,512]{2,1,0:T(8,128)(2,1)} custom-call(bf16[14,256,512]{2,1,0:T(8,128)(2,1)} %bitcast.22), custom_call_target="tpu_custom_call" | custom-call | tf_op jit(solution)/shard_map/cut/pallas_call | solution.py:64
  3.3 0.0 copy-start.1
  3.4 3.3 %collective-permute-start.4 = (bf16[6,256,512]{2,1,0:T(8,128)(2,1)}, bf16[6,256,512]{2,1,0:T(8,128)(2,1)S(1)}, u32[]{:S(2)}, u32[]{:S(2)}) collective-permute-start(bf16[6,256,512]{2,1,0:T(8,128)(2,1)} %cut.1), channel_id=1, source_target_pairs={{2,0},{4,2},{6,4},{8,6},{10,8},{12,10},{14,12},{16,14},{18,16},{20... | collective-permute-start | bytes 4718600 | tf_op jit(solution)/shard_map/ppermute | solution.py:22
  6.7 1.5 %fusion.1 = (bf16[1,2,256,2,512]{4,3,2,1,0:T(2,128)(2,1)S(1)}, bf16[1,2,256,2,512]{4,3,2,1,0:T(2,128)(2,1)S(1)}) fusion(bf16[1,4,256,2,512]{4,3,2,1,0:T(2,128)(2,1)S(1)} %copy-done.2), kind=kLoop, calls=%fused_computation.4 | loop fusion | bytes 4194304 | tf_op jit(solution)/shard_map/slice | solution.py:436
  8.2 1.2 %copy.17 = bf16[1,2,256,2,512]{4,2,3,1,0:T(8,128)(2,1)} copy(bf16[1,2,256,2,512]{4,3,2,1,0:T(2,128)(2,1)S(1)} %get-tuple-element.25) | data formatting | bytes 2097152
  9.4 1.0 collective-permute-start
  10.3 1.2 %copy.16 = bf16[1,2,256,2,512]{4,2,3,1,0:T(8,128)(2,1)} copy(bf16[1,2,256,2,512]{4,3,2,1,0:T(2,128)(2,1)S(1)} %get-tuple-element.24) | data formatting | bytes 2097152
  11.5 1.4 %slice.17 = bf16[7,256,512]{2,1,0:T(8,128)(2,1)} slice(bf16[14,256,512]{2,1,0:T(8,128)(2,1)S(1)} %bitcast.24), slice={[6:13], [0:256], [0:512]} | slice | bytes 3670016 | tf_op jit(solution)/shard_map/slice | solution.py:428
  12.9 2.2 %collective-permute-start.3 = (bf16[7,256,512]{2,1,0:T(8,128)(2,1)}, bf16[7,256,512]{2,1,0:T(8,128)(2,1)S(1)}, u32[]{:S(2)}, u32[]{:S(2)}) collective-permute-start(bf16[7,256,512]{2,1,0:T(8,128)(2,1)} %slice.17), channel_id=1, source_target_pairs={{2,0},{4,2},{6,4},{8,6},{10,8},{12,10},{14,12},{16,14},{18,16},{20... | collective-permute-start | bytes 5505032 | tf_op jit(solution)/shard_map/ppermute | solution.py:22
  15.1 0.1 copy.9
  15.2 0.7 reshape.7.bonds_ref
  15.9 49.8 %sweep.1 = (bf16[6,4,512,512]{3,2,1,0:T(8,128)(2,1)}, bf16[7,4,512,512]{3,2,1,0:T(8,128)(2,1)}, bf16[1,4,512,512]{3,2,1,0:T(8,128)(2,1)}, f32[8,128]{1,0:T(8,128...) custom-call(bf16[28,28]{1,0:T(8,128)(2,1)} %reshape.7.bonds_ref, bf16[14,256,512]{2,1,0:T(8,128)(2,1)} %bitcast.25, ...), custom_call_target="tpu_custom_call" | custom-call | tf_op jit(solution)/shard_map/sweep/pallas_call | solution.py:256
  65.7 0.9 collective-permute-start.8
  66.5 0.1 collective-permute-start.5
  66.6 8.1 %collective-permute-done.5.refs_1_ = bf16[6,256,512]{2,1,0:T(8,128)(2,1)S(1)} collective-permute-done((bf16[6,256,512]{2,1,0:T(8,128)(2,1)S(1)}, bf16[6,256,512]{2,1,0:T(8,128)(2,1)S(1)}, u32[]{:S(2)}, u32[]{:S(2)}) %collective-permute-start.5) | collective-permute-done | bytes 1572896 | tf_op jit(solution)/shard_map/ppermute | solution.py:26
  74.7 9.3 %applied_part.3 = (f32[4,512,512]{2,1,0:T(8,128)S(1)}, f32[8,128]{1,0:T(8,128)S(1)}) custom-call(bf16[6,4,512,512]{3,2,1,0:T(8,128)(2,1)} %get-tuple-element.15.through_in, bf16[6,256,512]{2,1,0:T(8,128)(2,1)S(1)} %after.3.refs_0_, bf16[6,256,512]{2,1,0:T(8,128)(2,1)S(1)} %collective-permute-done.5.refs_1_), custom_call_target="tpu_custom_call" | custom-call | tf_op jit(solution)/shard_map/applied_part/pallas_call | solution.py:393
  84.0 0.2 collective-permute-start.6
  84.2 1.0 slice.16
  85.2 4.1 %collective-permute-start.2 = (bf16[1,256,512]{2,1,0:T(8,128)(2,1)S(1)}, bf16[1,256,512]{2,1,0:T(8,128)(2,1)S(1)}, u32[]{:S(2)}, u32[]{:S(2)}) collective-permute-start(bf16[1,256,512]{2,1,0:T(8,128)(2,1)S(1)} %slice.16), channel_id=1, source_target_pairs={{2,0},{4,2},{6,4},{8,6},{10,8},{12,10},{14,12},{16,14},{18,16},{20... | collective-permute-start | bytes 786440 | tf_op jit(solution)/shard_map/ppermute | solution.py:22
  89.3 0.0 copy-start.3
  89.4 10.7 %applied_part.4 = (f32[4,512,512]{2,1,0:T(8,128)S(1)}, f32[8,128]{1,0:T(8,128)S(1)}) custom-call(bf16[7,4,512,512]{3,2,1,0:T(8,128)(2,1)} %get-tuple-element.14.through_in, bf16[7,256,512]{2,1,0:T(8,128)(2,1)S(1)} %after.4.refs_0_, bf16[7,256,512]{2,1,0:T(8,128)(2,1)S(1)} %collective-permute-done.6.refs_1_, f32[4,512,512]{2,1,0:T(8,128)S(1)} %get-tuple-element.18.refs_2_), custom_call_target="tpu_custom_call" | custom-call | tf_op jit(solution)/shard_map/applied_part/pallas_call | solution.py:393
  100.1 0.7 collective-permute-start.7
  100.8 3.0 %fusion = bf16[1,256,14,512]{3,1,2,0:T(8,128)(2,1)} fusion(bf16[14,256,512]{2,1,0:T(8,128)(2,1)S(1)} %collective-permute-done.8, bf16[14,256,512]{2,1,0:T(8,128)(2,1)S(1)} %copy-done.3), kind=kLoop, calls=%fused_computation.1 | loop fusion | flops 7340032 | bytes 11010048 | tf_op jit(solution)/shard_map/broadcast_in_dim | solution.py:462
  103.9 3.4 %applied_part.5 = (bf16[4,256,2,512]{3,2,1,0:T(2,128)(2,1)}, f32[8,128]{1,0:T(8,128)}) custom-call(bf16[1,4,512,512]{3,2,1,0:T(8,128)(2,1)S(1)} %copy-done, bf16[1,256,512]{2,1,0:T(8,128)(2,1)S(1)} %after.5.refs_0_, bf16[1,256,512]{2,1,0:T(8,128)(2,1)S(1)} %collective-permute-done.7.refs_1_, f32[4,512,512]{2,1,0:T(8,128)S(1)} %get-tuple-element.20.refs_2_), custom_call_target="tpu_custom_call" | custom-call | tf_op jit(solution)/shard_map/applied_part/pallas_call | solution.py:393
  (20 shorter events, 0.0 us)
Async XLA Ops:
  0.6 6.1 %copy-start.2 = (bf16[1,4,256,2,512]{4,3,2,1,0:T(2,128)(2,1)S(1)}, bf16[1,4,256,2,512]{4,3,2,1,0:T(2,128)(2,1)}, u32[]{:S(2)}) copy-start(bf16[1,4,256,2,512]{4,3,2,1,0:T(2,128)(2,1)} %here_hbm.1) | copy-start | bytes 6291460
  3.3 8.2 %copy-start.1 = (bf16[1,256,14,512]{3,1,2,0:T(8,128)(2,1)S(1)}, bf16[1,256,14,512]{3,1,2,0:T(8,128)(2,1)}, u32[]{:S(2)}) copy-start(bf16[1,256,14,512]{3,1,2,0:T(8,128)(2,1)} %param.5) | copy-start | bytes 11010052
  3.4 63.2 %collective-permute-start.4 = (bf16[6,256,512]{2,1,0:T(8,128)(2,1)}, bf16[6,256,512]{2,1,0:T(8,128)(2,1)S(1)}, u32[]{:S(2)}, u32[]{:S(2)}) collective-permute-start(bf16[6,256,512]{2,1,0:T(8,128)(2,1)} %cut.1), channel_id=1, source_target_pairs={{2,0},{4,2},{6,4},{8,6},{10,8},{12,10},{14,12},{16,14},{18,16},{20... | collective-permute-start | bytes 4718600 | tf_op jit(solution)/shard_map/ppermute | solution.py:22
  8.2 6.9 %copy-start.4 = (bf16[14,2,2,14]{3,2,1,0:T(2,128)(2,1)S(1)}, bf16[14,2,2,14]{3,2,1,0:T(2,128)(2,1)}, u32[]{:S(2)}) copy-start(bf16[14,2,2,14]{3,2,1,0:T(2,128)(2,1)} %param.7) | copy-start | bytes 4708
  9.4 6.5 %collective-permute-start = (bf16[2,2,256,512]{3,2,1,0:T(8,128)(2,1)}, bf16[2,2,256,512]{3,2,1,0:T(8,128)(2,1)}, u32[]{:S(2)}, u32[]{:S(2)}) collective-permute-start(bf16[2,2,256,512]{3,2,1,0:T(8,128)(2,1)} %bitcast.21.refs_0_), channel_id=1, source_target_pairs={{0,1},{1,0},{2,3},{3,2},{4,5},{5,4},{6,7},{7,6},{8,9},{9,8},{10,11... | collective-permute-start | bytes 3145736 | tf_op jit(solution)/shard_map/ppermute | solution.py:26
  11.5 4.4 %collective-permute-start.1 = (bf16[2,2,256,512]{3,2,1,0:T(8,128)(2,1)}, bf16[2,2,256,512]{3,2,1,0:T(8,128)(2,1)}, u32[]{:S(2)}, u32[]{:S(2)}) collective-permute-start(bf16[2,2,256,512]{3,2,1,0:T(8,128)(2,1)} %bitcast.20.refs_2_), channel_id=1, source_target_pairs={{0,1},{1,0},{2,3},{3,2},{4,5},{5,4},{6,7},{7,6},{8,9},{9,8},{10,11... | collective-permute-start | bytes 3145736 | tf_op jit(solution)/shard_map/ppermute | solution.py:26
  12.9 71.1 %collective-permute-start.3 = (bf16[7,256,512]{2,1,0:T(8,128)(2,1)}, bf16[7,256,512]{2,1,0:T(8,128)(2,1)S(1)}, u32[]{:S(2)}, u32[]{:S(2)}) collective-permute-start(bf16[7,256,512]{2,1,0:T(8,128)(2,1)} %slice.17), channel_id=1, source_target_pairs={{2,0},{4,2},{6,4},{8,6},{10,8},{12,10},{14,12},{16,14},{18,16},{20... | collective-permute-start | bytes 5505032 | tf_op jit(solution)/shard_map/ppermute | solution.py:22
  65.7 35.2 %collective-permute-start.8 = (bf16[14,256,512]{2,1,0:T(8,128)(2,1)}, bf16[14,256,512]{2,1,0:T(8,128)(2,1)S(1)}, u32[]{:S(2)}, u32[]{:S(2)}) collective-permute-start(bf16[14,256,512]{2,1,0:T(8,128)(2,1)} %get-tuple-element.23), channel_id=1, source_target_pairs={{0,1},{1,0},{2,3},{3,2},{4,5},{5,4},{6,7},{7,6},{8,9},{9,8},{10,11... | collective-permute-start | bytes 11010056 | tf_op jit(solution)/shard_map/ppermute | solution.py:26
  66.5 8.1 %collective-permute-start.5 = (bf16[6,256,512]{2,1,0:T(8,128)(2,1)S(1)}, bf16[6,256,512]{2,1,0:T(8,128)(2,1)S(1)}, u32[]{:S(2)}, u32[]{:S(2)}) collective-permute-start(bf16[6,256,512]{2,1,0:T(8,128)(2,1)S(1)} %after.3.refs_0_), channel_id=1, source_target_pairs={{0,1},{1,0},{2,3},{3,2},{4,5},{5,4},{6,7},{7,6},{8,9},{9,8},{10,11... | collective-permute-start | bytes 4718600 | tf_op jit(solution)/shard_map/ppermute | solution.py:26
  84.0 5.3 %collective-permute-start.6 = (bf16[7,256,512]{2,1,0:T(8,128)(2,1)S(1)}, bf16[7,256,512]{2,1,0:T(8,128)(2,1)S(1)}, u32[]{:S(2)}, u32[]{:S(2)}) collective-permute-start(bf16[7,256,512]{2,1,0:T(8,128)(2,1)S(1)} %after.4.refs_0_), channel_id=1, source_target_pairs={{0,1},{1,0},{2,3},{3,2},{4,5},{5,4},{6,7},{7,6},{8,9},{9,8},{10,11... | collective-permute-start | bytes 5505032 | tf_op jit(solution)/shard_map/ppermute | solution.py:26
  85.2 14.9 %collective-permute-start.2 = (bf16[1,256,512]{2,1,0:T(8,128)(2,1)S(1)}, bf16[1,256,512]{2,1,0:T(8,128)(2,1)S(1)}, u32[]{:S(2)}, u32[]{:S(2)}) collective-permute-start(bf16[1,256,512]{2,1,0:T(8,128)(2,1)S(1)} %slice.16), channel_id=1, source_target_pairs={{2,0},{4,2},{6,4},{8,6},{10,8},{12,10},{14,12},{16,14},{18,16},{20... | collective-permute-start | bytes 786440 | tf_op jit(solution)/shard_map/ppermute | solution.py:22
  89.3 11.5 %copy-start.3 = (bf16[14,256,512]{2,1,0:T(8,128)(2,1)S(1)}, bf16[14,256,512]{2,1,0:T(8,128)(2,1)}, u32[]{:S(2)}) copy-start(bf16[14,256,512]{2,1,0:T(8,128)(2,1)} %get-tuple-element.22) | copy-start | bytes 11010052
  100.1 3.8 %collective-permute-start.7 = (bf16[1,256,512]{2,1,0:T(8,128)(2,1)S(1)}, bf16[1,256,512]{2,1,0:T(8,128)(2,1)S(1)}, u32[]{:S(2)}, u32[]{:S(2)}) collective-permute-start(bf16[1,256,512]{2,1,0:T(8,128)(2,1)S(1)} %after.5.refs_0_), channel_id=1, source_target_pairs={{0,1},{1,0},{2,3},{3,2},{4,5},{5,4},{6,7},{7,6},{8,9},{9,8},{10,11... | collective-permute-start | bytes 786440 | tf_op jit(solution)/shard_map/ppermute | solution.py:26
  100.8 3.0 %copy-start = (bf16[1,4,512,512]{3,2,1,0:T(8,128)(2,1)S(1)}, bf16[1,4,512,512]{3,2,1,0:T(8,128)(2,1)}, u32[]{:S(2)}) copy-start(bf16[1,4,512,512]{3,2,1,0:T(8,128)(2,1)} %get-tuple-element.13.through_in) | copy-start | bytes 6291460
